TPU v7x, 32 devices: a whole 2x2x4 slice. The times are simulated.
32 devices in a mesh: section: 1, expert: 32 (over z, y, x, core).
Axes of the slice: x: 2, y: 2, z: 4, core: 2. Of those that a mesh axis runs over, the one named last changes fastest.
Arguments:
- act_send: bfloat16 [256, 3584], P(('section', 'expert')), may hold values from -6 to 6
- grad_send: bfloat16 [256, 3584], P(('section', 'expert')), may hold values from -6 to 6
- x_back: bfloat16 [256, 3584], P(('section', 'expert')), may hold values from -6 to 6
- routes_fwd: int32 [256, 2], P(('section', 'expert')), may hold values from 0 to 3, all different within a row; in each aligned block of 8 rows (0 to 7, 8 to 15, ...) at most 8 rows name the same one
- gates_fwd: float32 [256, 2], P(('section', 'expert')), may hold values from 0.3 to 1
- routes_back: int32 [256, 2], P(('section', 'expert')), may hold values from 0 to 3, all different within a row; in each aligned block of 8 rows (0 to 7, 8 to 15, ...) at most 8 rows name the same one
- gates_back: float32 [256, 2], P(('section', 'expert')), may hold values from 0.3 to 1
- norm_gain: float32 [1, 3584], P('section'), may hold values from 0.5 to 1.5
- w_gate: bfloat16 [1, 32, 3584, 128], P('section', 'expert'), may hold values from -0.09375 to 0.09375
- w_up: bfloat16 [1, 32, 3584, 128], P('section', 'expert'), may hold values from -0.09375 to 0.09375
- w_down: bfloat16 [1, 32, 128, 3584], P('section', 'expert'), may hold values from -0.1875 to 0.1875
- stash: bfloat16 [1, 32, 32, 8, 256], P('section', 'expert'), may hold values from -6 to 6
Outputs:
- outbound: bfloat16 [256, 3584], P(('section', 'expert'))
- input_grad: bfloat16 [256, 3584], P(('section', 'expert'))
Inputs may be any that keep to these rules, and one draw needn't show every extreme that they name: `routes_fwd`: each row names 2 different experts; among the rows of one device no expert is named more than 8 times, a bound that some block reaches. `routes_back`: each row names 2 different experts; among the rows of one device no expert is named more than 8 times, a bound that some block reaches.
All inputs are finite; a program needn't handle non-finite values.
Results may differ from a plain program's by a relative error of at most 0.0055.
Values may be sent and summed in bfloat16 or wider, within the bound.
No kernel may reach another device: no remote copies, remote signals or barrier semaphores. Data moves between devices by JAX's collectives and lax.ppermute only.
A program may use at most 64 MiB of HBM per device.

v0:
```python
import jax
import jax.numpy as jnp
from jax import lax
from jax.sharding import PartitionSpec as P

EPSILON = 1e-06
HIGHEST = lax.Precision.HIGHEST


def from_behind(value, axis, by):
    size = lax.axis_size(axis)
    return lax.ppermute(value, axis, [(i, (i + by) % size) for i in range(size)])


def slot_tables(routes, gates, experts, capacity):
    tokens_here = routes.shape[0]
    chosen = routes.reshape(-1)
    onehot = (chosen[:, None] == jnp.arange(experts, dtype=jnp.int32)[None, :]).astype(jnp.int32)
    earlier = jnp.cumsum(onehot, axis=0) - onehot
    within = jnp.sum(earlier * onehot, axis=1)
    target = chosen * capacity + within
    slot_table = (
        target[:, None] == jnp.arange(experts * capacity, dtype=jnp.int32)[None, :]
    ).astype(jnp.float32)
    slot_table = slot_table.reshape(tokens_here, routes.shape[1], experts * capacity)
    occupancy = jnp.sum(slot_table, axis=1).T
    weighted = jnp.sum(slot_table * gates[:, :, None], axis=1)
    return (occupancy, weighted)


def normalize(values, scale_row):
    factor = lax.rsqrt(jnp.mean(values * values, axis=-1, keepdims=True) + EPSILON)
    return (values * factor * scale_row, factor)


def fan_out(slot_rows, groups, shards):
    capacity = slot_rows.shape[0] // groups
    columns = slot_rows.shape[1]
    spread = jnp.broadcast_to(
        slot_rows.reshape(groups, 1, capacity, columns), (groups, shards, capacity, columns)
    )
    return spread.reshape(groups * shards, capacity, columns)


def return_sums(partial_value, groups, shards):
    sources, capacity, columns = partial_value.shape
    arrived = lax.all_to_all(partial_value, "expert", split_axis=0, concat_axis=0, tiled=True)
    summed = arrived.reshape(groups, shards, capacity, columns).astype(jnp.float32).sum(axis=1)
    return summed.reshape(groups * capacity, columns)


def body(
    act_send,
    grad_send,
    x_back,
    routes_fwd,
    gates_fwd,
    routes_back,
    gates_back,
    norm_gain,
    w_gate,
    w_up,
    w_down,
    stash,
):
    sources = lax.axis_size("expert")
    shards = min(8, sources // 2)
    groups = sources // shards
    capacity = stash.shape[3]
    hidden_dev = w_gate.shape[3]
    columns = act_send.shape[1]
    scale_row = norm_gain[0]
    gate_weight = w_gate[0, 0]
    up_weight = w_up[0, 0]
    down_weight = w_down[0, 0]
    inbound = from_behind(act_send, "section", 1)
    cotangent = from_behind(grad_send, "section", -1)
    normed = normalize(inbound.astype(jnp.float32), scale_row)[0].astype(jnp.bfloat16)
    occupancy_fwd, weighted_fwd = slot_tables(routes_fwd, gates_fwd, groups, capacity)
    slot_rows = jnp.dot(
        occupancy_fwd.astype(jnp.bfloat16), normed, preferred_element_type=jnp.float32
    ).astype(jnp.bfloat16)
    received = lax.all_to_all(
        fan_out(slot_rows, groups, shards), "expert", split_axis=0, concat_axis=0, tiled=True
    )
    flat_rows = received.reshape(-1, columns)
    gate_pre = jnp.dot(flat_rows, gate_weight, preferred_element_type=jnp.float32)
    up_pre = jnp.dot(flat_rows, up_weight, preferred_element_type=jnp.float32)
    hidden = (jax.nn.silu(gate_pre) * up_pre).astype(jnp.bfloat16)
    partial_value = jnp.dot(hidden, down_weight, preferred_element_type=jnp.float32).astype(
        jnp.bfloat16
    )
    summed = return_sums(partial_value.reshape(sources, capacity, columns), groups, shards)
    mixture = jnp.dot(weighted_fwd, summed, precision=HIGHEST)
    outbound = (inbound.astype(jnp.float32) + mixture).astype(jnp.bfloat16)
    occupancy_back, weighted_back = slot_tables(routes_back, gates_back, groups, capacity)
    grad_rows = jnp.dot(weighted_back.T, cotangent.astype(jnp.float32), precision=HIGHEST).astype(
        jnp.bfloat16
    )
    grad_received = lax.all_to_all(
        fan_out(grad_rows, groups, shards), "expert", split_axis=0, concat_axis=0, tiled=True
    )
    grad_flat = grad_received.reshape(-1, columns)
    saved_pre = stash[0, 0].reshape(-1, 2 * hidden_dev).astype(jnp.float32)
    saved_gate = saved_pre[:, :hidden_dev]
    saved_up = saved_pre[:, hidden_dev:]
    grad_hidden = jnp.einsum(
        "rd,hd->rh", grad_flat, down_weight, preferred_element_type=jnp.float32
    )
    sigmoid = jax.nn.sigmoid(saved_gate)
    d_gate = (grad_hidden * saved_up * sigmoid * (1.0 + saved_gate * (1.0 - sigmoid))).astype(
        jnp.bfloat16
    )
    d_up = (grad_hidden * saved_gate * sigmoid).astype(jnp.bfloat16)
    grad_total = jnp.einsum("rh,dh->rd", d_gate, gate_weight, preferred_element_type=jnp.float32)
    grad_total = grad_total + jnp.einsum(
        "rh,dh->rd", d_up, up_weight, preferred_element_type=jnp.float32
    )
    grad_partial = grad_total.astype(jnp.bfloat16)
    grad_summed = return_sums(grad_partial.reshape(sources, capacity, columns), groups, shards)
    grad_normed = jnp.dot(occupancy_back.T, grad_summed, precision=HIGHEST)
    saved32 = x_back.astype(jnp.float32)
    factor = normalize(saved32, scale_row)[1]
    scaled_grad = grad_normed * scale_row
    through = factor * scaled_grad - saved32 * factor**3 * jnp.mean(
        scaled_grad * saved32, axis=-1, keepdims=True
    )
    input_grad = (cotangent.astype(jnp.float32) + through).astype(jnp.bfloat16)
    return (outbound, input_grad)


def solution(mesh):
    placed = (
        P(("section", "expert"), None),
        P(("section", "expert"), None),
        P(("section", "expert"), None),
        P(("section", "expert"), None),
        P(("section", "expert"), None),
        P(("section", "expert"), None),
        P(("section", "expert"), None),
        P("section", None),
        P("section", "expert", None, None),
        P("section", "expert", None, None),
        P("section", "expert", None, None),
        P("section", "expert", None, None, None),
    )
    return jax.shard_map(
        body,
        mesh=mesh,
        in_specs=placed,
        out_specs=(P(("section", "expert"), None), P(("section", "expert"), None)),
        check_vma=False,
    )
```

profile of v0, /device:TPU:0, one launch (start us, length us, event | category | flops | bytes accessed | tf_op | source)
XLA Modules:
  0.0 201.5 jit_solution(13718537868850624561)
XLA Ops:
  0.6 0.9 collective-permute-start.1
  1.5 0.8 copy.29
  2.5 0.2 select_reduce_fusion.1
  2.8 0.1 copy.31
  2.9 0.8 select_reduce_fusion
  3.6 0.4 fusion.4
  4.0 1.4 broadcast_in_dim.11
  5.4 7.3 %all-to-all-start.2 = ((bf16[32,8,3584]{2,1,0:T(8,128)(2,1)}), bf16[32,8,3584]{2,1,0:T(8,128)(2,1)S(1)}, u32[]{:S(2)}, u32[]{:S(2)}) async-start(bf16[32,8,3584]{2,1,0:T(8,128)(2,1)} %bitcast.62), calls=%async_computation.2 | async-start | bytes 3670016 | tf_op jit(solution)/shard_map/all_to_all | solution.py:100
  12.7 0.1 copy.26
  13.0 0.2 select_reduce_fusion.3
  13.3 0.1 copy.28
  13.5 0.1 fusion.38
  13.7 0.3 fusion.3
  14.0 42.0 %all-to-all-done.2 = bf16[32,8,3584]{2,1,0:T(8,128)(2,1)S(1)} async-done(((bf16[32,8,3584]{2,1,0:T(8,128)(2,1)}), bf16[32,8,3584]{2,1,0:T(8,128)(2,1)S(1)}, u32[]{:S(2)}, u32[]{:S(2)}) %all-to-all-start.2) | async-done | bytes 1835040 | tf_op jit(solution)/shard_map/all_to_all | solution.py:100
  55.9 1.4 broadcast_in_dim.9
  57.4 0.4 copy-done.1
  57.8 4.0 %all-to-all-start = ((bf16[32,8,3584]{2,1,0:T(8,128)(2,1)}), bf16[32,8,3584]{2,1,0:T(8,128)(2,1)S(1)}, u32[]{:S(2)}, u32[]{:S(2)}) async-start(bf16[32,8,3584]{2,1,0:T(8,128)(2,1)} %bitcast.63), calls=%async_computation | async-start | bytes 3670016 | tf_op jit(solution)/shard_map/all_to_all | solution.py:83
  61.9 2.4 %fusion.6 = f32[256,128]{1,0:T(8,128)S(1)} fusion(bf16[32,8,3584]{2,1,0:T(8,128)(2,1)} %copy-done.1, bf16[1,1,128,3584]{3,2,1,0:T(8,128)(2,1)} %param.22), kind=kOutput, calls=%fused_computation.14 | convolution fusion | flops 234881024 | bytes 2883584 | tf_op jit(solution)/shard_map/rd,hd->rh/dot_general | solution.py:107
  64.3 0.7 fusion.25
  65.0 1.9 fusion.2
  66.9 38.1 %all-to-all-done = bf16[32,8,3584]{2,1,0:T(8,128)(2,1)S(1)} async-done(((bf16[32,8,3584]{2,1,0:T(8,128)(2,1)}), bf16[32,8,3584]{2,1,0:T(8,128)(2,1)S(1)}, u32[]{:S(2)}, u32[]{:S(2)}) %all-to-all-start) | async-done | bytes 1835040 | tf_op jit(solution)/shard_map/all_to_all | solution.py:83
  105.0 4.1 %all-to-all-start.3 = ((bf16[32,8,3584]{2,1,0:T(8,128)(2,1)}), bf16[32,8,3584]{2,1,0:T(8,128)(2,1)}, u32[]{:S(2)}, u32[]{:S(2)}) async-start(bf16[32,8,3584]{2,1,0:T(8,128)(2,1)} %fusion.2), calls=%async_computation.3 | async-start | bytes 3670016 | tf_op jit(solution)/shard_map/all_to_all | solution.py:47
  109.2 1.8 fusion.10
  111.0 3.6 %fusion.1 = bf16[32,8,3584]{2,1,0:T(8,128)(2,1)} fusion(bf16[32,8,3584]{2,1,0:T(8,128)(2,1)S(1)} %all-to-all-done, bf16[1,1,128,3584]{3,2,1,0:T(8,128)(2,1)} %param.22, bf16[1,1,3584,128]{3,2,1,0:T(8,128)(2,1)S(1)} %copy-done, f32[256,128]{1,0:T(8,128)S(1)} %fusion.10), kind=kOutput, calls=%fused_computation.3 | convolution fusion | flops 470876160 | bytes 5636096 | tf_op jit(solution)/shard_map/dot_general | solution.py:90
  114.6 37.8 %all-to-all-done.3 = bf16[32,8,3584]{2,1,0:T(8,128)(2,1)} async-done(((bf16[32,8,3584]{2,1,0:T(8,128)(2,1)}), bf16[32,8,3584]{2,1,0:T(8,128)(2,1)}, u32[]{:S(2)}, u32[]{:S(2)}) %all-to-all-start.3) | async-done | bytes 1835040 | tf_op jit(solution)/shard_map/all_to_all | solution.py:47
  152.4 4.0 %all-to-all-start.1 = ((bf16[32,8,3584]{2,1,0:T(8,128)(2,1)}), bf16[32,8,3584]{2,1,0:T(8,128)(2,1)S(1)}, u32[]{:S(2)}, u32[]{:S(2)}) async-start(bf16[32,8,3584]{2,1,0:T(8,128)(2,1)} %fusion.1), calls=%async_computation.1 | async-start | bytes 3670016 | tf_op jit(solution)/shard_map/all_to_all | solution.py:47
  156.4 1.8 convert_reduce_fusion
  158.2 0.5 fusion.41
  158.7 40.9 %all-to-all-done.1 = bf16[32,8,3584]{2,1,0:T(8,128)(2,1)S(1)} async-done(((bf16[32,8,3584]{2,1,0:T(8,128)(2,1)}), bf16[32,8,3584]{2,1,0:T(8,128)(2,1)S(1)}, u32[]{:S(2)}, u32[]{:S(2)}) %all-to-all-start.1) | async-done | bytes 1835040 | tf_op jit(solution)/shard_map/all_to_all | solution.py:47
  199.6 0.3 convert_reduce_fusion.1
  199.9 1.0 fusion.5
  200.8 0.7 fusion.45
  (36 shorter events, 0.8 us)
Async XLA Ops:
  0.6 64.3 %copy-start = (bf16[1,1,3584,128]{3,2,1,0:T(8,128)(2,1)S(1)}, bf16[1,1,3584,128]{3,2,1,0:T(8,128)(2,1)}, u32[]{:S(2)}) copy-start(bf16[1,1,3584,128]{3,2,1,0:T(8,128)(2,1)} %param.21) | copy-start | bytes 2752516
  0.6 3.0 %collective-permute-start.1 = (bf16[8,3584]{1,0:T(8,128)(2,1)}, bf16[8,3584]{1,0:T(8,128)(2,1)S(1)}, u32[]{:S(2)}, u32[]{:S(2)}) collective-permute-start(bf16[8,3584]{1,0:T(8,128)(2,1)} %param.13), channel_id=1, source_target_pairs={{0,0},{1,1},{2,2},{3,3},{4,4},{5,5},{6,6},{7,7},{8,8},{9,9},{10,10... | collective-permute-start | bytes 172040 | tf_op jit(solution)/shard_map/ppermute | solution.py:12
  5.4 7.3 %copy-start.8 = (bf16[8,3584]{1,0:T(8,128)(2,1)S(1)}, bf16[8,3584]{1,0:T(8,128)(2,1)}, u32[]{:S(2)}) copy-start(bf16[8,3584]{1,0:T(8,128)(2,1)} %param.12) | copy-start | bytes 172036
  5.4 7.3 %copy-start.6 = (s32[8,2]{0,1:T(2,128)S(1)}, s32[8,2]{0,1:T(2,128)}, u32[]{:S(2)}) copy-start(s32[8,2]{0,1:T(2,128)} %param.15) | copy-start | bytes 196
  5.4 8.0 %copy-start.7 = (f32[8,2]{0,1:T(2,128)S(1)}, f32[8,2]{0,1:T(2,128)}, u32[]{:S(2)}) copy-start(f32[8,2]{0,1:T(2,128)} %param.16) | copy-start | bytes 196
  5.4 8.1 %copy-start.5 = (f32[1,3584]{1,0:T(1,128)S(1)}, f32[1,3584]{1,0:T(1,128)}, u32[]{:S(2)}) copy-start(f32[1,3584]{1,0:T(1,128)} %param.19) | copy-start | bytes 43012
  5.4 50.5 %all-to-all-start.2 = ((bf16[32,8,3584]{2,1,0:T(8,128)(2,1)}), bf16[32,8,3584]{2,1,0:T(8,128)(2,1)S(1)}, u32[]{:S(2)}, u32[]{:S(2)}) async-start(bf16[32,8,3584]{2,1,0:T(8,128)(2,1)} %bitcast.62), calls=%async_computation.2 | async-start | bytes 3670016 | tf_op jit(solution)/shard_map/all_to_all | solution.py:100
  12.7 0.8 collective-permute-start
  55.9 1.8 copy-start.1
  57.4 4.4 %copy-start.4 = (bf16[1,1,32,8,256]{4,3,2,1,0:T(8,128)(2,1)S(1)}, bf16[1,1,32,8,256]{4,3,2,1,0:T(8,128)(2,1)}, u32[]{:S(2)}) copy-start(bf16[1,1,32,8,256]{4,3,2,1,0:T(8,128)(2,1)} %param.23) | copy-start | bytes 393220
  57.8 47.2 %all-to-all-start = ((bf16[32,8,3584]{2,1,0:T(8,128)(2,1)}), bf16[32,8,3584]{2,1,0:T(8,128)(2,1)S(1)}, u32[]{:S(2)}, u32[]{:S(2)}) async-start(bf16[32,8,3584]{2,1,0:T(8,128)(2,1)} %bitcast.63), calls=%async_computation | async-start | bytes 3670016 | tf_op jit(solution)/shard_map/all_to_all | solution.py:83
  61.8 2.5 %copy-start.2 = (bf16[1,1,3584,128]{3,2,1,0:T(8,128)(2,1)S(1)}, bf16[1,1,3584,128]{3,2,1,0:T(8,128)(2,1)}, u32[]{:S(2)}) copy-start(bf16[1,1,3584,128]{3,2,1,0:T(8,128)(2,1)} %param.20) | copy-start | bytes 2752516
  105.0 47.4 %all-to-all-start.3 = ((bf16[32,8,3584]{2,1,0:T(8,128)(2,1)}), bf16[32,8,3584]{2,1,0:T(8,128)(2,1)}, u32[]{:S(2)}, u32[]{:S(2)}) async-start(bf16[32,8,3584]{2,1,0:T(8,128)(2,1)} %fusion.2), calls=%async_computation.3 | async-start | bytes 3670016 | tf_op jit(solution)/shard_map/all_to_all | solution.py:47
  152.4 47.2 %all-to-all-start.1 = ((bf16[32,8,3584]{2,1,0:T(8,128)(2,1)}), bf16[32,8,3584]{2,1,0:T(8,128)(2,1)S(1)}, u32[]{:S(2)}, u32[]{:S(2)}) async-start(bf16[32,8,3584]{2,1,0:T(8,128)(2,1)} %fusion.1), calls=%async_computation.1 | async-start | bytes 3670016 | tf_op jit(solution)/shard_map/all_to_all | solution.py:47
  156.4 1.8 copy-start.3
where the time goes:
time: 202 us
  waiting for transfers between devices  159 us (79%)
  starting transfers between devices  20.4 us (10%)
  matrix products  12.5 us (6%)
  local copies, waits for them, and re-layouts  4.59 us (2%)
  other arithmetic  4.45 us (2%)
    all_to_all x2, waiting for transfers between devices, return_sums(): lax.all_to_all(partial_value, 'expert', split_axis=0, concat_axis=0, tile...  78.7 us
    all_to_all x1, waiting for transfers between devices, body(): lax.all_to_all(fan_out(grad_rows, groups, shards), 'expert', split_axis=0...  42 us
    all_to_all x1, waiting for transfers between devices, body(): lax.all_to_all(fan_out(slot_rows, groups, shards), 'expert', split_axis=0...  38.1 us
    all_to_all x2, starting transfers between devices, return_sums(): lax.all_to_all(partial_value, 'expert', split_axis=0, concat_axis=0, tile...  8.17 us
    all_to_all x1, starting transfers between devices, body(): lax.all_to_all(fan_out(grad_rows, groups, shards), 'expert', split_axis=0...  7.3 us
  transfers between devices with their start and end apart: 6, of which 4 were waited for; matrix products, arithmetic and copies ran while one was open for 8% of the time, Pallas kernels for 0%

commit v1 on v0

v1 whole, which is shorter than its diff:
```python
import jax
import jax.numpy as jnp
from jax import lax
from jax.sharding import PartitionSpec as P

EPSILON = 1e-06
HIGHEST = lax.Precision.HIGHEST
F32 = jnp.float32
BF16 = jnp.bfloat16


def from_behind(value, axis, by):
    size = lax.axis_size(axis)
    if size == 1:
        return value
    return lax.ppermute(value, axis, [(i, (i + by) % size) for i in range(size)])


def swap(value, mask_of):
    size = lax.axis_size("expert")
    return lax.ppermute(value, "expert", [(i, i ^ mask_of(i)) for i in range(size)])


def with_core(value):
    return swap(value, lambda i: 1)


def with_first(value):
    return swap(value, lambda i: 4 if i & 1 else 2)


def with_second(value):
    return swap(value, lambda i: 2 if i & 1 else 4)


def slot_tables(routes, gates, experts, capacity):
    tokens_here = routes.shape[0]
    chosen = routes.reshape(-1)
    onehot = (chosen[:, None] == jnp.arange(experts, dtype=jnp.int32)[None, :]).astype(jnp.int32)
    earlier = jnp.cumsum(onehot, axis=0) - onehot
    within = jnp.sum(earlier * onehot, axis=1)
    target = chosen * capacity + within
    slot_table = (
        target[:, None] == jnp.arange(experts * capacity, dtype=jnp.int32)[None, :]
    ).astype(F32)
    slot_table = slot_table.reshape(tokens_here, routes.shape[1], experts * capacity)
    occupancy = jnp.sum(slot_table, axis=1).T
    weighted = jnp.sum(slot_table * gates[:, :, None], axis=1)
    return (occupancy, weighted)


def normalize(values, scale_row):
    factor = lax.rsqrt(jnp.mean(values * values, axis=-1, keepdims=True) + EPSILON)
    return (values * factor * scale_row, factor)


def dispatch(slot_rows, groups):
    capacity = slot_rows.shape[0] // groups
    chunks = [slot_rows[k * capacity : (k + 1) * capacity] for k in range(groups)]
    arrived = [chunks[0]] + [swap(chunks[k], lambda i, k=k: 8 * k) for k in range(1, groups)]
    own = jnp.concatenate(arrived, axis=0)
    half = jnp.concatenate([own, with_first(own)], axis=0)
    return jnp.concatenate([half, with_second(half)], axis=0)


def give_back(partial_value, groups):
    rows = partial_value.shape[0]
    half, quarter = rows // 2, rows // 4
    arrived = with_second(partial_value[half:].astype(BF16))
    summed = partial_value[:half] + arrived.astype(F32)
    arrived = with_first(summed[quarter:].astype(BF16))
    summed = (summed[:quarter] + arrived.astype(F32)).astype(BF16)
    capacity = quarter // groups
    chunks = [summed[k * capacity : (k + 1) * capacity] for k in range(groups)]
    arrived = [chunks[0]] + [swap(chunks[k], lambda i, k=k: 8 * k) for k in range(1, groups)]
    return jnp.concatenate(arrived, axis=0)


def stash_rows(stash_flat, group, place, core, groups, capacity):
    first = jnp.where(core == 0, 2, 4)
    second = 6 - first
    position = jnp.arange(4 * groups * capacity, dtype=jnp.int32)
    quarter = position // (groups * capacity)
    chunk = position // capacity % groups
    slot = position % capacity
    away = jnp.where(quarter % 2 == 1, first, 0) ^ jnp.where(quarter >= 2, second, 0)
    source = (group ^ chunk) * 8 + ((place & 6) ^ away) + core
    wanted = source * capacity + slot
    table = (
        wanted[:, None] == jnp.arange(stash_flat.shape[0], dtype=jnp.int32)[None, :]
    ).astype(BF16)
    return jnp.dot(table, stash_flat, preferred_element_type=F32).astype(BF16)


def body(
    act_send,
    grad_send,
    x_back,
    routes_fwd,
    gates_fwd,
    routes_back,
    gates_back,
    norm_gain,
    w_gate,
    w_up,
    w_down,
    stash,
):
    sources = lax.axis_size("expert")
    groups = sources // 8
    capacity = stash.shape[3]
    hidden_dev = w_gate.shape[3]
    hidden_two = 2 * hidden_dev
    index = lax.axis_index("expert")
    group, place, core = index // 8, index % 8, index % 2
    scale_row = norm_gain[0]

    gate_other = with_core(w_gate[0, 0])
    up_other = with_core(w_up[0, 0])
    down_other = with_core(w_down[0, 0])
    w_in = jnp.concatenate([w_gate[0, 0], gate_other, w_up[0, 0], up_other], axis=1)
    w_out = jnp.concatenate([w_down[0, 0], down_other], axis=0)

    stash_flat = stash[0, 0].reshape(sources * capacity, 2 * hidden_dev)
    stash_own = stash_rows(stash_flat, group, place, core, groups, capacity)
    stash_other = with_core(stash_rows(stash_flat, group, place, 1 - core, groups, capacity))
    saved_gate = jnp.concatenate(
        [stash_own[:, :hidden_dev], stash_other[:, :hidden_dev]], axis=1
    ).astype(F32)
    saved_up = jnp.concatenate(
        [stash_own[:, hidden_dev:], stash_other[:, hidden_dev:]], axis=1
    ).astype(F32)

    inbound = from_behind(act_send, "section", 1)
    cotangent = from_behind(grad_send, "section", -1)
    occupancy_fwd, weighted_fwd = slot_tables(routes_fwd ^ group, gates_fwd, groups, capacity)
    occupancy_back, weighted_back = slot_tables(routes_back ^ group, gates_back, groups, capacity)

    normed = normalize(inbound.astype(F32), scale_row)[0].astype(BF16)
    slot_rows = jnp.dot(
        occupancy_fwd.astype(BF16), normed, preferred_element_type=F32
    ).astype(BF16)
    flat_rows = dispatch(slot_rows, groups)

    grad_rows = jnp.dot(weighted_back.T, cotangent.astype(F32), precision=HIGHEST).astype(BF16)
    grad_flat = dispatch(grad_rows, groups)

    pre = jnp.dot(flat_rows, w_in, preferred_element_type=F32)
    hidden = (jax.nn.silu(pre[:, :hidden_two]) * pre[:, hidden_two:]).astype(BF16)
    summed = give_back(jnp.dot(hidden, w_out, preferred_element_type=F32), groups)
    mixture = jnp.dot(weighted_fwd, summed.astype(F32), precision=HIGHEST)
    outbound = (inbound.astype(F32) + mixture).astype(BF16)

    grad_hidden = jnp.einsum("rd,hd->rh", grad_flat, w_out, preferred_element_type=F32)
    sigmoid = jax.nn.sigmoid(saved_gate)
    d_gate = (grad_hidden * saved_up * sigmoid * (1.0 + saved_gate * (1.0 - sigmoid))).astype(BF16)
    d_up = (grad_hidden * saved_gate * sigmoid).astype(BF16)
    d_pre = jnp.concatenate([d_gate, d_up], axis=1)
    grad_total = jnp.einsum("rh,dh->rd", d_pre, w_in, preferred_element_type=F32)
    grad_summed = give_back(grad_total, groups)
    grad_normed = jnp.dot(occupancy_back.T, grad_summed.astype(F32), precision=HIGHEST)
    saved32 = x_back.astype(F32)
    factor = normalize(saved32, scale_row)[1]
    scaled_grad = grad_normed * scale_row
    through = factor * scaled_grad - saved32 * factor**3 * jnp.mean(
        scaled_grad * saved32, axis=-1, keepdims=True
    )
    input_grad = (cotangent.astype(F32) + through).astype(BF16)
    return (outbound, input_grad)


def solution(mesh):
    placed = (
        P(("section", "expert"), None),
        P(("section", "expert"), None),
        P(("section", "expert"), None),
        P(("section", "expert"), None),
        P(("section", "expert"), None),
        P(("section", "expert"), None),
        P(("section", "expert"), None),
        P("section", None),
        P("section", "expert", None, None),
        P("section", "expert", None, None),
        P("section", "expert", None, None),
        P("section", "expert", None, None, None),
    )
    return jax.shard_map(
        body,
        mesh=mesh,
        in_specs=placed,
        out_specs=(P(("section", "expert"), None), P(("section", "expert"), None)),
        check_vma=False,
    )
```

time: 202 us -> 87 us (0.43)
  waiting for transfers between devices: 159 us -> 33.2 us
  starting transfers between devices: 20.4 us -> 37.4 us
  matrix products: 12.5 us -> 6.97 us
    all_to_all x4 -> x0, waiting for transfers between devices: 159 us -> none  [the longest x2 78.7 us: return_sums(): lax.all_to_all(partial_value, 'expert', split_axis=0, concat_axis=0, tile...]
    ppermute x2 -> x24, starting transfers between devices: 0.91 us -> 37.4 us  [swap(): lax.ppermute(value, 'expert', [(i, i ^ mask_of(i)) for i in range(size)])]
    ppermute x2 -> x24, waiting for transfers between devices: 0.01 us -> 33.2 us  [swap(): lax.ppermute(value, 'expert', [(i, i ^ mask_of(i)) for i in range(size)])]
    all_to_all x4 -> x0, starting transfers between devices: 19.5 us -> none  [the longest x2 8.17 us: return_sums(): lax.all_to_all(partial_value, 'expert', split_axis=0, concat_axis=0, tile...]
    dot_general x9 -> x10, matrix products: 12.5 us -> 6.97 us  [the longest x1 1.31 us: body(): jnp.einsum('rh,dh->rd', d_pre, w_in, preferred_element_type=F32)]
    broadcast_in_dim x2 -> x0, local copies, waits for them, and re-layouts: 2.82 us -> none  [fan_out(): jnp.broadcast_to(slot_rows.reshape(groups, 1, capacity, columns), (groups...]
    reduce_sum x2 -> x0, other arithmetic: 2.05 us -> none  [return_sums(): arrived.reshape(groups, shards, capacity, columns).astype(jnp.float32)]
  transfers between devices with their start and end apart: 6 -> 24, of which waited for: 4 -> 9; matrix products, arithmetic and copies ran while one was open for 8% -> 9% of each run, Pallas kernels for 0% -> 0%
where the time goes in v1:
time: 87 us; the launch traced here: 86.6 us
  starting transfers between devices  37.4 us (43%)
  waiting for transfers between devices  33.2 us (38%)
  matrix products  6.97 us (8%)
  other arithmetic  5.03 us (6%)
  local copies, waits for them, and re-layouts  2.92 us (3%)
  between operations  1.05 us (1%)
    ppermute x24, starting transfers between devices, swap(): lax.ppermute(value, 'expert', [(i, i ^ mask_of(i)) for i in range(size)])  37.4 us
    ppermute x24, waiting for transfers between devices, swap(): lax.ppermute(value, 'expert', [(i, i ^ mask_of(i)) for i in range(size)])  33.2 us
    unnamed x24, local copies, waits for them, and re-layouts  2.11 us
  transfers between devices with their start and end apart: 24, of which 9 were waited for; matrix products, arithmetic and copies ran while one was open for 9% of the time, Pallas kernels for 0%

profile of v1, /device:TPU:0, one launch (start us, length us, event | category | flops | bytes accessed | tf_op | source)
XLA Modules:
  0.0 86.6 jit_solution(9403952380319948285)
XLA Ops:
  0.7 0.8 copy.22
  1.4 0.8 copy.24
  2.8 0.8 select_reduce_fusion
  3.5 1.2 %convolution_convert_fusion = bf16[32,3584]{1,0:T(8,128)(2,1)S(1)} fusion(f32[8,32]{1,0:T(8,128)S(1)} %get-tuple-element.4, bf16[8,3584]{1,0:T(8,128)(2,1)} %param.13), kind=kOutput, calls=%fused_computation | convolution fusion | flops 11124736 | bytes 287744 | tf_op jit(solution)/shard_map/dot_general | solution.py:145
  4.8 3.1 %collective-permute-start.13 = (bf16[8,3584]{1,0:T(8,128)(2,1)S(1)}, bf16[8,3584]{1,0:T(8,128)(2,1)S(1)}, u32[]{:S(2)}, u32[]{:S(2)}) collective-permute-start(bf16[8,3584]{1,0:T(8,128)(2,1)S(1)} %get-tuple-element.18), channel_id=1, source_target_pairs={{0,8},{1,9},{2,10},{3,11},{4,12},{5,13},{6,14},{7,15},{8,0},{9,1},... | collective-permute-start | bytes 172040 | tf_op jit(solution)/shard_map/ppermute | solution.py:21
  7.8 2.6 %collective-permute-start.14 = (bf16[8,3584]{1,0:T(8,128)(2,1)S(1)}, bf16[8,3584]{1,0:T(8,128)(2,1)S(1)}, u32[]{:S(2)}, u32[]{:S(2)}) collective-permute-start(bf16[8,3584]{1,0:T(8,128)(2,1)S(1)} %get-tuple-element.17), channel_id=1, source_target_pairs={{0,16},{1,17},{2,18},{3,19},{4,20},{5,21},{6,22},{7,23},{8,24},{9,... | collective-permute-start | bytes 172040 | tf_op jit(solution)/shard_map/ppermute | solution.py:21
  12.0 1.0 %fusion.35 = f32[8]{0:T(128)S(1)} fusion(bf16[8,3584]{1,0:T(8,128)(2,1)} %param.12), kind=kLoop, calls=%fused_computation.64 | loop fusion | flops 86008 | bytes 57376 | tf_op jit(solution)/shard_map/reduce_sum | solution.py:53
  13.0 0.8 reduce
  13.8 0.8 convert_reduce_fusion.1
  14.6 1.1 %convolution_convert_fusion.1 = bf16[32,3584]{1,0:T(8,128)(2,1)S(1)} fusion(bf16[8,3584]{1,0:T(8,128)(2,1)} %param.12, f32[3584]{0:T(1024)S(1)} %reduce, f32[8]{0:T(128)S(1)} %add_rsqrt_fusion.1, bf16[8,32]{1,0:T(8,128)(2,1)S(1)} %get-tuple-element.6), kind=kOutput, calls=%fused_computation.1 | convolution fusion | flops 2064384 | bytes 301600 | tf_op jit(solution)/shard_map/dot_general | solution.py:140
  15.9 1.0 %collective-permute-start = (bf16[8,3584]{1,0:T(8,128)(2,1)S(1)}, bf16[8,3584]{1,0:T(8,128)(2,1)S(1)}, u32[]{:S(2)}, u32[]{:S(2)}) collective-permute-start(bf16[8,3584]{1,0:T(8,128)(2,1)S(1)} %get-tuple-element.30), channel_id=1, source_target_pairs={{0,8},{1,9},{2,10},{3,11},{4,12},{5,13},{6,14},{7,15},{8,0},{9,1},... | collective-permute-start | bytes 172040 | tf_op jit(solution)/shard_map/ppermute | solution.py:21
  16.9 3.6 %collective-permute-start.1 = (bf16[8,3584]{1,0:T(8,128)(2,1)S(1)}, bf16[8,3584]{1,0:T(8,128)(2,1)S(1)}, u32[]{:S(2)}, u32[]{:S(2)}) collective-permute-start(bf16[8,3584]{1,0:T(8,128)(2,1)S(1)} %get-tuple-element.29), channel_id=1, source_target_pairs={{0,16},{1,17},{2,18},{3,19},{4,20},{5,21},{6,22},{7,23},{8,24},{9,... | collective-permute-start | bytes 172040 | tf_op jit(solution)/shard_map/ppermute | solution.py:21
  20.5 4.8 %collective-permute-start.2 = (bf16[8,3584]{1,0:T(8,128)(2,1)S(1)}, bf16[8,3584]{1,0:T(8,128)(2,1)S(1)}, u32[]{:S(2)}, u32[]{:S(2)}) collective-permute-start(bf16[8,3584]{1,0:T(8,128)(2,1)S(1)} %get-tuple-element.28), channel_id=1, source_target_pairs={{0,24},{1,25},{2,26},{3,27},{4,28},{5,29},{6,30},{7,31},{8,16},{9,... | collective-permute-start | bytes 172040 | tf_op jit(solution)/shard_map/ppermute | solution.py:21
  25.4 2.0 %collective-permute-done.2 = bf16[8,3584]{1,0:T(8,128)(2,1)S(1)} collective-permute-done((bf16[8,3584]{1,0:T(8,128)(2,1)S(1)}, bf16[8,3584]{1,0:T(8,128)(2,1)S(1)}, u32[]{:S(2)}, u32[]{:S(2)}) %collective-permute-start.2) | collective-permute-done | bytes 57376 | tf_op jit(solution)/shard_map/ppermute | solution.py:21
  27.4 1.5 %collective-permute-start.16 = (bf16[32,3584]{1,0:T(8,128)(2,1)S(1)}, bf16[32,3584]{1,0:T(8,128)(2,1)S(1)}, u32[]{:S(2)}, u32[]{:S(2)}) collective-permute-start(bf16[32,3584]{1,0:T(8,128)(2,1)S(1)} %pad_maximum_fusion.7), channel_id=1, source_target_pairs={{0,2},{1,5},{2,0},{3,7},{4,6},{5,1},{6,4},{7,3},{8,10},{9,13},{10,... | collective-permute-start | bytes 688136 | tf_op jit(solution)/shard_map/ppermute | solution.py:21
  29.6 3.8 %collective-permute-done.16 = bf16[32,3584]{1,0:T(8,128)(2,1)S(1)} collective-permute-done((bf16[32,3584]{1,0:T(8,128)(2,1)S(1)}, bf16[32,3584]{1,0:T(8,128)(2,1)S(1)}, u32[]{:S(2)}, u32[]{:S(2)}) %collective-permute-start.16) | collective-permute-done | bytes 229408 | tf_op jit(solution)/shard_map/ppermute | solution.py:21
  33.5 1.6 %collective-permute-start.17 = (bf16[64,3584]{1,0:T(8,128)(2,1)S(1)}, bf16[64,3584]{1,0:T(8,128)(2,1)S(1)}, u32[]{:S(2)}, u32[]{:S(2)}) collective-permute-start(bf16[64,3584]{1,0:T(8,128)(2,1)S(1)} %get-tuple-element.12), channel_id=1, source_target_pairs={{0,4},{1,3},{2,6},{3,1},{4,0},{5,7},{6,2},{7,5},{8,12},{9,11},{10,... | collective-permute-start | bytes 1376264 | tf_op jit(solution)/shard_map/ppermute | solution.py:21
  35.1 3.2 %collective-permute-done.3 = bf16[32,3584]{1,0:T(8,128)(2,1)S(1)} collective-permute-done((bf16[32,3584]{1,0:T(8,128)(2,1)S(1)}, bf16[32,3584]{1,0:T(8,128)(2,1)S(1)}, u32[]{:S(2)}, u32[]{:S(2)}) %collective-permute-start.3) | collective-permute-done | bytes 229408 | tf_op jit(solution)/shard_map/ppermute | solution.py:21
  38.3 1.6 %collective-permute-start.4 = (bf16[64,3584]{1,0:T(8,128)(2,1)S(1)}, bf16[64,3584]{1,0:T(8,128)(2,1)S(1)}, u32[]{:S(2)}, u32[]{:S(2)}) collective-permute-start(bf16[64,3584]{1,0:T(8,128)(2,1)S(1)} %get-tuple-element.24), channel_id=1, source_target_pairs={{0,4},{1,3},{2,6},{3,1},{4,0},{5,7},{6,2},{7,5},{8,12},{9,11},{10,... | collective-permute-start | bytes 1376264 | tf_op jit(solution)/shard_map/ppermute | solution.py:21
  39.9 2.1 %collective-permute-done.17 = bf16[64,3584]{1,0:T(8,128)(2,1)S(1)} collective-permute-done((bf16[64,3584]{1,0:T(8,128)(2,1)S(1)}, bf16[64,3584]{1,0:T(8,128)(2,1)S(1)}, u32[]{:S(2)}, u32[]{:S(2)}) %collective-permute-start.17) | collective-permute-done | bytes 458784 | tf_op jit(solution)/shard_map/ppermute | solution.py:21
  42.1 4.9 %collective-permute-done.4 = bf16[64,3584]{1,0:T(8,128)(2,1)S(1)} collective-permute-done((bf16[64,3584]{1,0:T(8,128)(2,1)S(1)}, bf16[64,3584]{1,0:T(8,128)(2,1)S(1)}, u32[]{:S(2)}, u32[]{:S(2)}) %collective-permute-start.4) | collective-permute-done | bytes 458784 | tf_op jit(solution)/shard_map/ppermute | solution.py:21
  48.2 1.3 %fusion.3 = f32[128,3584]{1,0:T(8,128)S(1)} fusion(bf16[3584,128]{1,0:T(8,128)(2,1)S(1)} %collective-permute-done.6, bf16[3584,128]{1,0:T(8,128)(2,1)S(1)} %bitcast.19, bf16[3584,128]{1,0:T(8,128)(2,1)S(1)} %collective-permute-done.5, bf16[3584,128]{1,0:T(8,128)(2,1)S(1)} %bitcast.22, bf16[128,256]{1,0:T(8,128)(2,1)S(1)} %get-tuple-element.33, ...), kind=kOutput, calls=%fused_computation.15 | convolution fusion | flops 484704256 | bytes 5636096 | tf_op jit(solution)/shard_map/rh,dh->rd/dot_general | solution.py:159
  49.6 1.6 %collective-permute-start.19 = (bf16[64,3584]{1,0:T(8,128)(2,1)S(1)}, bf16[64,3584]{1,0:T(8,128)(2,1)S(1)}, u32[]{:S(2)}, u32[]{:S(2)}) collective-permute-start(bf16[64,3584]{1,0:T(8,128)(2,1)S(1)} %slice.176), channel_id=1, source_target_pairs={{0,4},{1,3},{2,6},{3,1},{4,0},{5,7},{6,2},{7,5},{8,12},{9,11},{10,... | collective-permute-start | bytes 1376264 | tf_op jit(solution)/shard_map/ppermute | solution.py:21
  52.9 5.2 %collective-permute-done.19 = bf16[64,3584]{1,0:T(8,128)(2,1)S(1)} collective-permute-done((bf16[64,3584]{1,0:T(8,128)(2,1)S(1)}, bf16[64,3584]{1,0:T(8,128)(2,1)S(1)}, u32[]{:S(2)}, u32[]{:S(2)}) %collective-permute-start.19) | collective-permute-done | bytes 458784 | tf_op jit(solution)/shard_map/ppermute | solution.py:21
  58.3 1.6 %collective-permute-start.20 = (bf16[32,3584]{1,0:T(8,128)(2,1)S(1)}, bf16[32,3584]{1,0:T(8,128)(2,1)S(1)}, u32[]{:S(2)}, u32[]{:S(2)}) collective-permute-start(bf16[32,3584]{1,0:T(8,128)(2,1)S(1)} %slice.178), channel_id=1, source_target_pairs={{0,2},{1,5},{2,0},{3,7},{4,6},{5,1},{6,4},{7,3},{8,10},{9,13},{10,... | collective-permute-start | bytes 688136 | tf_op jit(solution)/shard_map/ppermute | solution.py:21
  59.8 7.2 %collective-permute-done.8 = bf16[64,3584]{1,0:T(8,128)(2,1)S(1)} collective-permute-done((bf16[64,3584]{1,0:T(8,128)(2,1)S(1)}, bf16[64,3584]{1,0:T(8,128)(2,1)S(1)}, u32[]{:S(2)}, u32[]{:S(2)}) %collective-permute-start.8) | collective-permute-done | bytes 458784 | tf_op jit(solution)/shard_map/ppermute | solution.py:21
  67.2 1.6 %collective-permute-start.9 = (bf16[32,3584]{1,0:T(8,128)(2,1)S(1)}, bf16[32,3584]{1,0:T(8,128)(2,1)S(1)}, u32[]{:S(2)}, u32[]{:S(2)}) collective-permute-start(bf16[32,3584]{1,0:T(8,128)(2,1)S(1)} %slice.179), channel_id=1, source_target_pairs={{0,2},{1,5},{2,0},{3,7},{4,6},{5,1},{6,4},{7,3},{8,10},{9,13},{10,... | collective-permute-start | bytes 688136 | tf_op jit(solution)/shard_map/ppermute | solution.py:21
  68.9 6.3 %collective-permute-start.22 = (bf16[8,3584]{1,0:T(8,128)(2,1)S(1)}, bf16[8,3584]{1,0:T(8,128)(2,1)S(1)}, u32[]{:S(2)}, u32[]{:S(2)}) collective-permute-start(bf16[8,3584]{1,0:T(8,128)(2,1)S(1)} %get-tuple-element.10), channel_id=1, source_target_pairs={{0,16},{1,17},{2,18},{3,19},{4,20},{5,21},{6,22},{7,23},{8,24},{9,... | collective-permute-start | bytes 172040 | tf_op jit(solution)/shard_map/ppermute | solution.py:21
  75.9 3.8 %collective-permute-start.11 = (bf16[8,3584]{1,0:T(8,128)(2,1)S(1)}, bf16[8,3584]{1,0:T(8,128)(2,1)S(1)}, u32[]{:S(2)}, u32[]{:S(2)}) collective-permute-start(bf16[8,3584]{1,0:T(8,128)(2,1)S(1)} %get-tuple-element.22), channel_id=1, source_target_pairs={{0,16},{1,17},{2,18},{3,19},{4,20},{5,21},{6,22},{7,23},{8,24},{9,... | collective-permute-start | bytes 172040 | tf_op jit(solution)/shard_map/ppermute | solution.py:21
  80.1 1.1 %collective-permute-done.23 = bf16[8,3584]{1,0:T(8,128)(2,1)S(1)} collective-permute-done((bf16[8,3584]{1,0:T(8,128)(2,1)S(1)}, bf16[8,3584]{1,0:T(8,128)(2,1)S(1)}, u32[]{:S(2)}, u32[]{:S(2)}) %collective-permute-start.23) | collective-permute-done | bytes 57376 | tf_op jit(solution)/shard_map/ppermute | solution.py:21
  82.3 3.4 %collective-permute-done.12 = bf16[8,3584]{1,0:T(8,128)(2,1)S(1)} collective-permute-done((bf16[8,3584]{1,0:T(8,128)(2,1)S(1)}, bf16[8,3584]{1,0:T(8,128)(2,1)S(1)}, u32[]{:S(2)}, u32[]{:S(2)}) %collective-permute-start.12) | collective-permute-done | bytes 57376 | tf_op jit(solution)/shard_map/ppermute | solution.py:21
  85.7 0.8 fusion
  (92 shorter events, 8.6 us)
Async XLA Ops:
  0.6 9.8 %copy-start = (bf16[1,1,32,8,256]{4,3,2,1,0:T(8,128)(2,1)S(1)}, bf16[1,1,32,8,256]{4,3,2,1,0:T(8,128)(2,1)}, u32[]{:S(2)}) copy-start(bf16[1,1,32,8,256]{4,3,2,1,0:T(8,128)(2,1)} %param.23) | copy-start | bytes 393220
  4.8 11.0 %collective-permute-start.13 = (bf16[8,3584]{1,0:T(8,128)(2,1)S(1)}, bf16[8,3584]{1,0:T(8,128)(2,1)S(1)}, u32[]{:S(2)}, u32[]{:S(2)}) collective-permute-start(bf16[8,3584]{1,0:T(8,128)(2,1)S(1)} %get-tuple-element.18), channel_id=1, source_target_pairs={{0,8},{1,9},{2,10},{3,11},{4,12},{5,13},{6,14},{7,15},{8,0},{9,1},... | collective-permute-start | bytes 172040 | tf_op jit(solution)/shard_map/ppermute | solution.py:21
  7.8 8.1 %collective-permute-start.14 = (bf16[8,3584]{1,0:T(8,128)(2,1)S(1)}, bf16[8,3584]{1,0:T(8,128)(2,1)S(1)}, u32[]{:S(2)}, u32[]{:S(2)}) collective-permute-start(bf16[8,3584]{1,0:T(8,128)(2,1)S(1)} %get-tuple-element.17), channel_id=1, source_target_pairs={{0,16},{1,17},{2,18},{3,19},{4,20},{5,21},{6,22},{7,23},{8,24},{9,... | collective-permute-start | bytes 172040 | tf_op jit(solution)/shard_map/ppermute | solution.py:21
  10.4 6.5 %collective-permute-start.15 = (bf16[8,3584]{1,0:T(8,128)(2,1)S(1)}, bf16[8,3584]{1,0:T(8,128)(2,1)S(1)}, u32[]{:S(2)}, u32[]{:S(2)}) collective-permute-start(bf16[8,3584]{1,0:T(8,128)(2,1)S(1)} %get-tuple-element.16), channel_id=1, source_target_pairs={{0,24},{1,25},{2,26},{3,27},{4,28},{5,29},{6,30},{7,31},{8,16},{9,... | collective-permute-start | bytes 172040 | tf_op jit(solution)/shard_map/ppermute | solution.py:21
  10.7 18.3 %collective-permute-start.18 = (bf16[128,256]{1,0:T(8,128)(2,1)S(1)}, bf16[128,256]{1,0:T(8,128)(2,1)S(1)}, u32[]{:S(2)}, u32[]{:S(2)}) collective-permute-start(bf16[128,256]{1,0:T(8,128)(2,1)S(1)} %convolution_convert_fusion.2), channel_id=1, source_target_pairs={{0,1},{1,0},{2,3},{3,2},{4,5},{5,4},{6,7},{7,6},{8,9},{9,8},{10,11... | collective-permute-start | bytes 196616 | tf_op jit(solution)/shard_map/ppermute | solution.py:21
  10.7 36.2 %collective-permute-start.7 = (bf16[128,3584]{1,0:T(8,128)(2,1)}, bf16[128,3584]{1,0:T(8,128)(2,1)S(1)}, u32[]{:S(2)}, u32[]{:S(2)}) collective-permute-start(bf16[128,3584]{1,0:T(8,128)(2,1)} %bitcast.15), channel_id=1, source_target_pairs={{0,1},{1,0},{2,3},{3,2},{4,5},{5,4},{6,7},{7,6},{8,9},{9,8},{10,11... | collective-permute-start | bytes 2752520 | tf_op jit(solution)/shard_map/ppermute | solution.py:21
  13.7 11.6 %copy-start.5 = (bf16[1,1,3584,128]{3,2,1,0:T(8,128)(2,1)S(1)}, bf16[1,1,3584,128]{3,2,1,0:T(8,128)(2,1)}, u32[]{:S(2)}) copy-start(bf16[1,1,3584,128]{3,2,1,0:T(8,128)(2,1)} %param.21) | copy-start | bytes 2752516
  15.7 32.0 %collective-permute-start.5 = (bf16[3584,128]{1,0:T(8,128)(2,1)}, bf16[3584,128]{1,0:T(8,128)(2,1)S(1)}, u32[]{:S(2)}, u32[]{:S(2)}) collective-permute-start(bf16[3584,128]{1,0:T(8,128)(2,1)} %bitcast.21), channel_id=1, source_target_pairs={{0,1},{1,0},{2,3},{3,2},{4,5},{5,4},{6,7},{7,6},{8,9},{9,8},{10,11... | collective-permute-start | bytes 2752520 | tf_op jit(solution)/shard_map/ppermute | solution.py:21
  15.9 4.6 %collective-permute-start = (bf16[8,3584]{1,0:T(8,128)(2,1)S(1)}, bf16[8,3584]{1,0:T(8,128)(2,1)S(1)}, u32[]{:S(2)}, u32[]{:S(2)}) collective-permute-start(bf16[8,3584]{1,0:T(8,128)(2,1)S(1)} %get-tuple-element.30), channel_id=1, source_target_pairs={{0,8},{1,9},{2,10},{3,11},{4,12},{5,13},{6,14},{7,15},{8,0},{9,1},... | collective-permute-start | bytes 172040 | tf_op jit(solution)/shard_map/ppermute | solution.py:21
  16.9 8.4 %collective-permute-start.1 = (bf16[8,3584]{1,0:T(8,128)(2,1)S(1)}, bf16[8,3584]{1,0:T(8,128)(2,1)S(1)}, u32[]{:S(2)}, u32[]{:S(2)}) collective-permute-start(bf16[8,3584]{1,0:T(8,128)(2,1)S(1)} %get-tuple-element.29), channel_id=1, source_target_pairs={{0,16},{1,17},{2,18},{3,19},{4,20},{5,21},{6,22},{7,23},{8,24},{9,... | collective-permute-start | bytes 172040 | tf_op jit(solution)/shard_map/ppermute | solution.py:21
  20.5 6.9 %collective-permute-start.2 = (bf16[8,3584]{1,0:T(8,128)(2,1)S(1)}, bf16[8,3584]{1,0:T(8,128)(2,1)S(1)}, u32[]{:S(2)}, u32[]{:S(2)}) collective-permute-start(bf16[8,3584]{1,0:T(8,128)(2,1)S(1)} %get-tuple-element.28), channel_id=1, source_target_pairs={{0,24},{1,25},{2,26},{3,27},{4,28},{5,29},{6,30},{7,31},{8,16},{9,... | collective-permute-start | bytes 172040 | tf_op jit(solution)/shard_map/ppermute | solution.py:21
  25.3 22.5 %collective-permute-start.6 = (bf16[3584,128]{1,0:T(8,128)(2,1)S(1)}, bf16[3584,128]{1,0:T(8,128)(2,1)S(1)}, u32[]{:S(2)}, u32[]{:S(2)}) collective-permute-start(bf16[3584,128]{1,0:T(8,128)(2,1)S(1)} %bitcast.18), channel_id=1, source_target_pairs={{0,1},{1,0},{2,3},{3,2},{4,5},{5,4},{6,7},{7,6},{8,9},{9,8},{10,11... | collective-permute-start | bytes 2752520 | tf_op jit(solution)/shard_map/ppermute | solution.py:21
  27.4 6.0 %collective-permute-start.16 = (bf16[32,3584]{1,0:T(8,128)(2,1)S(1)}, bf16[32,3584]{1,0:T(8,128)(2,1)S(1)}, u32[]{:S(2)}, u32[]{:S(2)}) collective-permute-start(bf16[32,3584]{1,0:T(8,128)(2,1)S(1)} %pad_maximum_fusion.7), channel_id=1, source_target_pairs={{0,2},{1,5},{2,0},{3,7},{4,6},{5,1},{6,4},{7,3},{8,10},{9,13},{10,... | collective-permute-start | bytes 688136 | tf_op jit(solution)/shard_map/ppermute | solution.py:21
  29.0 18.1 %copy-start.1 = (bf16[1,1,128,3584]{3,2,1,0:T(8,128)(2,1)S(1)}, bf16[1,1,128,3584]{3,2,1,0:T(8,128)(2,1)}, u32[]{:S(2)}) copy-start(bf16[1,1,128,3584]{3,2,1,0:T(8,128)(2,1)} %param.22) | copy-start | bytes 2752516
  29.0 9.3 %collective-permute-start.3 = (bf16[32,3584]{1,0:T(8,128)(2,1)S(1)}, bf16[32,3584]{1,0:T(8,128)(2,1)S(1)}, u32[]{:S(2)}, u32[]{:S(2)}) collective-permute-start(bf16[32,3584]{1,0:T(8,128)(2,1)S(1)} %pad_maximum_fusion.6), channel_id=1, source_target_pairs={{0,2},{1,5},{2,0},{3,7},{4,6},{5,1},{6,4},{7,3},{8,10},{9,13},{10,... | collective-permute-start | bytes 688136 | tf_op jit(solution)/shard_map/ppermute | solution.py:21
  33.5 8.5 %collective-permute-start.17 = (bf16[64,3584]{1,0:T(8,128)(2,1)S(1)}, bf16[64,3584]{1,0:T(8,128)(2,1)S(1)}, u32[]{:S(2)}, u32[]{:S(2)}) collective-permute-start(bf16[64,3584]{1,0:T(8,128)(2,1)S(1)} %get-tuple-element.12), channel_id=1, source_target_pairs={{0,4},{1,3},{2,6},{3,1},{4,0},{5,7},{6,2},{7,5},{8,12},{9,11},{10,... | collective-permute-start | bytes 1376264 | tf_op jit(solution)/shard_map/ppermute | solution.py:21
  38.3 8.6 %collective-permute-start.4 = (bf16[64,3584]{1,0:T(8,128)(2,1)S(1)}, bf16[64,3584]{1,0:T(8,128)(2,1)S(1)}, u32[]{:S(2)}, u32[]{:S(2)}) collective-permute-start(bf16[64,3584]{1,0:T(8,128)(2,1)S(1)} %get-tuple-element.24), channel_id=1, source_target_pairs={{0,4},{1,3},{2,6},{3,1},{4,0},{5,7},{6,2},{7,5},{8,12},{9,11},{10,... | collective-permute-start | bytes 1376264 | tf_op jit(solution)/shard_map/ppermute | solution.py:21
  47.0 1.2 %copy-start.6 = (bf16[1,1,3584,128]{3,2,1,0:T(8,128)(2,1)S(1)}, bf16[1,1,3584,128]{3,2,1,0:T(8,128)(2,1)}, u32[]{:S(2)}) copy-start(bf16[1,1,3584,128]{3,2,1,0:T(8,128)(2,1)} %param.20) | copy-start | bytes 2752516
  49.6 8.5 %collective-permute-start.19 = (bf16[64,3584]{1,0:T(8,128)(2,1)S(1)}, bf16[64,3584]{1,0:T(8,128)(2,1)S(1)}, u32[]{:S(2)}, u32[]{:S(2)}) collective-permute-start(bf16[64,3584]{1,0:T(8,128)(2,1)S(1)} %slice.176), channel_id=1, source_target_pairs={{0,4},{1,3},{2,6},{3,1},{4,0},{5,7},{6,2},{7,5},{8,12},{9,11},{10,... | collective-permute-start | bytes 1376264 | tf_op jit(solution)/shard_map/ppermute | solution.py:21
  52.3 14.7 %collective-permute-start.8 = (bf16[64,3584]{1,0:T(8,128)(2,1)S(1)}, bf16[64,3584]{1,0:T(8,128)(2,1)S(1)}, u32[]{:S(2)}, u32[]{:S(2)}) collective-permute-start(bf16[64,3584]{1,0:T(8,128)(2,1)S(1)} %slice.177), channel_id=1, source_target_pairs={{0,4},{1,3},{2,6},{3,1},{4,0},{5,7},{6,2},{7,5},{8,12},{9,11},{10,... | collective-permute-start | bytes 1376264 | tf_op jit(solution)/shard_map/ppermute | solution.py:21
  58.3 10.5 %collective-permute-start.20 = (bf16[32,3584]{1,0:T(8,128)(2,1)S(1)}, bf16[32,3584]{1,0:T(8,128)(2,1)S(1)}, u32[]{:S(2)}, u32[]{:S(2)}) collective-permute-start(bf16[32,3584]{1,0:T(8,128)(2,1)S(1)} %slice.178), channel_id=1, source_target_pairs={{0,2},{1,5},{2,0},{3,7},{4,6},{5,1},{6,4},{7,3},{8,10},{9,13},{10,... | collective-permute-start | bytes 688136 | tf_op jit(solution)/shard_map/ppermute | solution.py:21
  67.1 14.1 %copy-start.4 = (bf16[8,3584]{1,0:T(8,128)(2,1)S(1)}, bf16[8,3584]{1,0:T(8,128)(2,1)}, u32[]{:S(2)}) copy-start(bf16[8,3584]{1,0:T(8,128)(2,1)} %param.14) | copy-start | bytes 172036
  67.2 14.4 %copy-start.3 = (bf16[8,3584]{1,0:T(8,128)(2,1)S(1)}, bf16[8,3584]{1,0:T(8,128)(2,1)}, u32[]{:S(2)}) copy-start(bf16[8,3584]{1,0:T(8,128)(2,1)} %param.13) | copy-start | bytes 172036
  67.2 18.6 %copy-start.2 = (bf16[8,3584]{1,0:T(8,128)(2,1)S(1)}, bf16[8,3584]{1,0:T(8,128)(2,1)}, u32[]{:S(2)}) copy-start(bf16[8,3584]{1,0:T(8,128)(2,1)} %param.12) | copy-start | bytes 172036
  67.2 8.0 %collective-permute-start.9 = (bf16[32,3584]{1,0:T(8,128)(2,1)S(1)}, bf16[32,3584]{1,0:T(8,128)(2,1)S(1)}, u32[]{:S(2)}, u32[]{:S(2)}) collective-permute-start(bf16[32,3584]{1,0:T(8,128)(2,1)S(1)} %slice.179), channel_id=1, source_target_pairs={{0,2},{1,5},{2,0},{3,7},{4,6},{5,1},{6,4},{7,3},{8,10},{9,13},{10,... | collective-permute-start | bytes 688136 | tf_op jit(solution)/shard_map/ppermute | solution.py:21
  68.8 10.9 %collective-permute-start.21 = (bf16[8,3584]{1,0:T(8,128)(2,1)S(1)}, bf16[8,3584]{1,0:T(8,128)(2,1)S(1)}, u32[]{:S(2)}, u32[]{:S(2)}) collective-permute-start(bf16[8,3584]{1,0:T(8,128)(2,1)S(1)} %get-tuple-element.11), channel_id=1, source_target_pairs={{0,8},{1,9},{2,10},{3,11},{4,12},{5,13},{6,14},{7,15},{8,0},{9,1},... | collective-permute-start | bytes 172040 | tf_op jit(solution)/shard_map/ppermute | solution.py:21
  68.9 11.2 %collective-permute-start.22 = (bf16[8,3584]{1,0:T(8,128)(2,1)S(1)}, bf16[8,3584]{1,0:T(8,128)(2,1)S(1)}, u32[]{:S(2)}, u32[]{:S(2)}) collective-permute-start(bf16[8,3584]{1,0:T(8,128)(2,1)S(1)} %get-tuple-element.10), channel_id=1, source_target_pairs={{0,16},{1,17},{2,18},{3,19},{4,20},{5,21},{6,22},{7,23},{8,24},{9,... | collective-permute-start | bytes 172040 | tf_op jit(solution)/shard_map/ppermute | solution.py:21
  75.2 6.0 %collective-permute-start.23 = (bf16[8,3584]{1,0:T(8,128)(2,1)S(1)}, bf16[8,3584]{1,0:T(8,128)(2,1)S(1)}, u32[]{:S(2)}, u32[]{:S(2)}) collective-permute-start(bf16[8,3584]{1,0:T(8,128)(2,1)S(1)} %get-tuple-element.9), channel_id=1, source_target_pairs={{0,24},{1,25},{2,26},{3,27},{4,28},{5,29},{6,30},{7,31},{8,16},{9,... | collective-permute-start | bytes 172040 | tf_op jit(solution)/shard_map/ppermute | solution.py:21
  75.3 7.0 %collective-permute-start.10 = (bf16[8,3584]{1,0:T(8,128)(2,1)S(1)}, bf16[8,3584]{1,0:T(8,128)(2,1)S(1)}, u32[]{:S(2)}, u32[]{:S(2)}) collective-permute-start(bf16[8,3584]{1,0:T(8,128)(2,1)S(1)} %get-tuple-element.23), channel_id=1, source_target_pairs={{0,8},{1,9},{2,10},{3,11},{4,12},{5,13},{6,14},{7,15},{8,0},{9,1},... | collective-permute-start | bytes 172040 | tf_op jit(solution)/shard_map/ppermute | solution.py:21
  75.9 6.4 %collective-permute-start.11 = (bf16[8,3584]{1,0:T(8,128)(2,1)S(1)}, bf16[8,3584]{1,0:T(8,128)(2,1)S(1)}, u32[]{:S(2)}, u32[]{:S(2)}) collective-permute-start(bf16[8,3584]{1,0:T(8,128)(2,1)S(1)} %get-tuple-element.22), channel_id=1, source_target_pairs={{0,16},{1,17},{2,18},{3,19},{4,20},{5,21},{6,22},{7,23},{8,24},{9,... | collective-permute-start | bytes 172040 | tf_op jit(solution)/shard_map/ppermute | solution.py:21
  79.8 6.0 %collective-permute-start.12 = (bf16[8,3584]{1,0:T(8,128)(2,1)S(1)}, bf16[8,3584]{1,0:T(8,128)(2,1)S(1)}, u32[]{:S(2)}, u32[]{:S(2)}) collective-permute-start(bf16[8,3584]{1,0:T(8,128)(2,1)S(1)} %get-tuple-element.21), channel_id=1, source_target_pairs={{0,24},{1,25},{2,26},{3,27},{4,28},{5,29},{6,30},{7,31},{8,16},{9,... | collective-permute-start | bytes 172040 | tf_op jit(solution)/shard_map/ppermute | solution.py:21

commit v2 on v1

--- a/solution.py
+++ b/solution.py
@@ -1,6 +1,10 @@
+import functools
+
 import jax
 import jax.numpy as jnp
 from jax import lax
+from jax.experimental import pallas as pl
+from jax.experimental.pallas import tpu as pltpu
 from jax.sharding import PartitionSpec as P
 
 EPSILON = 1e-06
@@ -33,20 +37,68 @@
     return swap(value, lambda i: 2 if i & 1 else 4)
 
 
-def slot_tables(routes, gates, experts, capacity):
-    tokens_here = routes.shape[0]
-    chosen = routes.reshape(-1)
-    onehot = (chosen[:, None] == jnp.arange(experts, dtype=jnp.int32)[None, :]).astype(jnp.int32)
-    earlier = jnp.cumsum(onehot, axis=0) - onehot
-    within = jnp.sum(earlier * onehot, axis=1)
-    target = chosen * capacity + within
-    slot_table = (
-        target[:, None] == jnp.arange(experts * capacity, dtype=jnp.int32)[None, :]
-    ).astype(F32)
-    slot_table = slot_table.reshape(tokens_here, routes.shape[1], experts * capacity)
-    occupancy = jnp.sum(slot_table, axis=1).T
-    weighted = jnp.sum(slot_table * gates[:, :, None], axis=1)
-    return (occupancy, weighted)
+def slot_table(routes, gates, experts, capacity):
+    tokens = routes.shape[1]
+    slots = experts * capacity
+    slot = lax.broadcasted_iota(jnp.int32, (slots, tokens), 0)
+    token = lax.broadcasted_iota(jnp.int32, (slots, tokens), 1)
+    expert, place = slot // capacity, slot % capacity
+    first = routes[0:1, :] == expert
+    second = routes[1:2, :] == expert
+    named = jnp.where(first | second, 1.0, 0.0)
+    rank = jnp.zeros((slots, tokens), F32)
+    for t in range(tokens - 1):
+        rank = rank + jnp.where(token > t, named[:, t : t + 1], 0.0)
+    here = (named > 0.0) & (rank == place.astype(F32))
+    occupied = jnp.where(here, 1.0, 0.0)
+    weighted = jnp.where(here, jnp.where(first, gates[0:1, :], gates[1:2, :]), 0.0)
+    return occupied, weighted
+
+
+def prepare_kernel(
+    groups,
+    capacity,
+    inbound_ref,
+    cotangent_ref,
+    scale_ref,
+    routes_fwd_ref,
+    gates_fwd_ref,
+    routes_back_ref,
+    gates_back_ref,
+    rows_ref,
+    grad_rows_ref,
+    weighted_ref,
+    occupied_ref,
+):
+    occupied, weighted = slot_table(routes_fwd_ref[...], gates_fwd_ref[...], groups, capacity)
+    inbound = inbound_ref[...].astype(F32)
+    factor = lax.rsqrt(jnp.mean(inbound * inbound, axis=-1, keepdims=True) + EPSILON)
+    normed = (inbound * factor * scale_ref[...]).astype(BF16)
+    rows_ref[...] = jnp.dot(
+        occupied.astype(BF16), normed, preferred_element_type=F32
+    ).astype(BF16)
+    weighted_ref[...] = weighted
+    occupied, weighted = slot_table(routes_back_ref[...], gates_back_ref[...], groups, capacity)
+    gate = jnp.sum(weighted, axis=1, keepdims=True)
+    grad_rows_ref[...] = (
+        jnp.dot(occupied.astype(BF16), cotangent_ref[...], preferred_element_type=F32) * gate
+    ).astype(BF16)
+    occupied_ref[...] = occupied
+
+
+def prepare(groups, capacity, inbound, cotangent, scale, routes_fwd, gates_fwd, routes_back, gates_back):
+    tokens, columns = inbound.shape
+    slots = groups * capacity
+    return pl.pallas_call(
+        functools.partial(prepare_kernel, groups, capacity),
+        out_shape=(
+            jax.ShapeDtypeStruct((slots, columns), BF16),
+            jax.ShapeDtypeStruct((slots, columns), BF16),
+            jax.ShapeDtypeStruct((slots, tokens), F32),
+            jax.ShapeDtypeStruct((slots, tokens), F32),
+        ),
+        name="prepare",
+    )(inbound, cotangent, scale, routes_fwd, gates_fwd, routes_back, gates_back)
 
 
 def normalize(values, scale_row):
@@ -54,11 +106,14 @@
     return (values * factor * scale_row, factor)
 
 
-def dispatch(slot_rows, groups):
+def along_groups(slot_rows, groups):
     capacity = slot_rows.shape[0] // groups
     chunks = [slot_rows[k * capacity : (k + 1) * capacity] for k in range(groups)]
     arrived = [chunks[0]] + [swap(chunks[k], lambda i, k=k: 8 * k) for k in range(1, groups)]
-    own = jnp.concatenate(arrived, axis=0)
+    return jnp.concatenate(arrived, axis=0)
+
+
+def within_group(own):
     half = jnp.concatenate([own, with_first(own)], axis=0)
     return jnp.concatenate([half, with_second(half)], axis=0)
 
@@ -70,10 +125,7 @@
     summed = partial_value[:half] + arrived.astype(F32)
     arrived = with_first(summed[quarter:].astype(BF16))
     summed = (summed[:quarter] + arrived.astype(F32)).astype(BF16)
-    capacity = quarter // groups
-    chunks = [summed[k * capacity : (k + 1) * capacity] for k in range(groups)]
-    arrived = [chunks[0]] + [swap(chunks[k], lambda i, k=k: 8 * k) for k in range(1, groups)]
-    return jnp.concatenate(arrived, axis=0)
+    return along_groups(summed, groups)
 
 
 def stash_rows(stash_flat, group, place, core, groups, capacity):
@@ -115,12 +167,6 @@
     group, place, core = index // 8, index % 8, index % 2
     scale_row = norm_gain[0]
 
-    gate_other = with_core(w_gate[0, 0])
-    up_other = with_core(w_up[0, 0])
-    down_other = with_core(w_down[0, 0])
-    w_in = jnp.concatenate([w_gate[0, 0], gate_other, w_up[0, 0], up_other], axis=1)
-    w_out = jnp.concatenate([w_down[0, 0], down_other], axis=0)
-
     stash_flat = stash[0, 0].reshape(sources * capacity, 2 * hidden_dev)
     stash_own = stash_rows(stash_flat, group, place, core, groups, capacity)
     stash_other = with_core(stash_rows(stash_flat, group, place, 1 - core, groups, capacity))
@@ -133,22 +179,32 @@
 
     inbound = from_behind(act_send, "section", 1)
     cotangent = from_behind(grad_send, "section", -1)
-    occupancy_fwd, weighted_fwd = slot_tables(routes_fwd ^ group, gates_fwd, groups, capacity)
-    occupancy_back, weighted_back = slot_tables(routes_back ^ group, gates_back, groups, capacity)
-
-    normed = normalize(inbound.astype(F32), scale_row)[0].astype(BF16)
-    slot_rows = jnp.dot(
-        occupancy_fwd.astype(BF16), normed, preferred_element_type=F32
-    ).astype(BF16)
-    flat_rows = dispatch(slot_rows, groups)
-
-    grad_rows = jnp.dot(weighted_back.T, cotangent.astype(F32), precision=HIGHEST).astype(BF16)
-    grad_flat = dispatch(grad_rows, groups)
+    slot_rows, grad_rows, weighted_fwd, occupied_back = prepare(
+        groups,
+        capacity,
+        inbound,
+        cotangent,
+        norm_gain,
+        routes_fwd.T ^ group,
+        gates_fwd.T,
+        routes_back.T ^ group,
+        gates_back.T,
+    )
+    own = along_groups(slot_rows, groups)
+    w_gate, w_up, w_down, own = lax.optimization_barrier((w_gate, w_up, w_down, own))
+    gate_other = with_core(w_gate[0, 0])
+    up_other = with_core(w_up[0, 0])
+    down_other = with_core(w_down[0, 0])
+    w_in = jnp.concatenate([w_gate[0, 0], gate_other, w_up[0, 0], up_other], axis=1)
+    w_out = jnp.concatenate([w_down[0, 0], down_other], axis=0)
+    flat_rows = within_group(own)
+    grad_own = along_groups(grad_rows, groups)
+    grad_flat = within_group(grad_own)
 
     pre = jnp.dot(flat_rows, w_in, preferred_element_type=F32)
     hidden = (jax.nn.silu(pre[:, :hidden_two]) * pre[:, hidden_two:]).astype(BF16)
     summed = give_back(jnp.dot(hidden, w_out, preferred_element_type=F32), groups)
-    mixture = jnp.dot(weighted_fwd, summed.astype(F32), precision=HIGHEST)
+    mixture = jnp.dot(weighted_fwd.T, summed.astype(F32), precision=HIGHEST)
     outbound = (inbound.astype(F32) + mixture).astype(BF16)
 
     grad_hidden = jnp.einsum("rd,hd->rh", grad_flat, w_out, preferred_element_type=F32)
@@ -158,7 +214,7 @@
     d_pre = jnp.concatenate([d_gate, d_up], axis=1)
     grad_total = jnp.einsum("rh,dh->rd", d_pre, w_in, preferred_element_type=F32)
     grad_summed = give_back(grad_total, groups)
-    grad_normed = jnp.dot(occupancy_back.T, grad_summed.astype(F32), precision=HIGHEST)
+    grad_normed = jnp.dot(occupied_back.T, grad_summed.astype(F32), precision=HIGHEST)
     saved32 = x_back.astype(F32)
     factor = normalize(saved32, scale_row)[1]
     scaled_grad = grad_normed * scale_row

time: 87 us -> 69.9 us (0.80)
  waiting for transfers between devices: 33.2 us -> 21.8 us
  starting transfers between devices: 37.4 us -> 33.8 us
  matrix products: 6.97 us -> 4.83 us
  Pallas kernels: 0 us -> 1.94 us
  other arithmetic: 5.03 us -> 3.23 us
    ppermute x24, waiting for transfers between devices: 33.2 us -> 21.8 us  [swap(): lax.ppermute(value, 'expert', [(i, i ^ mask_of(i)) for i in range(size)])]
    ppermute x24, starting transfers between devices: 37.4 us -> 33.8 us  [swap(): lax.ppermute(value, 'expert', [(i, i ^ mask_of(i)) for i in range(size)])]
    reduce_sum x5 -> x0, other arithmetic: 2.95 us -> none  [the longest x1 0.98 us: normalize(): jnp.mean(values * values, axis=-1, keepdims=True) + EPSILON]
    dot_general x4 -> x2, matrix products: 3.45 us -> 1.29 us  [the longest x1 0.9 us: body(): mixture = jnp.dot(weighted_fwd.T, summed.astype(F32), precision=HIGHEST)]
    pallas_call x0 -> x1, Pallas kernels: none -> 1.94 us  [prepare(): pl.pallas_call(functools.partial(prepare_kernel, groups, capacity), out_s...]
    xor x1, other arithmetic: 0.01 us -> 1.36 us  [body(): routes_back.T ^ group]
    slice x2 -> x3, local copies, waits for them, and re-layouts: 0.04 us -> 0.95 us  [along_groups(): chunks = [slot_rows[k * capacity:(k + 1) * capacity] for k in range(groups)]]
    unnamed x24 -> x22, local copies, waits for them, and re-layouts: 2.11 us -> 1.7 us
  transfers between devices with their start and end apart: 24 -> 24, of which waited for: 9 -> 8; matrix products, arithmetic and copies ran while one was open for 9% -> 10% of each run, Pallas kernels for 0% -> 0%
where the time goes in v2:
time: 69.9 us; the launch traced here: 69.5 us
  starting transfers between devices  33.8 us (48%)
  waiting for transfers between devices  21.8 us (31%)
  matrix products  4.83 us (7%)
  other arithmetic  3.23 us (5%)
  local copies, waits for them, and re-layouts  2.87 us (4%)
  Pallas kernels  1.94 us (3%)
  between operations  1.03 us (1%)
    ppermute x24, starting transfers between devices, swap(): lax.ppermute(value, 'expert', [(i, i ^ mask_of(i)) for i in range(size)])  33.8 us
    ppermute x24, waiting for transfers between devices, swap(): lax.ppermute(value, 'expert', [(i, i ^ mask_of(i)) for i in range(size)])  21.8 us
    pallas_call x1, Pallas kernels, prepare(): pl.pallas_call(functools.partial(prepare_kernel, groups, capacity), out_s...  1.94 us
    unnamed x22, local copies, waits for them, and re-layouts  1.7 us
  transfers between devices with their start and end apart: 24, of which 8 were waited for; matrix products, arithmetic and copies ran while one was open for 10% of the time, Pallas kernels for 0%

profile of v2, /device:TPU:0, one launch (start us, length us, event | category | flops | bytes accessed | tf_op | source)
XLA Modules:
  0.0 69.5 jit_solution(14380470481523487166)
XLA Ops:
  0.7 1.4 %xor_bitcast_fusion = (s32[2,8]{1,0:T(2,128)}, s32[2,8]{1,0:T(2,128)}) fusion(s32[8,2]{0,1:T(2,128)} %param.17, s32[]{:T(128)S(6)} %select_n.126, s32[8,2]{0,1:T(2,128)} %param.15), kind=kLoop, calls=%fused_computation.103 | loop fusion | flops 32 | bytes 260 | tf_op jit(solution)/shard_map/xor | solution.py:190
  2.0 1.9 %prepare.1 = (bf16[32,3584]{1,0:T(8,128)(2,1)}, bf16[32,3584]{1,0:T(8,128)(2,1)}, f32[32,8]{1,0:T(8,128)}, f32[32,8]{1,0:T(8,128)}) custom-call(bf16[8,3584]{1,0:T(8,128)(2,1)} %inbound_ref.1, bf16[8,3584]{1,0:T(8,128)(2,1)} %cotangent_ref.1, f32[1,3584]{1,0:T(1,128)} %scale_ref.1, s32[2,8]{1,0:T(2,128)} %get-tuple-element.56.routes_fwd_ref, ...), custom_call_target="tpu_custom_call" | custom-call | tf_op jit(solution)/shard_map/prepare/pallas_call | solution.py:92
  4.0 0.9 %constant_dynamic-update-slice_fusion.4 = (bf16[64,3584]{1,0:T(8,128)(2,1)S(1)}, bf16[128,3584]{1,0:T(8,128)(2,1)S(1)}, bf16[8,3584]{1,0:T(8,128)(2,1)S(1)}, bf1...) fusion(bf16[32,3584]{1,0:T(8,128)(2,1)} %get-tuple-element.17), kind=kLoop, calls=%fused_computation.80 | loop fusion | bytes 573440
  4.9 3.1 %collective-permute-start.13 = (bf16[8,3584]{1,0:T(8,128)(2,1)S(1)}, bf16[8,3584]{1,0:T(8,128)(2,1)S(1)}, u32[]{:S(2)}, u32[]{:S(2)}) collective-permute-start(bf16[8,3584]{1,0:T(8,128)(2,1)S(1)} %get-tuple-element.30), channel_id=1, source_target_pairs={{0,8},{1,9},{2,10},{3,11},{4,12},{5,13},{6,14},{7,15},{8,0},{9,1},... | collective-permute-start | bytes 172040 | tf_op jit(solution)/shard_map/ppermute | solution.py:25
  8.0 2.6 %collective-permute-start.14 = (bf16[8,3584]{1,0:T(8,128)(2,1)S(1)}, bf16[8,3584]{1,0:T(8,128)(2,1)S(1)}, u32[]{:S(2)}, u32[]{:S(2)}) collective-permute-start(bf16[8,3584]{1,0:T(8,128)(2,1)S(1)} %get-tuple-element.29), channel_id=1, source_target_pairs={{0,16},{1,17},{2,18},{3,19},{4,20},{5,21},{6,22},{7,23},{8,24},{9,... | collective-permute-start | bytes 172040 | tf_op jit(solution)/shard_map/ppermute | solution.py:25
  10.6 0.9 %fusion.65 = (bf16[8,3584]{1,0:T(8,128)(2,1)S(1)}, bf16[8,3584]{1,0:T(8,128)(2,1)S(1)}, bf16[8,3584]{1,0:T(8,128)(2,1)S(1)}, bf16[8,3584]{1,0:T(8,128)(2,1)S(1)}) fusion(bf16[32,3584]{1,0:T(8,128)(2,1)} %get-tuple-element.11), kind=kLoop, calls=%fused_computation.127 | loop fusion | bytes 458752 | tf_op jit(solution)/shard_map/slice | solution.py:111
  11.5 1.0 %collective-permute-start = (bf16[8,3584]{1,0:T(8,128)(2,1)S(1)}, bf16[8,3584]{1,0:T(8,128)(2,1)S(1)}, u32[]{:S(2)}, u32[]{:S(2)}) collective-permute-start(bf16[8,3584]{1,0:T(8,128)(2,1)S(1)} %get-tuple-element.39), channel_id=1, source_target_pairs={{0,8},{1,9},{2,10},{3,11},{4,12},{5,13},{6,14},{7,15},{8,0},{9,1},... | collective-permute-start | bytes 172040 | tf_op jit(solution)/shard_map/ppermute | solution.py:25
  12.5 3.5 %collective-permute-start.1 = (bf16[8,3584]{1,0:T(8,128)(2,1)S(1)}, bf16[8,3584]{1,0:T(8,128)(2,1)S(1)}, u32[]{:S(2)}, u32[]{:S(2)}) collective-permute-start(bf16[8,3584]{1,0:T(8,128)(2,1)S(1)} %get-tuple-element.38), channel_id=1, source_target_pairs={{0,16},{1,17},{2,18},{3,19},{4,20},{5,21},{6,22},{7,23},{8,24},{9,... | collective-permute-start | bytes 172040 | tf_op jit(solution)/shard_map/ppermute | solution.py:25
  16.4 0.8 %reduce = f32[3584]{0:T(1024)S(1)} reduce(f32[1,3584]{1,0:T(1,128)} %scale_ref.1, f32[]{:T(128)} %constant.134), dimensions={0}, to_apply=%param.19.reduce_sub_computation | reduce | bytes 28676 | tf_op args[7]
  17.4 1.7 %collective-permute-start.16 = (bf16[32,3584]{1,0:T(8,128)(2,1)S(1)}, bf16[32,3584]{1,0:T(8,128)(2,1)S(1)}, u32[]{:S(2)}, u32[]{:S(2)}) collective-permute-start(bf16[32,3584]{1,0:T(8,128)(2,1)S(1)} %pad_maximum_fusion.8), channel_id=1, source_target_pairs={{0,2},{1,5},{2,0},{3,7},{4,6},{5,1},{6,4},{7,3},{8,10},{9,13},{10,... | collective-permute-start | bytes 688136 | tf_op jit(solution)/shard_map/ppermute | solution.py:25
  19.1 4.2 %collective-permute-done.2 = bf16[8,3584]{1,0:T(8,128)(2,1)S(1)} collective-permute-done((bf16[8,3584]{1,0:T(8,128)(2,1)S(1)}, bf16[8,3584]{1,0:T(8,128)(2,1)S(1)}, u32[]{:S(2)}, u32[]{:S(2)}) %collective-permute-start.2) | collective-permute-done | bytes 57376 | tf_op jit(solution)/shard_map/ppermute | solution.py:25
  24.0 1.6 %collective-permute-start.3 = (bf16[32,3584]{1,0:T(8,128)(2,1)S(1)}, bf16[32,3584]{1,0:T(8,128)(2,1)S(1)}, u32[]{:S(2)}, u32[]{:S(2)}) collective-permute-start(bf16[32,3584]{1,0:T(8,128)(2,1)S(1)} %pad_maximum_fusion.7), channel_id=1, source_target_pairs={{0,2},{1,5},{2,0},{3,7},{4,6},{5,1},{6,4},{7,3},{8,10},{9,13},{10,... | collective-permute-start | bytes 688136 | tf_op jit(solution)/shard_map/ppermute | solution.py:25
  25.6 1.6 %collective-permute-start.17 = (bf16[64,3584]{1,0:T(8,128)(2,1)S(1)}, bf16[64,3584]{1,0:T(8,128)(2,1)S(1)}, u32[]{:S(2)}, u32[]{:S(2)}) collective-permute-start(bf16[64,3584]{1,0:T(8,128)(2,1)S(1)} %get-tuple-element.24), channel_id=1, source_target_pairs={{0,4},{1,3},{2,6},{3,1},{4,0},{5,7},{6,2},{7,5},{8,12},{9,11},{10,... | collective-permute-start | bytes 1376264 | tf_op jit(solution)/shard_map/ppermute | solution.py:25
  27.2 4.6 %collective-permute-done.3 = bf16[32,3584]{1,0:T(8,128)(2,1)S(1)} collective-permute-done((bf16[32,3584]{1,0:T(8,128)(2,1)S(1)}, bf16[32,3584]{1,0:T(8,128)(2,1)S(1)}, u32[]{:S(2)}, u32[]{:S(2)}) %collective-permute-start.3) | collective-permute-done | bytes 229408 | tf_op jit(solution)/shard_map/ppermute | solution.py:25
  31.8 2.4 %collective-permute-start.4 = (bf16[64,3584]{1,0:T(8,128)(2,1)S(1)}, bf16[64,3584]{1,0:T(8,128)(2,1)S(1)}, u32[]{:S(2)}, u32[]{:S(2)}) collective-permute-start(bf16[64,3584]{1,0:T(8,128)(2,1)S(1)} %pad_maximum_fusion.6), channel_id=1, source_target_pairs={{0,4},{1,3},{2,6},{3,1},{4,0},{5,7},{6,2},{7,5},{8,12},{9,11},{10,... | collective-permute-start | bytes 1376264 | tf_op jit(solution)/shard_map/ppermute | solution.py:25
  34.5 0.7 %fusion.31 = (bf16[128,256]{1,0:T(8,128)(2,1)S(1)}, bf16[128,256]{1,0:T(8,128)(2,1)S(1)}) fusion(bf16[128,128]{1,0:T(8,128)(2,1)S(1)} %get-tuple-element.44, bf16[128,128]{1,0:T(8,128)(2,1)S(1)} %get-tuple-element.42, bf16[128,128]{1,0:T(8,128)(2,1)S(1)} %get-tuple-element.45, bf16[128,128]{1,0:T(8,128)(2,1)S(1)} %get-tuple-element.43, ...), kind=kOutput, calls=%fused_computation.54 | convolution fusion | flops 239239168 | bytes 3014656 | tf_op jit(solution)/shard_map/rd,hd->rh/dot_general | solution.py:210
  35.9 1.3 %fusion.9 = f32[128,3584]{1,0:T(8,128)S(1)} fusion(bf16[3584,128]{1,0:T(8,128)(2,1)S(1)} %collective-permute-done.6, bf16[3584,128]{1,0:T(8,128)(2,1)S(1)} %bitcast.23, bf16[3584,128]{1,0:T(8,128)(2,1)S(1)} %collective-permute-done.5, bf16[3584,128]{1,0:T(8,128)(2,1)S(1)} %bitcast.26, bf16[128,256]{1,0:T(8,128)(2,1)S(1)} %get-tuple-element.41, ...), kind=kOutput, calls=%fused_computation.19 | convolution fusion | flops 484704256 | bytes 5636096 | tf_op jit(solution)/shard_map/rh,dh->rd/dot_general | solution.py:215
  37.3 1.6 %collective-permute-start.19 = (bf16[64,3584]{1,0:T(8,128)(2,1)S(1)}, bf16[64,3584]{1,0:T(8,128)(2,1)S(1)}, u32[]{:S(2)}, u32[]{:S(2)}) collective-permute-start(bf16[64,3584]{1,0:T(8,128)(2,1)S(1)} %slice.166), channel_id=1, source_target_pairs={{0,4},{1,3},{2,6},{3,1},{4,0},{5,7},{6,2},{7,5},{8,12},{9,11},{10,... | collective-permute-start | bytes 1376264 | tf_op jit(solution)/shard_map/ppermute | solution.py:25
  38.9 1.7 %collective-permute-done.4 = bf16[64,3584]{1,0:T(8,128)(2,1)S(1)} collective-permute-done((bf16[64,3584]{1,0:T(8,128)(2,1)S(1)}, bf16[64,3584]{1,0:T(8,128)(2,1)S(1)}, u32[]{:S(2)}, u32[]{:S(2)}) %collective-permute-start.4) | collective-permute-done | bytes 458784 | tf_op jit(solution)/shard_map/ppermute | solution.py:25
  40.6 0.6 fusion.3
  41.7 2.1 %collective-permute-start.8 = (bf16[64,3584]{1,0:T(8,128)(2,1)S(1)}, bf16[64,3584]{1,0:T(8,128)(2,1)S(1)}, u32[]{:S(2)}, u32[]{:S(2)}) collective-permute-start(bf16[64,3584]{1,0:T(8,128)(2,1)S(1)} %slice.167), channel_id=1, source_target_pairs={{0,4},{1,3},{2,6},{3,1},{4,0},{5,7},{6,2},{7,5},{8,12},{9,11},{10,... | collective-permute-start | bytes 1376264 | tf_op jit(solution)/shard_map/ppermute | solution.py:25
  43.8 2.0 %collective-permute-done.19 = bf16[64,3584]{1,0:T(8,128)(2,1)S(1)} collective-permute-done((bf16[64,3584]{1,0:T(8,128)(2,1)S(1)}, bf16[64,3584]{1,0:T(8,128)(2,1)S(1)}, u32[]{:S(2)}, u32[]{:S(2)}) %collective-permute-start.19) | collective-permute-done | bytes 458784 | tf_op jit(solution)/shard_map/ppermute | solution.py:25
  46.0 1.6 %collective-permute-start.20 = (bf16[32,3584]{1,0:T(8,128)(2,1)S(1)}, bf16[32,3584]{1,0:T(8,128)(2,1)S(1)}, u32[]{:S(2)}, u32[]{:S(2)}) collective-permute-start(bf16[32,3584]{1,0:T(8,128)(2,1)S(1)} %slice.168), channel_id=1, source_target_pairs={{0,2},{1,5},{2,0},{3,7},{4,6},{5,1},{6,4},{7,3},{8,10},{9,13},{10,... | collective-permute-start | bytes 688136 | tf_op jit(solution)/shard_map/ppermute | solution.py:25
  47.6 5.7 %collective-permute-done.8 = bf16[64,3584]{1,0:T(8,128)(2,1)S(1)} collective-permute-done((bf16[64,3584]{1,0:T(8,128)(2,1)S(1)}, bf16[64,3584]{1,0:T(8,128)(2,1)S(1)}, u32[]{:S(2)}, u32[]{:S(2)}) %collective-permute-start.8) | collective-permute-done | bytes 458784 | tf_op jit(solution)/shard_map/ppermute | solution.py:25
  53.5 1.6 %collective-permute-start.9 = (bf16[32,3584]{1,0:T(8,128)(2,1)S(1)}, bf16[32,3584]{1,0:T(8,128)(2,1)S(1)}, u32[]{:S(2)}, u32[]{:S(2)}) collective-permute-start(bf16[32,3584]{1,0:T(8,128)(2,1)S(1)} %slice.169), channel_id=1, source_target_pairs={{0,2},{1,5},{2,0},{3,7},{4,6},{5,1},{6,4},{7,3},{8,10},{9,13},{10,... | collective-permute-start | bytes 688136 | tf_op jit(solution)/shard_map/ppermute | solution.py:25
  55.2 2.8 %collective-permute-start.22 = (bf16[8,3584]{1,0:T(8,128)(2,1)S(1)}, bf16[8,3584]{1,0:T(8,128)(2,1)S(1)}, u32[]{:S(2)}, u32[]{:S(2)}) collective-permute-start(bf16[8,3584]{1,0:T(8,128)(2,1)S(1)} %get-tuple-element.22), channel_id=1, source_target_pairs={{0,16},{1,17},{2,18},{3,19},{4,20},{5,21},{6,22},{7,23},{8,24},{9,... | collective-permute-start | bytes 172040 | tf_op jit(solution)/shard_map/ppermute | solution.py:25
  58.0 1.6 %collective-permute-start.23 = (bf16[8,3584]{1,0:T(8,128)(2,1)S(1)}, bf16[8,3584]{1,0:T(8,128)(2,1)S(1)}, u32[]{:S(2)}, u32[]{:S(2)}) collective-permute-start(bf16[8,3584]{1,0:T(8,128)(2,1)S(1)} %get-tuple-element.21), channel_id=1, source_target_pairs={{0,24},{1,25},{2,26},{3,27},{4,28},{5,29},{6,30},{7,31},{8,16},{9,... | collective-permute-start | bytes 172040 | tf_op jit(solution)/shard_map/ppermute | solution.py:25
  59.7 2.9 %collective-permute-start.11 = (bf16[8,3584]{1,0:T(8,128)(2,1)S(1)}, bf16[8,3584]{1,0:T(8,128)(2,1)S(1)}, u32[]{:S(2)}, u32[]{:S(2)}) collective-permute-start(bf16[8,3584]{1,0:T(8,128)(2,1)S(1)} %get-tuple-element.34), channel_id=1, source_target_pairs={{0,16},{1,17},{2,18},{3,19},{4,20},{5,21},{6,22},{7,23},{8,24},{9,... | collective-permute-start | bytes 172040 | tf_op jit(solution)/shard_map/ppermute | solution.py:25
  62.6 1.5 %collective-permute-start.12 = (bf16[8,3584]{1,0:T(8,128)(2,1)S(1)}, bf16[8,3584]{1,0:T(8,128)(2,1)S(1)}, u32[]{:S(2)}, u32[]{:S(2)}) collective-permute-start(bf16[8,3584]{1,0:T(8,128)(2,1)S(1)} %get-tuple-element.33), channel_id=1, source_target_pairs={{0,24},{1,25},{2,26},{3,27},{4,28},{5,29},{6,30},{7,31},{8,16},{9,... | collective-permute-start | bytes 172040 | tf_op jit(solution)/shard_map/ppermute | solution.py:25
  64.5 0.7 %fusion.44 = bf16[8,3584]{1,0:T(8,128)(2,1)} fusion(bf16[8,3584]{1,0:T(8,128)(2,1)S(1)} %copy-done.4, f32[8,3584]{1,0:T(8,128)S(1)} %get-tuple-element.54, bf16[8,3584]{1,0:T(8,128)(2,1)S(1)} %copy-done.2, f32[8]{0:T(128)S(1)} %broadcast_multiply_fusion, f32[8]{0:T(128)S(1)} %get-tuple-element.53, f32[8]{0:T(128)S(1)} %get-tuple-element.52), kind=kLoop, calls=%fused_computation.70 | loop fusion | flops 229376 | bytes 286816 | tf_op jit(solution)/shard_map/convert_element_type | solution.py:224
  65.6 3.0 %collective-permute-done.12 = bf16[8,3584]{1,0:T(8,128)(2,1)S(1)} collective-permute-done((bf16[8,3584]{1,0:T(8,128)(2,1)S(1)}, bf16[8,3584]{1,0:T(8,128)(2,1)S(1)}, u32[]{:S(2)}, u32[]{:S(2)}) %collective-permute-start.12) | collective-permute-done | bytes 57376 | tf_op jit(solution)/shard_map/ppermute | solution.py:25
  68.6 0.9 %fusion = bf16[8,3584]{1,0:T(8,128)(2,1)} fusion(f32[32,8]{1,0:T(8,128)S(1)} %copy-done.7, bf16[8,3584]{1,0:T(8,128)(2,1)S(1)} %collective-permute-done.12, bf16[8,3584]{1,0:T(8,128)(2,1)S(1)} %collective-permute-done.11, bf16[8,3584]{1,0:T(8,128)(2,1)S(1)} %collective-permute-done.10, bf16[8,3584]{1,0:T(8,128)(2,1)S(1)} %get-tuple-element.32, ...), kind=kOutput, calls=%fused_computation.2 | convolution fusion | flops 12013568 | bytes 345088 | tf_op jit(solution)/shard_map/dot_general | solution.py:207
  (71 shorter events, 4.3 us)
Async XLA Ops:
  0.6 15.4 %copy-start = (bf16[1,1,32,8,256]{4,3,2,1,0:T(8,128)(2,1)S(1)}, bf16[1,1,32,8,256]{4,3,2,1,0:T(8,128)(2,1)}, u32[]{:S(2)}) copy-start(bf16[1,1,32,8,256]{4,3,2,1,0:T(8,128)(2,1)} %param.23) | copy-start | bytes 393220
  0.6 22.6 %copy-start.1 = (bf16[1,1,128,3584]{3,2,1,0:T(8,128)(2,1)S(1)}, bf16[1,1,128,3584]{3,2,1,0:T(8,128)(2,1)}, u32[]{:S(2)}) copy-start(bf16[1,1,128,3584]{3,2,1,0:T(8,128)(2,1)} %param.22) | copy-start | bytes 2752516
  4.9 12.3 %collective-permute-start.13 = (bf16[8,3584]{1,0:T(8,128)(2,1)S(1)}, bf16[8,3584]{1,0:T(8,128)(2,1)S(1)}, u32[]{:S(2)}, u32[]{:S(2)}) collective-permute-start(bf16[8,3584]{1,0:T(8,128)(2,1)S(1)} %get-tuple-element.30), channel_id=1, source_target_pairs={{0,8},{1,9},{2,10},{3,11},{4,12},{5,13},{6,14},{7,15},{8,0},{9,1},... | collective-permute-start | bytes 172040 | tf_op jit(solution)/shard_map/ppermute | solution.py:25
  8.0 9.3 %collective-permute-start.14 = (bf16[8,3584]{1,0:T(8,128)(2,1)S(1)}, bf16[8,3584]{1,0:T(8,128)(2,1)S(1)}, u32[]{:S(2)}, u32[]{:S(2)}) collective-permute-start(bf16[8,3584]{1,0:T(8,128)(2,1)S(1)} %get-tuple-element.29), channel_id=1, source_target_pairs={{0,16},{1,17},{2,18},{3,19},{4,20},{5,21},{6,22},{7,23},{8,24},{9,... | collective-permute-start | bytes 172040 | tf_op jit(solution)/shard_map/ppermute | solution.py:25
  10.6 6.8 %collective-permute-start.15 = (bf16[8,3584]{1,0:T(8,128)(2,1)S(1)}, bf16[8,3584]{1,0:T(8,128)(2,1)S(1)}, u32[]{:S(2)}, u32[]{:S(2)}) collective-permute-start(bf16[8,3584]{1,0:T(8,128)(2,1)S(1)} %get-tuple-element.28), channel_id=1, source_target_pairs={{0,24},{1,25},{2,26},{3,27},{4,28},{5,29},{6,30},{7,31},{8,16},{9,... | collective-permute-start | bytes 172040 | tf_op jit(solution)/shard_map/ppermute | solution.py:25
  11.5 7.6 %collective-permute-start = (bf16[8,3584]{1,0:T(8,128)(2,1)S(1)}, bf16[8,3584]{1,0:T(8,128)(2,1)S(1)}, u32[]{:S(2)}, u32[]{:S(2)}) collective-permute-start(bf16[8,3584]{1,0:T(8,128)(2,1)S(1)} %get-tuple-element.39), channel_id=1, source_target_pairs={{0,8},{1,9},{2,10},{3,11},{4,12},{5,13},{6,14},{7,15},{8,0},{9,1},... | collective-permute-start | bytes 172040 | tf_op jit(solution)/shard_map/ppermute | solution.py:25
  12.5 6.6 %collective-permute-start.1 = (bf16[8,3584]{1,0:T(8,128)(2,1)S(1)}, bf16[8,3584]{1,0:T(8,128)(2,1)S(1)}, u32[]{:S(2)}, u32[]{:S(2)}) collective-permute-start(bf16[8,3584]{1,0:T(8,128)(2,1)S(1)} %get-tuple-element.38), channel_id=1, source_target_pairs={{0,16},{1,17},{2,18},{3,19},{4,20},{5,21},{6,22},{7,23},{8,24},{9,... | collective-permute-start | bytes 172040 | tf_op jit(solution)/shard_map/ppermute | solution.py:25
  17.2 6.0 %collective-permute-start.2 = (bf16[8,3584]{1,0:T(8,128)(2,1)S(1)}, bf16[8,3584]{1,0:T(8,128)(2,1)S(1)}, u32[]{:S(2)}, u32[]{:S(2)}) collective-permute-start(bf16[8,3584]{1,0:T(8,128)(2,1)S(1)} %get-tuple-element.37), channel_id=1, source_target_pairs={{0,24},{1,25},{2,26},{3,27},{4,28},{5,29},{6,30},{7,31},{8,16},{9,... | collective-permute-start | bytes 172040 | tf_op jit(solution)/shard_map/ppermute | solution.py:25
  17.3 6.7 %collective-permute-start.18 = (bf16[128,256]{1,0:T(8,128)(2,1)S(1)}, bf16[128,256]{1,0:T(8,128)(2,1)S(1)}, u32[]{:S(2)}, u32[]{:S(2)}) collective-permute-start(bf16[128,256]{1,0:T(8,128)(2,1)S(1)} %convolution_convert_fusion), channel_id=1, source_target_pairs={{0,1},{1,0},{2,3},{3,2},{4,5},{5,4},{6,7},{7,6},{8,9},{9,8},{10,11... | collective-permute-start | bytes 196616 | tf_op jit(solution)/shard_map/ppermute | solution.py:25
  17.4 8.1 %collective-permute-start.16 = (bf16[32,3584]{1,0:T(8,128)(2,1)S(1)}, bf16[32,3584]{1,0:T(8,128)(2,1)S(1)}, u32[]{:S(2)}, u32[]{:S(2)}) collective-permute-start(bf16[32,3584]{1,0:T(8,128)(2,1)S(1)} %pad_maximum_fusion.8), channel_id=1, source_target_pairs={{0,2},{1,5},{2,0},{3,7},{4,6},{5,1},{6,4},{7,3},{8,10},{9,13},{10,... | collective-permute-start | bytes 688136 | tf_op jit(solution)/shard_map/ppermute | solution.py:25
  23.3 11.2 %collective-permute-start.7 = (bf16[128,3584]{1,0:T(8,128)(2,1)S(1)}, bf16[128,3584]{1,0:T(8,128)(2,1)S(1)}, u32[]{:S(2)}, u32[]{:S(2)}) collective-permute-start(bf16[128,3584]{1,0:T(8,128)(2,1)S(1)} %bitcast.17), channel_id=1, source_target_pairs={{0,1},{1,0},{2,3},{3,2},{4,5},{5,4},{6,7},{7,6},{8,9},{9,8},{10,11... | collective-permute-start | bytes 2752520 | tf_op jit(solution)/shard_map/ppermute | solution.py:25
  23.3 11.9 %collective-permute-start.5 = (bf16[3584,128]{1,0:T(8,128)(2,1)}, bf16[3584,128]{1,0:T(8,128)(2,1)S(1)}, u32[]{:S(2)}, u32[]{:S(2)}) collective-permute-start(bf16[3584,128]{1,0:T(8,128)(2,1)} %bitcast.25), channel_id=1, source_target_pairs={{0,1},{1,0},{2,3},{3,2},{4,5},{5,4},{6,7},{7,6},{8,9},{9,8},{10,11... | collective-permute-start | bytes 2752520 | tf_op jit(solution)/shard_map/ppermute | solution.py:25
  23.8 11.4 %collective-permute-start.6 = (bf16[3584,128]{1,0:T(8,128)(2,1)}, bf16[3584,128]{1,0:T(8,128)(2,1)S(1)}, u32[]{:S(2)}, u32[]{:S(2)}) collective-permute-start(bf16[3584,128]{1,0:T(8,128)(2,1)} %bitcast.22), channel_id=1, source_target_pairs={{0,1},{1,0},{2,3},{3,2},{4,5},{5,4},{6,7},{7,6},{8,9},{9,8},{10,11... | collective-permute-start | bytes 2752520 | tf_op jit(solution)/shard_map/ppermute | solution.py:25
  24.0 7.7 %collective-permute-start.3 = (bf16[32,3584]{1,0:T(8,128)(2,1)S(1)}, bf16[32,3584]{1,0:T(8,128)(2,1)S(1)}, u32[]{:S(2)}, u32[]{:S(2)}) collective-permute-start(bf16[32,3584]{1,0:T(8,128)(2,1)S(1)} %pad_maximum_fusion.7), channel_id=1, source_target_pairs={{0,2},{1,5},{2,0},{3,7},{4,6},{5,1},{6,4},{7,3},{8,10},{9,13},{10,... | collective-permute-start | bytes 688136 | tf_op jit(solution)/shard_map/ppermute | solution.py:25
  25.6 8.9 %collective-permute-start.17 = (bf16[64,3584]{1,0:T(8,128)(2,1)S(1)}, bf16[64,3584]{1,0:T(8,128)(2,1)S(1)}, u32[]{:S(2)}, u32[]{:S(2)}) collective-permute-start(bf16[64,3584]{1,0:T(8,128)(2,1)S(1)} %get-tuple-element.24), channel_id=1, source_target_pairs={{0,4},{1,3},{2,6},{3,1},{4,0},{5,7},{6,2},{7,5},{8,12},{9,11},{10,... | collective-permute-start | bytes 1376264 | tf_op jit(solution)/shard_map/ppermute | solution.py:25
  31.8 8.8 %collective-permute-start.4 = (bf16[64,3584]{1,0:T(8,128)(2,1)S(1)}, bf16[64,3584]{1,0:T(8,128)(2,1)S(1)}, u32[]{:S(2)}, u32[]{:S(2)}) collective-permute-start(bf16[64,3584]{1,0:T(8,128)(2,1)S(1)} %pad_maximum_fusion.6), channel_id=1, source_target_pairs={{0,4},{1,3},{2,6},{3,1},{4,0},{5,7},{6,2},{7,5},{8,12},{9,11},{10,... | collective-permute-start | bytes 1376264 | tf_op jit(solution)/shard_map/ppermute | solution.py:25
  34.5 1.4 %copy-start.6 = (bf16[1,1,3584,128]{3,2,1,0:T(8,128)(2,1)S(1)}, bf16[1,1,3584,128]{3,2,1,0:T(8,128)(2,1)}, u32[]{:S(2)}) copy-start(bf16[1,1,3584,128]{3,2,1,0:T(8,128)(2,1)} %param.20) | copy-start | bytes 2752516
  37.3 8.5 %collective-permute-start.19 = (bf16[64,3584]{1,0:T(8,128)(2,1)S(1)}, bf16[64,3584]{1,0:T(8,128)(2,1)S(1)}, u32[]{:S(2)}, u32[]{:S(2)}) collective-permute-start(bf16[64,3584]{1,0:T(8,128)(2,1)S(1)} %slice.166), channel_id=1, source_target_pairs={{0,4},{1,3},{2,6},{3,1},{4,0},{5,7},{6,2},{7,5},{8,12},{9,11},{10,... | collective-permute-start | bytes 1376264 | tf_op jit(solution)/shard_map/ppermute | solution.py:25
  41.7 11.5 %collective-permute-start.8 = (bf16[64,3584]{1,0:T(8,128)(2,1)S(1)}, bf16[64,3584]{1,0:T(8,128)(2,1)S(1)}, u32[]{:S(2)}, u32[]{:S(2)}) collective-permute-start(bf16[64,3584]{1,0:T(8,128)(2,1)S(1)} %slice.167), channel_id=1, source_target_pairs={{0,4},{1,3},{2,6},{3,1},{4,0},{5,7},{6,2},{7,5},{8,12},{9,11},{10,... | collective-permute-start | bytes 1376264 | tf_op jit(solution)/shard_map/ppermute | solution.py:25
  46.0 9.0 %collective-permute-start.20 = (bf16[32,3584]{1,0:T(8,128)(2,1)S(1)}, bf16[32,3584]{1,0:T(8,128)(2,1)S(1)}, u32[]{:S(2)}, u32[]{:S(2)}) collective-permute-start(bf16[32,3584]{1,0:T(8,128)(2,1)S(1)} %slice.168), channel_id=1, source_target_pairs={{0,2},{1,5},{2,0},{3,7},{4,6},{5,1},{6,4},{7,3},{8,10},{9,13},{10,... | collective-permute-start | bytes 688136 | tf_op jit(solution)/shard_map/ppermute | solution.py:25
  53.4 10.7 %copy-start.4 = (bf16[8,3584]{1,0:T(8,128)(2,1)S(1)}, bf16[8,3584]{1,0:T(8,128)(2,1)}, u32[]{:S(2)}) copy-start(bf16[8,3584]{1,0:T(8,128)(2,1)} %param.14) | copy-start | bytes 172036
  53.4 10.7 %copy-start.8 = (f32[32,8]{1,0:T(8,128)S(1)}, f32[32,8]{1,0:T(8,128)}, u32[]{:S(2)}) copy-start(f32[32,8]{1,0:T(8,128)} %get-tuple-element.16) | copy-start | bytes 3076
  53.4 11.1 %copy-start.2 = (bf16[8,3584]{1,0:T(8,128)(2,1)S(1)}, bf16[8,3584]{1,0:T(8,128)(2,1)}, u32[]{:S(2)}) copy-start(bf16[8,3584]{1,0:T(8,128)(2,1)} %cotangent_ref.1) | copy-start | bytes 172036
  53.4 15.2 %copy-start.3 = (bf16[8,3584]{1,0:T(8,128)(2,1)S(1)}, bf16[8,3584]{1,0:T(8,128)(2,1)}, u32[]{:S(2)}) copy-start(bf16[8,3584]{1,0:T(8,128)(2,1)} %inbound_ref.1) | copy-start | bytes 172036
  53.4 15.1 %copy-start.7 = (f32[32,8]{1,0:T(8,128)S(1)}, f32[32,8]{1,0:T(8,128)}, u32[]{:S(2)}) copy-start(f32[32,8]{1,0:T(8,128)} %get-tuple-element.10) | copy-start | bytes 3076
  53.5 6.1 %collective-permute-start.9 = (bf16[32,3584]{1,0:T(8,128)(2,1)S(1)}, bf16[32,3584]{1,0:T(8,128)(2,1)S(1)}, u32[]{:S(2)}, u32[]{:S(2)}) collective-permute-start(bf16[32,3584]{1,0:T(8,128)(2,1)S(1)} %slice.169), channel_id=1, source_target_pairs={{0,2},{1,5},{2,0},{3,7},{4,6},{5,1},{6,4},{7,3},{8,10},{9,13},{10,... | collective-permute-start | bytes 688136 | tf_op jit(solution)/shard_map/ppermute | solution.py:25
  55.1 7.5 %collective-permute-start.21 = (bf16[8,3584]{1,0:T(8,128)(2,1)S(1)}, bf16[8,3584]{1,0:T(8,128)(2,1)S(1)}, u32[]{:S(2)}, u32[]{:S(2)}) collective-permute-start(bf16[8,3584]{1,0:T(8,128)(2,1)S(1)} %get-tuple-element.23), channel_id=1, source_target_pairs={{0,8},{1,9},{2,10},{3,11},{4,12},{5,13},{6,14},{7,15},{8,0},{9,1},... | collective-permute-start | bytes 172040 | tf_op jit(solution)/shard_map/ppermute | solution.py:25
  55.2 8.9 %collective-permute-start.22 = (bf16[8,3584]{1,0:T(8,128)(2,1)S(1)}, bf16[8,3584]{1,0:T(8,128)(2,1)S(1)}, u32[]{:S(2)}, u32[]{:S(2)}) collective-permute-start(bf16[8,3584]{1,0:T(8,128)(2,1)S(1)} %get-tuple-element.22), channel_id=1, source_target_pairs={{0,16},{1,17},{2,18},{3,19},{4,20},{5,21},{6,22},{7,23},{8,24},{9,... | collective-permute-start | bytes 172040 | tf_op jit(solution)/shard_map/ppermute | solution.py:25
  58.0 6.1 %collective-permute-start.23 = (bf16[8,3584]{1,0:T(8,128)(2,1)S(1)}, bf16[8,3584]{1,0:T(8,128)(2,1)S(1)}, u32[]{:S(2)}, u32[]{:S(2)}) collective-permute-start(bf16[8,3584]{1,0:T(8,128)(2,1)S(1)} %get-tuple-element.21), channel_id=1, source_target_pairs={{0,24},{1,25},{2,26},{3,27},{4,28},{5,29},{6,30},{7,31},{8,16},{9,... | collective-permute-start | bytes 172040 | tf_op jit(solution)/shard_map/ppermute | solution.py:25
  59.6 5.6 %collective-permute-start.10 = (bf16[8,3584]{1,0:T(8,128)(2,1)S(1)}, bf16[8,3584]{1,0:T(8,128)(2,1)S(1)}, u32[]{:S(2)}, u32[]{:S(2)}) collective-permute-start(bf16[8,3584]{1,0:T(8,128)(2,1)S(1)} %get-tuple-element.35), channel_id=1, source_target_pairs={{0,8},{1,9},{2,10},{3,11},{4,12},{5,13},{6,14},{7,15},{8,0},{9,1},... | collective-permute-start | bytes 172040 | tf_op jit(solution)/shard_map/ppermute | solution.py:25
  59.7 5.9 %collective-permute-start.11 = (bf16[8,3584]{1,0:T(8,128)(2,1)S(1)}, bf16[8,3584]{1,0:T(8,128)(2,1)S(1)}, u32[]{:S(2)}, u32[]{:S(2)}) collective-permute-start(bf16[8,3584]{1,0:T(8,128)(2,1)S(1)} %get-tuple-element.34), channel_id=1, source_target_pairs={{0,16},{1,17},{2,18},{3,19},{4,20},{5,21},{6,22},{7,23},{8,24},{9,... | collective-permute-start | bytes 172040 | tf_op jit(solution)/shard_map/ppermute | solution.py:25
  62.6 6.0 %collective-permute-start.12 = (bf16[8,3584]{1,0:T(8,128)(2,1)S(1)}, bf16[8,3584]{1,0:T(8,128)(2,1)S(1)}, u32[]{:S(2)}, u32[]{:S(2)}) collective-permute-start(bf16[8,3584]{1,0:T(8,128)(2,1)S(1)} %get-tuple-element.33), channel_id=1, source_target_pairs={{0,24},{1,25},{2,26},{3,27},{4,28},{5,29},{6,30},{7,31},{8,16},{9,... | collective-permute-start | bytes 172040 | tf_op jit(solution)/shard_map/ppermute | solution.py:25
  (1 other events, 1.2 us)

commit v3 on v2

v3 whole, which is shorter than its diff:
```python
import functools

import jax
import jax.numpy as jnp
from jax import lax
from jax.experimental import pallas as pl
from jax.experimental.pallas import tpu as pltpu
from jax.sharding import PartitionSpec as P

EPSILON = 1e-06
HIGHEST = lax.Precision.HIGHEST
F32 = jnp.float32
BF16 = jnp.bfloat16


def from_behind(value, axis, by):
    size = lax.axis_size(axis)
    if size == 1:
        return value
    return lax.ppermute(value, axis, [(i, (i + by) % size) for i in range(size)])


def swap(value, mask_of):
    size = lax.axis_size("expert")
    return lax.ppermute(value, "expert", [(i, i ^ mask_of(i)) for i in range(size)])


def with_core(value):
    return swap(value, lambda i: 1)


def with_first(value):
    return swap(value, lambda i: 4 if i & 1 else 2)


def with_second(value):
    return swap(value, lambda i: 2 if i & 1 else 4)


def join(parts):
    return jnp.concatenate(parts, axis=0)


def slot_table(routes, gates, experts, capacity):
    tokens = routes.shape[1]
    slots = experts * capacity
    slot = lax.broadcasted_iota(jnp.int32, (slots, tokens), 0)
    token = lax.broadcasted_iota(jnp.int32, (slots, tokens), 1)
    expert, place = slot // capacity, slot % capacity
    first = routes[0:1, :] == expert
    second = routes[1:2, :] == expert
    named = jnp.where(first | second, 1.0, 0.0)
    rank = jnp.zeros((slots, tokens), F32)
    for t in range(tokens - 1):
        rank = rank + jnp.where(token > t, named[:, t : t + 1], 0.0)
    here = (named > 0.0) & (rank == place.astype(F32))
    occupied = jnp.where(here, 1.0, 0.0)
    weighted = jnp.where(here, jnp.where(first, gates[0:1, :], gates[1:2, :]), 0.0)
    return occupied, weighted


def forward_rows_kernel(groups, capacity, inbound_ref, scale_ref, routes_ref, gates_ref, *out_refs):
    group = lax.axis_index("expert") // 8
    occupied, weighted = slot_table(routes_ref[...] ^ group, gates_ref[...], groups, capacity)
    inbound = inbound_ref[...].astype(F32)
    factor = lax.rsqrt(jnp.mean(inbound * inbound, axis=-1, keepdims=True) + EPSILON)
    normed = (inbound * factor * scale_ref[...]).astype(BF16)
    rows = jnp.dot(occupied.astype(BF16), normed, preferred_element_type=F32).astype(BF16)
    for k in range(groups):
        out_refs[k][...] = rows[k * capacity : (k + 1) * capacity]
    out_refs[groups][...] = weighted
    out_refs[groups + 1][...] = jnp.broadcast_to(scale_ref[...], inbound.shape)


def backward_rows_kernel(groups, capacity, cotangent_ref, routes_ref, gates_ref, held_ref, *refs):
    out_refs = refs[:-1]
    refs[-1][...] = held_ref[...]
    group = lax.axis_index("expert") // 8
    occupied, weighted = slot_table(routes_ref[...] ^ group, gates_ref[...], groups, capacity)
    gate = jnp.sum(weighted, axis=1, keepdims=True)
    rows = jnp.dot(occupied.astype(BF16), cotangent_ref[...], preferred_element_type=F32)
    rows = (rows * gate).astype(BF16)
    for k in range(groups):
        out_refs[k][...] = rows[k * capacity : (k + 1) * capacity]
    out_refs[groups][...] = occupied


def in_vmem(value):
    return pltpu.with_memory_space_constraint(value, pltpu.VMEM)


def slot_rows(kernel, name, groups, capacity, value, *rest, held=(), more=()):
    tokens, columns = value.shape
    chunk = pltpu.VMEM((capacity, columns), BF16)
    table = jax.ShapeDtypeStruct((groups * capacity, tokens), F32)
    out = pl.pallas_call(
        functools.partial(kernel, groups, capacity),
        out_shape=(chunk,) * groups + (table,) + (chunk,) * len(held) + more,
        name=name,
        compiler_params=pltpu.CompilerParams(vmem_limit_bytes=4 * 1024 * 1024),
    )(*[pltpu.with_memory_space_constraint(v, pltpu.HBM) for v in (value, *rest)], *[in_vmem(v) for v in held])
    return out[:groups], *out[groups:]


def along_groups(chunks):
    return [chunks[0]] + [swap(chunks[k], lambda i, k=k: 8 * k) for k in range(1, len(chunks))]


def halve(value, exchange):
    rows = value.shape[0] // 2
    return value[:rows] + exchange(value[rows:].astype(BF16)).astype(F32)


def give_back(partial, groups, first, second):
    summed = halve(halve(partial, second), first).astype(BF16)
    capacity = summed.shape[0] // groups
    return join(along_groups([summed[k * capacity : (k + 1) * capacity] for k in range(groups)]))


def stash_rows(stash_flat, group, place, core, groups, capacity):
    first = jnp.where(core == 0, 4, 2)
    second = 6 - first
    position = jnp.arange(4 * groups * capacity, dtype=jnp.int32)
    quarter = position // (groups * capacity)
    chunk = position // capacity % groups
    slot = position % capacity
    away = jnp.where(quarter % 2 == 1, first, 0) ^ jnp.where(quarter >= 2, second, 0)
    source = (group ^ chunk) * 8 + ((place & 6) ^ away) + core
    wanted = source * capacity + slot
    table = (
        wanted[:, None] == jnp.arange(stash_flat.shape[0], dtype=jnp.int32)[None, :]
    ).astype(BF16)
    return jnp.dot(table, stash_flat, preferred_element_type=F32)


def body(
    act_send,
    grad_send,
    x_back,
    routes_fwd,
    gates_fwd,
    routes_back,
    gates_back,
    norm_gain,
    w_gate,
    w_up,
    w_down,
    stash,
):
    sources = lax.axis_size("expert")
    groups = sources // 8
    capacity = stash.shape[3]
    hidden_dev = w_gate.shape[3]
    hidden_two = 2 * hidden_dev
    index = lax.axis_index("expert")
    group, place, core = index // 8, index % 8, index % 2

    inbound = from_behind(act_send, "section", 1)
    cotangent = from_behind(grad_send, "section", -1)
    with jax.named_scope("swaps"):
        gate_other = with_core(w_gate[0, 0])
        up_other = with_core(w_up[0, 0])
        down_other = with_core(w_down[0, 0])
        stash_other = with_core(stash[0, 0])
    chunks, weighted_fwd, scale_rows = slot_rows(
        forward_rows_kernel,
        "forward_rows",
        groups,
        capacity,
        inbound,
        norm_gain,
        routes_fwd.T,
        gates_fwd.T,
        more=(pltpu.VMEM(inbound.shape, F32),),
    )
    with jax.named_scope("forward"):
        arrived = along_groups(chunks)
    routes_back, gate_other, up_other = lax.optimization_barrier(
        (routes_back, gate_other, up_other)
    )
    chunks, occupied_back, own_chunk = slot_rows(
        backward_rows_kernel,
        "backward_rows",
        groups,
        capacity,
        cotangent,
        routes_back.T,
        gates_back.T,
        held=(arrived[0],),
    )
    with jax.named_scope("forward"):
        own = join([own_chunk] + arrived[1:])
    with jax.named_scope("backward"):
        grad_own = join(along_groups(chunks))
    with jax.named_scope("forward"):
        half = join([own, with_first(own)])
        half, stash_other = lax.optimization_barrier(
            (half, stash_other)
        )
        flat_rows = join([half, with_second(half)])
    with jax.named_scope("backward"):
        half = join([grad_own, with_first(grad_own)])
        last = with_second(half)
        rows = grad_own.shape[0]
        grad_flat = join([half[:rows], last[:rows], half[rows:], last[rows:]])

    w_in = jnp.concatenate([w_gate[0, 0], gate_other, w_up[0, 0], up_other], axis=1)
    w_out = join([w_down[0, 0], down_other])
    stash_flat = jnp.concatenate([stash[0, 0], stash_other], axis=2).reshape(sources * capacity, -1)
    saved = stash_rows(stash_flat, group, place, core, groups, capacity)
    saved_gate = jnp.concatenate(
        [saved[:, :hidden_dev], saved[:, hidden_two : hidden_two + hidden_dev]], axis=1
    )
    saved_up = jnp.concatenate(
        [saved[:, hidden_dev:hidden_two], saved[:, hidden_two + hidden_dev :]], axis=1
    )

    pre = jnp.dot(flat_rows, w_in, preferred_element_type=F32)
    hidden = (jax.nn.silu(pre[:, :hidden_two]) * pre[:, hidden_two:]).astype(BF16)
    partial_fwd = jnp.dot(hidden, w_out, preferred_element_type=F32)
    with jax.named_scope("forward"):
        summed = give_back(partial_fwd, groups, with_first, with_second)
    mixture = jnp.dot(weighted_fwd.T, summed.astype(F32), precision=HIGHEST)
    outbound = (inbound.astype(F32) + mixture).astype(BF16)

    grad_hidden = jnp.einsum("rd,hd->rh", grad_flat, w_out, preferred_element_type=F32)
    sigmoid = jax.nn.sigmoid(saved_gate)
    d_gate = (grad_hidden * saved_up * sigmoid * (1.0 + saved_gate * (1.0 - sigmoid))).astype(BF16)
    d_up = (grad_hidden * saved_gate * sigmoid).astype(BF16)
    d_pre = jnp.concatenate([d_gate, d_up], axis=1)
    grad_total = jnp.einsum("rh,dh->rd", d_pre, w_in, preferred_element_type=F32)
    with jax.named_scope("backward"):
        grad_summed = give_back(grad_total, groups, with_second, with_first)
    grad_normed = jnp.dot(occupied_back.T, grad_summed.astype(F32), precision=HIGHEST)
    saved32 = x_back.astype(F32)
    factor = lax.rsqrt(jnp.mean(saved32 * saved32, axis=-1, keepdims=True) + EPSILON)
    scaled_grad = grad_normed * scale_rows
    through = factor * scaled_grad - saved32 * factor**3 * jnp.mean(
        scaled_grad * saved32, axis=-1, keepdims=True
    )
    input_grad = (cotangent.astype(F32) + through).astype(BF16)
    return (outbound, input_grad)


def solution(mesh):
    placed = (
        P(("section", "expert"), None),
        P(("section", "expert"), None),
        P(("section", "expert"), None),
        P(("section", "expert"), None),
        P(("section", "expert"), None),
        P(("section", "expert"), None),
        P(("section", "expert"), None),
        P("section", None),
        P("section", "expert", None, None),
        P("section", "expert", None, None),
        P("section", "expert", None, None),
        P("section", "expert", None, None, None),
    )
    return jax.shard_map(
        body,
        mesh=mesh,
        in_specs=placed,
        out_specs=(P(("section", "expert"), None), P(("section", "expert"), None)),
        check_vma=False,
    )
```

time: 69.9 us -> 66.2 us (0.947)
  local copies, waits for them, and re-layouts: 2.87 us -> 0.39 us
  other arithmetic: 3.23 us -> 1.07 us
  waiting for transfers between devices: 21.8 us -> 22.7 us
    unnamed x22 -> x24, local copies, waits for them, and re-layouts: 1.7 us -> 0.13 us
    xor x1 -> x0, other arithmetic: 1.36 us -> none  [body(): routes_back.T ^ group]
    slice x9 -> x7, local copies, waits for them, and re-layouts: 1.12 us -> 0.21 us  [the longest x4 0.15 us: halve(): return value[:rows] + exchange(value[rows:].astype(BF16)).astype(F32)]
    ppermute x24, waiting for transfers between devices: 21.8 us -> 22.7 us  [swap(): lax.ppermute(value, 'expert', [(i, i ^ mask_of(i)) for i in range(size)])]
    unnamed x1 -> x0, other arithmetic: 0.75 us -> none
    pallas_call x1 -> x2, Pallas kernels: 1.94 us -> 2.27 us  [slot_rows(): pl.pallas_call(functools.partial(kernel, groups, capacity), out_shape=(ch...]
  transfers between devices with their start and end apart: 24 -> 24, of which waited for: 8 -> 14; matrix products, arithmetic and copies ran while one was open for 10% -> 7% of each run, Pallas kernels for 0% -> 3%
where the time goes in v3:
time: 66.2 us; the launch traced here: 66 us
  starting transfers between devices  34 us (51%)
  waiting for transfers between devices  22.7 us (34%)
  matrix products  4.63 us (7%)
  Pallas kernels  2.27 us (3%)
  other arithmetic  1.07 us (2%)
  between operations  0.96 us (1%)
    ppermute x24, starting transfers between devices, swap(): lax.ppermute(value, 'expert', [(i, i ^ mask_of(i)) for i in range(size)])  34 us
    ppermute x24, waiting for transfers between devices, swap(): lax.ppermute(value, 'expert', [(i, i ^ mask_of(i)) for i in range(size)])  22.7 us
    pallas_call x2, Pallas kernels, slot_rows(): pl.pallas_call(functools.partial(kernel, groups, capacity), out_shape=(ch...  2.27 us
  transfers between devices with their start and end apart: 24, of which 14 were waited for; matrix products, arithmetic and copies ran while one was open for 7% of the time, Pallas kernels for 3%

profile of v3, /device:TPU:0, one launch (start us, length us, event | category | flops | bytes accessed | tf_op | source)
XLA Modules:
  0.0 66.0 jit_solution(11525448004144982638)
XLA Ops:
  1.7 1.1 %forward_rows.1 = (bf16[8,3584]{1,0:T(8,128)(2,1)S(1)}, bf16[8,3584]{1,0:T(8,128)(2,1)S(1)}, bf16[8,3584]{1,0:T(8,128)(2,1)S(1)}, bf16[8,3584]{1,0:T(8,128)(2,1)...) custom-call(bf16[8,3584]{1,0:T(8,128)(2,1)} %inbound_ref.1, f32[1,3584]{1,0:T(1,128)} %scale_ref.1, s32[2,8]{1,0:T(2,128)} %bitcast.19, ...), custom_call_target="tpu_custom_call" | custom-call | tf_op jit(solution)/shard_map/forward_rows/pallas_call | solution.py:96
  2.8 2.7 %collective-permute-start.2 = (bf16[8,3584]{1,0:T(8,128)(2,1)S(1)}, bf16[8,3584]{1,0:T(8,128)(2,1)S(1)}, u32[]{:S(2)}, u32[]{:S(2)}) collective-permute-start(bf16[8,3584]{1,0:T(8,128)(2,1)S(1)} %get-tuple-element.23), channel_id=1, source_target_pairs={{0,8},{1,9},{2,10},{3,11},{4,12},{5,13},{6,14},{7,15},{8,0},{9,1},... | collective-permute-start | bytes 172040 | tf_op jit(solution)/shard_map/forward/ppermute | solution.py:25
  5.5 2.6 %collective-permute-start.3 = (bf16[8,3584]{1,0:T(8,128)(2,1)S(1)}, bf16[8,3584]{1,0:T(8,128)(2,1)S(1)}, u32[]{:S(2)}, u32[]{:S(2)}) collective-permute-start(bf16[8,3584]{1,0:T(8,128)(2,1)S(1)} %get-tuple-element.24), channel_id=1, source_target_pairs={{0,16},{1,17},{2,18},{3,19},{4,20},{5,21},{6,22},{7,23},{8,24},{9,... | collective-permute-start | bytes 172040 | tf_op jit(solution)/shard_map/forward/ppermute | solution.py:25
  8.4 1.1 %backward_rows.1 = (bf16[8,3584]{1,0:T(8,128)(2,1)S(1)}, bf16[8,3584]{1,0:T(8,128)(2,1)S(1)}, bf16[8,3584]{1,0:T(8,128)(2,1)S(1)}, bf16[8,3584]{1,0:T(8,128)(2,1...) custom-call(bf16[8,3584]{1,0:T(8,128)(2,1)} %cotangent_ref.1, s32[2,8]{1,0:T(2,128)} %bitcast.21, ...), custom_call_target="tpu_custom_call" | custom-call | tf_op jit(solution)/shard_map/backward_rows/pallas_call | solution.py:96
  9.6 0.7 %collective-permute-start.14 = (bf16[8,3584]{1,0:T(8,128)(2,1)S(1)}, bf16[8,3584]{1,0:T(8,128)(2,1)S(1)}, u32[]{:S(2)}, u32[]{:S(2)}) collective-permute-start(bf16[8,3584]{1,0:T(8,128)(2,1)S(1)} %get-tuple-element.31), channel_id=1, source_target_pairs={{0,8},{1,9},{2,10},{3,11},{4,12},{5,13},{6,14},{7,15},{8,0},{9,1},... | collective-permute-start | bytes 172040 | tf_op jit(solution)/shard_map/backward/ppermute | solution.py:25
  10.4 1.7 %collective-permute-done.3 = bf16[8,3584]{1,0:T(8,128)(2,1)S(1)} collective-permute-done((bf16[8,3584]{1,0:T(8,128)(2,1)S(1)}, bf16[8,3584]{1,0:T(8,128)(2,1)S(1)}, u32[]{:S(2)}, u32[]{:S(2)}) %collective-permute-start.3) | collective-permute-done | bytes 57376 | tf_op jit(solution)/shard_map/forward/ppermute | solution.py:25
  12.1 1.9 %collective-permute-start.15 = (bf16[8,3584]{1,0:T(8,128)(2,1)S(1)}, bf16[8,3584]{1,0:T(8,128)(2,1)S(1)}, u32[]{:S(2)}, u32[]{:S(2)}) collective-permute-start(bf16[8,3584]{1,0:T(8,128)(2,1)S(1)} %get-tuple-element.32), channel_id=1, source_target_pairs={{0,16},{1,17},{2,18},{3,19},{4,20},{5,21},{6,22},{7,23},{8,24},{9,... | collective-permute-start | bytes 172040 | tf_op jit(solution)/shard_map/backward/ppermute | solution.py:25
  14.3 1.8 %collective-permute-start.16 = (bf16[8,3584]{1,0:T(8,128)(2,1)S(1)}, bf16[8,3584]{1,0:T(8,128)(2,1)S(1)}, u32[]{:S(2)}, u32[]{:S(2)}) collective-permute-start(bf16[8,3584]{1,0:T(8,128)(2,1)S(1)} %get-tuple-element.33), channel_id=1, source_target_pairs={{0,24},{1,25},{2,26},{3,27},{4,28},{5,29},{6,30},{7,31},{8,16},{9,... | collective-permute-start | bytes 172040 | tf_op jit(solution)/shard_map/backward/ppermute | solution.py:25
  16.1 1.6 %collective-permute-start.5 = (bf16[32,3584]{1,0:T(8,128)(2,1)S(1)}, bf16[32,3584]{1,0:T(8,128)(2,1)S(1)}, u32[]{:S(2)}, u32[]{:S(2)}) collective-permute-start(bf16[32,3584]{1,0:T(8,128)(2,1)S(1)} %pad_maximum_fusion.6), channel_id=1, source_target_pairs={{0,2},{1,5},{2,0},{3,7},{4,6},{5,1},{6,4},{7,3},{8,10},{9,13},{10,... | collective-permute-start | bytes 688136 | tf_op jit(solution)/shard_map/forward/ppermute | solution.py:25
  18.3 2.0 %collective-permute-done.16 = bf16[8,3584]{1,0:T(8,128)(2,1)S(1)} collective-permute-done((bf16[8,3584]{1,0:T(8,128)(2,1)S(1)}, bf16[8,3584]{1,0:T(8,128)(2,1)S(1)}, u32[]{:S(2)}, u32[]{:S(2)}) %collective-permute-start.16) | collective-permute-done | bytes 57376 | tf_op jit(solution)/shard_map/backward/ppermute | solution.py:25
  20.4 1.6 %collective-permute-start.17 = (bf16[32,3584]{1,0:T(8,128)(2,1)S(1)}, bf16[32,3584]{1,0:T(8,128)(2,1)S(1)}, u32[]{:S(2)}, u32[]{:S(2)}) collective-permute-start(bf16[32,3584]{1,0:T(8,128)(2,1)S(1)} %pad_maximum_fusion.7), channel_id=1, source_target_pairs={{0,2},{1,5},{2,0},{3,7},{4,6},{5,1},{6,4},{7,3},{8,10},{9,13},{10,... | collective-permute-start | bytes 688136 | tf_op jit(solution)/shard_map/backward/ppermute | solution.py:25
  22.2 1.6 %collective-permute-start.7 = (bf16[64,3584]{1,0:T(8,128)(2,1)S(1)}, bf16[64,3584]{1,0:T(8,128)(2,1)S(1)}, u32[]{:S(2)}, u32[]{:S(2)}) collective-permute-start(bf16[64,3584]{1,0:T(8,128)(2,1)S(1)} %constant_dynamic-update-slice_fusion), channel_id=1, source_target_pairs={{0,4},{1,3},{2,6},{3,1},{4,0},{5,7},{6,2},{7,5},{8,12},{9,11},{10,... | collective-permute-start | bytes 1376264 | tf_op jit(solution)/shard_map/forward/ppermute | solution.py:25
  24.1 4.8 %collective-permute-done.17 = bf16[32,3584]{1,0:T(8,128)(2,1)S(1)} collective-permute-done((bf16[32,3584]{1,0:T(8,128)(2,1)S(1)}, bf16[32,3584]{1,0:T(8,128)(2,1)S(1)}, u32[]{:S(2)}, u32[]{:S(2)}) %collective-permute-start.17) | collective-permute-done | bytes 229408 | tf_op jit(solution)/shard_map/backward/ppermute | solution.py:25
  28.9 1.6 %collective-permute-start.18 = (bf16[64,3584]{1,0:T(8,128)(2,1)S(1)}, bf16[64,3584]{1,0:T(8,128)(2,1)S(1)}, u32[]{:S(2)}, u32[]{:S(2)}) collective-permute-start(bf16[64,3584]{1,0:T(8,128)(2,1)S(1)} %constant_dynamic-update-slice_fusion.5), channel_id=1, source_target_pairs={{0,4},{1,3},{2,6},{3,1},{4,0},{5,7},{6,2},{7,5},{8,12},{9,11},{10,... | collective-permute-start | bytes 1376264 | tf_op jit(solution)/shard_map/backward/ppermute | solution.py:25
  31.9 1.6 %collective-permute-start.9 = (bf16[64,3584]{1,0:T(8,128)(2,1)S(1)}, bf16[64,3584]{1,0:T(8,128)(2,1)S(1)}, u32[]{:S(2)}, u32[]{:S(2)}) collective-permute-start(bf16[64,3584]{1,0:T(8,128)(2,1)S(1)} %slice.145), channel_id=1, source_target_pairs={{0,4},{1,3},{2,6},{3,1},{4,0},{5,7},{6,2},{7,5},{8,12},{9,11},{10,... | collective-permute-start | bytes 1376264 | tf_op jit(solution)/shard_map/forward/ppermute | solution.py:25
  33.5 4.0 %collective-permute-done.18 = bf16[64,3584]{1,0:T(8,128)(2,1)S(1)} collective-permute-done((bf16[64,3584]{1,0:T(8,128)(2,1)S(1)}, bf16[64,3584]{1,0:T(8,128)(2,1)S(1)}, u32[]{:S(2)}, u32[]{:S(2)}) %collective-permute-start.18) | collective-permute-done | bytes 458784 | tf_op jit(solution)/shard_map/backward/ppermute | solution.py:25
  37.5 0.7 %fusion.31 = (bf16[128,256]{1,0:T(8,128)(2,1)S(1)}, bf16[128,256]{1,0:T(8,128)(2,1)S(1)}) fusion(f32[128,128]{1,0:T(8,128)S(1)} %get-tuple-element.43, f32[128,128]{1,0:T(8,128)S(1)} %get-tuple-element.40, f32[128,128]{1,0:T(8,128)S(1)} %get-tuple-element.41, f32[128,128]{1,0:T(8,128)S(1)} %get-tuple-element.42, ...), kind=kOutput, calls=%fused_computation.52 | convolution fusion | flops 239042560 | bytes 3145728 | tf_op jit(solution)/shard_map/rd,hd->rh/dot_general | solution.py:226
  38.3 1.3 %fusion.7 = f32[128,3584]{1,0:T(8,128)S(1)} fusion(bf16[3584,128]{1,0:T(8,128)(2,1)S(1)} %collective-permute-done.1, bf16[3584,128]{1,0:T(8,128)(2,1)S(1)} %bitcast.25, bf16[3584,128]{1,0:T(8,128)(2,1)S(1)} %collective-permute-done, bf16[3584,128]{1,0:T(8,128)(2,1)S(1)} %bitcast.28, bf16[128,256]{1,0:T(8,128)(2,1)S(1)} %get-tuple-element.39, ...), kind=kOutput, calls=%fused_computation.15 | convolution fusion | flops 484704256 | bytes 5636096 | tf_op jit(solution)/shard_map/rh,dh->rd/dot_general | solution.py:231
  39.6 1.6 %collective-permute-start.19 = (bf16[64,3584]{1,0:T(8,128)(2,1)S(1)}, bf16[64,3584]{1,0:T(8,128)(2,1)S(1)}, u32[]{:S(2)}, u32[]{:S(2)}) collective-permute-start(bf16[64,3584]{1,0:T(8,128)(2,1)S(1)} %slice.144), channel_id=1, source_target_pairs={{0,2},{1,5},{2,0},{3,7},{4,6},{5,1},{6,4},{7,3},{8,10},{9,13},{10,... | collective-permute-start | bytes 1376264 | tf_op jit(solution)/shard_map/backward/ppermute | solution.py:25
  41.2 3.3 %collective-permute-done.9 = bf16[64,3584]{1,0:T(8,128)(2,1)S(1)} collective-permute-done((bf16[64,3584]{1,0:T(8,128)(2,1)S(1)}, bf16[64,3584]{1,0:T(8,128)(2,1)S(1)}, u32[]{:S(2)}, u32[]{:S(2)}) %collective-permute-start.9) | collective-permute-done | bytes 458784 | tf_op jit(solution)/shard_map/forward/ppermute | solution.py:25
  44.6 1.6 %collective-permute-start.10 = (bf16[32,3584]{1,0:T(8,128)(2,1)S(1)}, bf16[32,3584]{1,0:T(8,128)(2,1)S(1)}, u32[]{:S(2)}, u32[]{:S(2)}) collective-permute-start(bf16[32,3584]{1,0:T(8,128)(2,1)S(1)} %slice.147), channel_id=1, source_target_pairs={{0,2},{1,5},{2,0},{3,7},{4,6},{5,1},{6,4},{7,3},{8,10},{9,13},{10,... | collective-permute-start | bytes 688136 | tf_op jit(solution)/shard_map/forward/ppermute | solution.py:25
  46.2 2.0 %collective-permute-done.19 = bf16[64,3584]{1,0:T(8,128)(2,1)S(1)} collective-permute-done((bf16[64,3584]{1,0:T(8,128)(2,1)S(1)}, bf16[64,3584]{1,0:T(8,128)(2,1)S(1)}, u32[]{:S(2)}, u32[]{:S(2)}) %collective-permute-start.19) | collective-permute-done | bytes 458784 | tf_op jit(solution)/shard_map/backward/ppermute | solution.py:25
  48.4 1.6 %collective-permute-start.20 = (bf16[32,3584]{1,0:T(8,128)(2,1)S(1)}, bf16[32,3584]{1,0:T(8,128)(2,1)S(1)}, u32[]{:S(2)}, u32[]{:S(2)}) collective-permute-start(bf16[32,3584]{1,0:T(8,128)(2,1)S(1)} %slice.146), channel_id=1, source_target_pairs={{0,4},{1,3},{2,6},{3,1},{4,0},{5,7},{6,2},{7,5},{8,12},{9,11},{10,... | collective-permute-start | bytes 688136 | tf_op jit(solution)/shard_map/backward/ppermute | solution.py:25
  49.9 1.1 %collective-permute-done.10 = bf16[32,3584]{1,0:T(8,128)(2,1)S(1)} collective-permute-done((bf16[32,3584]{1,0:T(8,128)(2,1)S(1)}, bf16[32,3584]{1,0:T(8,128)(2,1)S(1)}, u32[]{:S(2)}, u32[]{:S(2)}) %collective-permute-start.10) | collective-permute-done | bytes 229408 | tf_op jit(solution)/shard_map/forward/ppermute | solution.py:25
  51.1 1.8 %collective-permute-start.13 = (bf16[8,3584]{1,0:T(8,128)(2,1)S(1)}, bf16[8,3584]{1,0:T(8,128)(2,1)S(1)}, u32[]{:S(2)}, u32[]{:S(2)}) collective-permute-start(bf16[8,3584]{1,0:T(8,128)(2,1)S(1)} %get-tuple-element.49), channel_id=1, source_target_pairs={{0,24},{1,25},{2,26},{3,27},{4,28},{5,29},{6,30},{7,31},{8,16},{9,... | collective-permute-start | bytes 172040 | tf_op jit(solution)/shard_map/forward/ppermute | solution.py:25
  53.0 3.4 %collective-permute-start.12 = (bf16[8,3584]{1,0:T(8,128)(2,1)S(1)}, bf16[8,3584]{1,0:T(8,128)(2,1)S(1)}, u32[]{:S(2)}, u32[]{:S(2)}) collective-permute-start(bf16[8,3584]{1,0:T(8,128)(2,1)S(1)} %get-tuple-element.50), channel_id=1, source_target_pairs={{0,16},{1,17},{2,18},{3,19},{4,20},{5,21},{6,22},{7,23},{8,24},{9,... | collective-permute-start | bytes 172040 | tf_op jit(solution)/shard_map/forward/ppermute | solution.py:25
  56.5 1.5 %collective-permute-start.23 = (bf16[8,3584]{1,0:T(8,128)(2,1)S(1)}, bf16[8,3584]{1,0:T(8,128)(2,1)S(1)}, u32[]{:S(2)}, u32[]{:S(2)}) collective-permute-start(bf16[8,3584]{1,0:T(8,128)(2,1)S(1)} %get-tuple-element.45), channel_id=1, source_target_pairs={{0,24},{1,25},{2,26},{3,27},{4,28},{5,29},{6,30},{7,31},{8,16},{9,... | collective-permute-start | bytes 172040 | tf_op jit(solution)/shard_map/backward/ppermute | solution.py:25
  58.0 2.0 %collective-permute-start.22 = (bf16[8,3584]{1,0:T(8,128)(2,1)S(1)}, bf16[8,3584]{1,0:T(8,128)(2,1)S(1)}, u32[]{:S(2)}, u32[]{:S(2)}) collective-permute-start(bf16[8,3584]{1,0:T(8,128)(2,1)S(1)} %get-tuple-element.46), channel_id=1, source_target_pairs={{0,16},{1,17},{2,18},{3,19},{4,20},{5,21},{6,22},{7,23},{8,24},{9,... | collective-permute-start | bytes 172040 | tf_op jit(solution)/shard_map/backward/ppermute | solution.py:25
  60.0 1.5 %collective-permute-start.21 = (bf16[8,3584]{1,0:T(8,128)(2,1)S(1)}, bf16[8,3584]{1,0:T(8,128)(2,1)S(1)}, u32[]{:S(2)}, u32[]{:S(2)}) collective-permute-start(bf16[8,3584]{1,0:T(8,128)(2,1)S(1)} %get-tuple-element.47), channel_id=1, source_target_pairs={{0,8},{1,9},{2,10},{3,11},{4,12},{5,13},{6,14},{7,15},{8,0},{9,1},... | collective-permute-start | bytes 172040 | tf_op jit(solution)/shard_map/backward/ppermute | solution.py:25
  61.6 1.8 %collective-permute-done.12 = bf16[8,3584]{1,0:T(8,128)(2,1)S(1)} collective-permute-done((bf16[8,3584]{1,0:T(8,128)(2,1)S(1)}, bf16[8,3584]{1,0:T(8,128)(2,1)S(1)}, u32[]{:S(2)}, u32[]{:S(2)}) %collective-permute-start.12) | collective-permute-done | bytes 57376 | tf_op jit(solution)/shard_map/forward/ppermute | solution.py:25
  63.3 0.9 %fusion = bf16[8,3584]{1,0:T(8,128)(2,1)} fusion(f32[32,8]{1,0:T(8,128)S(1)} %get-tuple-element.19, bf16[8,3584]{1,0:T(8,128)(2,1)S(1)} %collective-permute-done.13, bf16[8,3584]{1,0:T(8,128)(2,1)S(1)} %collective-permute-done.12, bf16[8,3584]{1,0:T(8,128)(2,1)S(1)} %collective-permute-done.11, bf16[8,3584]{1,0:T(8,128)(2,1)S(1)} %get-tuple-element.48, ...), kind=kOutput, calls=%fused_computation.2 | convolution fusion | flops 12013568 | bytes 345088 | tf_op jit(solution)/shard_map/dot_general | solution.py:223
  65.2 0.7 %fusion.39 = bf16[8,3584]{1,0:T(8,128)(2,1)} fusion(bf16[8,3584]{1,0:T(8,128)(2,1)S(1)} %copy-done.4, f32[8,3584]{1,0:T(8,128)S(1)} %get-tuple-element.62, bf16[8,3584]{1,0:T(8,128)(2,1)S(1)} %copy-done.1, f32[8]{0:T(128)S(1)} %broadcast_multiply_fusion, f32[8]{0:T(128)S(1)} %get-tuple-element.61, f32[8]{0:T(128)S(1)} %get-tuple-element.60), kind=kLoop, calls=%fused_computation.64 | loop fusion | flops 229376 | bytes 286816 | tf_op jit(solution)/shard_map/convert_element_type | solution.py:241
  (69 shorter events, 5.8 us)
Async XLA Ops:
  0.6 23.2 %copy-start.2 = (bf16[1,1,32,8,256]{4,3,2,1,0:T(8,128)(2,1)S(1)}, bf16[1,1,32,8,256]{4,3,2,1,0:T(8,128)(2,1)}, u32[]{:S(2)}) copy-start(bf16[1,1,32,8,256]{4,3,2,1,0:T(8,128)(2,1)} %param.23) | copy-start | bytes 393220
  0.6 7.5 %collective-permute-start = (bf16[3584,128]{1,0:T(8,128)(2,1)}, bf16[3584,128]{1,0:T(8,128)(2,1)S(1)}, u32[]{:S(2)}, u32[]{:S(2)}) collective-permute-start(bf16[3584,128]{1,0:T(8,128)(2,1)} %bitcast.26), channel_id=1, source_target_pairs={{0,1},{1,0},{2,3},{3,2},{4,5},{5,4},{6,7},{7,6},{8,9},{9,8},{10,11... | collective-permute-start | bytes 2752520 | tf_op jit(solution)/shard_map/swaps/ppermute | solution.py:25
  1.2 7.3 %collective-permute-start.1 = (bf16[3584,128]{1,0:T(8,128)(2,1)}, bf16[3584,128]{1,0:T(8,128)(2,1)S(1)}, u32[]{:S(2)}, u32[]{:S(2)}) collective-permute-start(bf16[3584,128]{1,0:T(8,128)(2,1)} %bitcast.23), channel_id=1, source_target_pairs={{0,1},{1,0},{2,3},{3,2},{4,5},{5,4},{6,7},{7,6},{8,9},{9,8},{10,11... | collective-permute-start | bytes 2752520 | tf_op jit(solution)/shard_map/swaps/ppermute | solution.py:25
  1.2 30.2 %collective-permute-start.8 = (bf16[128,3584]{1,0:T(8,128)(2,1)}, bf16[128,3584]{1,0:T(8,128)(2,1)S(1)}, u32[]{:S(2)}, u32[]{:S(2)}) collective-permute-start(bf16[128,3584]{1,0:T(8,128)(2,1)} %bitcast.13), channel_id=1, source_target_pairs={{0,1},{1,0},{2,3},{3,2},{4,5},{5,4},{6,7},{7,6},{8,9},{9,8},{10,11... | collective-permute-start | bytes 2752520 | tf_op jit(solution)/shard_map/swaps/ppermute | solution.py:25
  2.8 6.8 %collective-permute-start.2 = (bf16[8,3584]{1,0:T(8,128)(2,1)S(1)}, bf16[8,3584]{1,0:T(8,128)(2,1)S(1)}, u32[]{:S(2)}, u32[]{:S(2)}) collective-permute-start(bf16[8,3584]{1,0:T(8,128)(2,1)S(1)} %get-tuple-element.23), channel_id=1, source_target_pairs={{0,8},{1,9},{2,10},{3,11},{4,12},{5,13},{6,14},{7,15},{8,0},{9,1},... | collective-permute-start | bytes 172040 | tf_op jit(solution)/shard_map/forward/ppermute | solution.py:25
  5.5 6.5 %collective-permute-start.3 = (bf16[8,3584]{1,0:T(8,128)(2,1)S(1)}, bf16[8,3584]{1,0:T(8,128)(2,1)S(1)}, u32[]{:S(2)}, u32[]{:S(2)}) collective-permute-start(bf16[8,3584]{1,0:T(8,128)(2,1)S(1)} %get-tuple-element.24), channel_id=1, source_target_pairs={{0,16},{1,17},{2,18},{3,19},{4,20},{5,21},{6,22},{7,23},{8,24},{9,... | collective-permute-start | bytes 172040 | tf_op jit(solution)/shard_map/forward/ppermute | solution.py:25
  8.2 6.1 %collective-permute-start.4 = (bf16[8,3584]{1,0:T(8,128)(2,1)S(1)}, bf16[8,3584]{1,0:T(8,128)(2,1)S(1)}, u32[]{:S(2)}, u32[]{:S(2)}) collective-permute-start(bf16[8,3584]{1,0:T(8,128)(2,1)S(1)} %get-tuple-element.25), channel_id=1, source_target_pairs={{0,24},{1,25},{2,26},{3,27},{4,28},{5,29},{6,30},{7,31},{8,16},{9,... | collective-permute-start | bytes 172040 | tf_op jit(solution)/shard_map/forward/ppermute | solution.py:25
  8.4 13.8 %collective-permute-start.6 = (bf16[32,8,256]{2,1,0:T(8,128)(2,1)}, bf16[32,8,256]{2,1,0:T(8,128)(2,1)S(1)}, u32[]{:S(2)}, u32[]{:S(2)}) collective-permute-start(bf16[32,8,256]{2,1,0:T(8,128)(2,1)} %bitcast.16), channel_id=1, source_target_pairs={{0,1},{1,0},{2,3},{3,2},{4,5},{5,4},{6,7},{7,6},{8,9},{9,8},{10,11... | collective-permute-start | bytes 393224 | tf_op jit(solution)/shard_map/swaps/ppermute | solution.py:25
  9.6 6.5 %collective-permute-start.14 = (bf16[8,3584]{1,0:T(8,128)(2,1)S(1)}, bf16[8,3584]{1,0:T(8,128)(2,1)S(1)}, u32[]{:S(2)}, u32[]{:S(2)}) collective-permute-start(bf16[8,3584]{1,0:T(8,128)(2,1)S(1)} %get-tuple-element.31), channel_id=1, source_target_pairs={{0,8},{1,9},{2,10},{3,11},{4,12},{5,13},{6,14},{7,15},{8,0},{9,1},... | collective-permute-start | bytes 172040 | tf_op jit(solution)/shard_map/backward/ppermute | solution.py:25
  10.4 20.4 %copy-start.5 = (bf16[1,1,3584,128]{3,2,1,0:T(8,128)(2,1)S(1)}, bf16[1,1,3584,128]{3,2,1,0:T(8,128)(2,1)}, u32[]{:S(2)}) copy-start(bf16[1,1,3584,128]{3,2,1,0:T(8,128)(2,1)} %param.21) | copy-start | bytes 2752516
  10.4 20.4 %copy-start.6 = (bf16[1,1,3584,128]{3,2,1,0:T(8,128)(2,1)S(1)}, bf16[1,1,3584,128]{3,2,1,0:T(8,128)(2,1)}, u32[]{:S(2)}) copy-start(bf16[1,1,3584,128]{3,2,1,0:T(8,128)(2,1)} %param.20) | copy-start | bytes 2752516
  12.1 6.3 %collective-permute-start.15 = (bf16[8,3584]{1,0:T(8,128)(2,1)S(1)}, bf16[8,3584]{1,0:T(8,128)(2,1)S(1)}, u32[]{:S(2)}, u32[]{:S(2)}) collective-permute-start(bf16[8,3584]{1,0:T(8,128)(2,1)S(1)} %get-tuple-element.32), channel_id=1, source_target_pairs={{0,16},{1,17},{2,18},{3,19},{4,20},{5,21},{6,22},{7,23},{8,24},{9,... | collective-permute-start | bytes 172040 | tf_op jit(solution)/shard_map/backward/ppermute | solution.py:25
  14.3 6.1 %collective-permute-start.16 = (bf16[8,3584]{1,0:T(8,128)(2,1)S(1)}, bf16[8,3584]{1,0:T(8,128)(2,1)S(1)}, u32[]{:S(2)}, u32[]{:S(2)}) collective-permute-start(bf16[8,3584]{1,0:T(8,128)(2,1)S(1)} %get-tuple-element.33), channel_id=1, source_target_pairs={{0,24},{1,25},{2,26},{3,27},{4,28},{5,29},{6,30},{7,31},{8,16},{9,... | collective-permute-start | bytes 172040 | tf_op jit(solution)/shard_map/backward/ppermute | solution.py:25
  16.1 6.1 %collective-permute-start.5 = (bf16[32,3584]{1,0:T(8,128)(2,1)S(1)}, bf16[32,3584]{1,0:T(8,128)(2,1)S(1)}, u32[]{:S(2)}, u32[]{:S(2)}) collective-permute-start(bf16[32,3584]{1,0:T(8,128)(2,1)S(1)} %pad_maximum_fusion.6), channel_id=1, source_target_pairs={{0,2},{1,5},{2,0},{3,7},{4,6},{5,1},{6,4},{7,3},{8,10},{9,13},{10,... | collective-permute-start | bytes 688136 | tf_op jit(solution)/shard_map/forward/ppermute | solution.py:25
  20.4 8.5 %collective-permute-start.17 = (bf16[32,3584]{1,0:T(8,128)(2,1)S(1)}, bf16[32,3584]{1,0:T(8,128)(2,1)S(1)}, u32[]{:S(2)}, u32[]{:S(2)}) collective-permute-start(bf16[32,3584]{1,0:T(8,128)(2,1)S(1)} %pad_maximum_fusion.7), channel_id=1, source_target_pairs={{0,2},{1,5},{2,0},{3,7},{4,6},{5,1},{6,4},{7,3},{8,10},{9,13},{10,... | collective-permute-start | bytes 688136 | tf_op jit(solution)/shard_map/backward/ppermute | solution.py:25
  22.2 8.5 %collective-permute-start.7 = (bf16[64,3584]{1,0:T(8,128)(2,1)S(1)}, bf16[64,3584]{1,0:T(8,128)(2,1)S(1)}, u32[]{:S(2)}, u32[]{:S(2)}) collective-permute-start(bf16[64,3584]{1,0:T(8,128)(2,1)S(1)} %constant_dynamic-update-slice_fusion), channel_id=1, source_target_pairs={{0,4},{1,3},{2,6},{3,1},{4,0},{5,7},{6,2},{7,5},{8,12},{9,11},{10,... | collective-permute-start | bytes 1376264 | tf_op jit(solution)/shard_map/forward/ppermute | solution.py:25
  28.9 2.5 %copy-start = (bf16[1,1,128,3584]{3,2,1,0:T(8,128)(2,1)S(1)}, bf16[1,1,128,3584]{3,2,1,0:T(8,128)(2,1)}, u32[]{:S(2)}) copy-start(bf16[1,1,128,3584]{3,2,1,0:T(8,128)(2,1)} %param.22) | copy-start | bytes 2752516
  28.9 8.5 %collective-permute-start.18 = (bf16[64,3584]{1,0:T(8,128)(2,1)S(1)}, bf16[64,3584]{1,0:T(8,128)(2,1)S(1)}, u32[]{:S(2)}, u32[]{:S(2)}) collective-permute-start(bf16[64,3584]{1,0:T(8,128)(2,1)S(1)} %constant_dynamic-update-slice_fusion.5), channel_id=1, source_target_pairs={{0,4},{1,3},{2,6},{3,1},{4,0},{5,7},{6,2},{7,5},{8,12},{9,11},{10,... | collective-permute-start | bytes 1376264 | tf_op jit(solution)/shard_map/backward/ppermute | solution.py:25
  31.9 12.5 %collective-permute-start.9 = (bf16[64,3584]{1,0:T(8,128)(2,1)S(1)}, bf16[64,3584]{1,0:T(8,128)(2,1)S(1)}, u32[]{:S(2)}, u32[]{:S(2)}) collective-permute-start(bf16[64,3584]{1,0:T(8,128)(2,1)S(1)} %slice.145), channel_id=1, source_target_pairs={{0,4},{1,3},{2,6},{3,1},{4,0},{5,7},{6,2},{7,5},{8,12},{9,11},{10,... | collective-permute-start | bytes 1376264 | tf_op jit(solution)/shard_map/forward/ppermute | solution.py:25
  39.6 8.5 %collective-permute-start.19 = (bf16[64,3584]{1,0:T(8,128)(2,1)S(1)}, bf16[64,3584]{1,0:T(8,128)(2,1)S(1)}, u32[]{:S(2)}, u32[]{:S(2)}) collective-permute-start(bf16[64,3584]{1,0:T(8,128)(2,1)S(1)} %slice.144), channel_id=1, source_target_pairs={{0,2},{1,5},{2,0},{3,7},{4,6},{5,1},{6,4},{7,3},{8,10},{9,13},{10,... | collective-permute-start | bytes 1376264 | tf_op jit(solution)/shard_map/backward/ppermute | solution.py:25
  44.6 6.5 %collective-permute-start.10 = (bf16[32,3584]{1,0:T(8,128)(2,1)S(1)}, bf16[32,3584]{1,0:T(8,128)(2,1)S(1)}, u32[]{:S(2)}, u32[]{:S(2)}) collective-permute-start(bf16[32,3584]{1,0:T(8,128)(2,1)S(1)} %slice.147), channel_id=1, source_target_pairs={{0,2},{1,5},{2,0},{3,7},{4,6},{5,1},{6,4},{7,3},{8,10},{9,13},{10,... | collective-permute-start | bytes 688136 | tf_op jit(solution)/shard_map/forward/ppermute | solution.py:25
  48.3 15.0 %copy-start.3 = (bf16[8,3584]{1,0:T(8,128)(2,1)S(1)}, bf16[8,3584]{1,0:T(8,128)(2,1)}, u32[]{:S(2)}) copy-start(bf16[8,3584]{1,0:T(8,128)(2,1)} %inbound_ref.1) | copy-start | bytes 172036
  48.3 16.5 %copy-start.4 = (bf16[8,3584]{1,0:T(8,128)(2,1)S(1)}, bf16[8,3584]{1,0:T(8,128)(2,1)}, u32[]{:S(2)}) copy-start(bf16[8,3584]{1,0:T(8,128)(2,1)} %param.14) | copy-start | bytes 172036
  48.4 8.0 %collective-permute-start.20 = (bf16[32,3584]{1,0:T(8,128)(2,1)S(1)}, bf16[32,3584]{1,0:T(8,128)(2,1)S(1)}, u32[]{:S(2)}, u32[]{:S(2)}) collective-permute-start(bf16[32,3584]{1,0:T(8,128)(2,1)S(1)} %slice.146), channel_id=1, source_target_pairs={{0,4},{1,3},{2,6},{3,1},{4,0},{5,7},{6,2},{7,5},{8,12},{9,11},{10,... | collective-permute-start | bytes 688136 | tf_op jit(solution)/shard_map/backward/ppermute | solution.py:25
  51.1 14.1 %copy-start.1 = (bf16[8,3584]{1,0:T(8,128)(2,1)S(1)}, bf16[8,3584]{1,0:T(8,128)(2,1)}, u32[]{:S(2)}) copy-start(bf16[8,3584]{1,0:T(8,128)(2,1)} %cotangent_ref.1) | copy-start | bytes 172036
  51.1 8.9 %collective-permute-start.13 = (bf16[8,3584]{1,0:T(8,128)(2,1)S(1)}, bf16[8,3584]{1,0:T(8,128)(2,1)S(1)}, u32[]{:S(2)}, u32[]{:S(2)}) collective-permute-start(bf16[8,3584]{1,0:T(8,128)(2,1)S(1)} %get-tuple-element.49), channel_id=1, source_target_pairs={{0,24},{1,25},{2,26},{3,27},{4,28},{5,29},{6,30},{7,31},{8,16},{9,... | collective-permute-start | bytes 172040 | tf_op jit(solution)/shard_map/forward/ppermute | solution.py:25
  53.0 10.4 %collective-permute-start.12 = (bf16[8,3584]{1,0:T(8,128)(2,1)S(1)}, bf16[8,3584]{1,0:T(8,128)(2,1)S(1)}, u32[]{:S(2)}, u32[]{:S(2)}) collective-permute-start(bf16[8,3584]{1,0:T(8,128)(2,1)S(1)} %get-tuple-element.50), channel_id=1, source_target_pairs={{0,16},{1,17},{2,18},{3,19},{4,20},{5,21},{6,22},{7,23},{8,24},{9,... | collective-permute-start | bytes 172040 | tf_op jit(solution)/shard_map/forward/ppermute | solution.py:25
  56.4 6.9 %collective-permute-start.11 = (bf16[8,3584]{1,0:T(8,128)(2,1)S(1)}, bf16[8,3584]{1,0:T(8,128)(2,1)S(1)}, u32[]{:S(2)}, u32[]{:S(2)}) collective-permute-start(bf16[8,3584]{1,0:T(8,128)(2,1)S(1)} %get-tuple-element.51), channel_id=1, source_target_pairs={{0,8},{1,9},{2,10},{3,11},{4,12},{5,13},{6,14},{7,15},{8,0},{9,1},... | collective-permute-start | bytes 172040 | tf_op jit(solution)/shard_map/forward/ppermute | solution.py:25
  56.5 7.8 %collective-permute-start.23 = (bf16[8,3584]{1,0:T(8,128)(2,1)S(1)}, bf16[8,3584]{1,0:T(8,128)(2,1)S(1)}, u32[]{:S(2)}, u32[]{:S(2)}) collective-permute-start(bf16[8,3584]{1,0:T(8,128)(2,1)S(1)} %get-tuple-element.45), channel_id=1, source_target_pairs={{0,24},{1,25},{2,26},{3,27},{4,28},{5,29},{6,30},{7,31},{8,16},{9,... | collective-permute-start | bytes 172040 | tf_op jit(solution)/shard_map/backward/ppermute | solution.py:25
  58.0 6.7 %collective-permute-start.22 = (bf16[8,3584]{1,0:T(8,128)(2,1)S(1)}, bf16[8,3584]{1,0:T(8,128)(2,1)S(1)}, u32[]{:S(2)}, u32[]{:S(2)}) collective-permute-start(bf16[8,3584]{1,0:T(8,128)(2,1)S(1)} %get-tuple-element.46), channel_id=1, source_target_pairs={{0,16},{1,17},{2,18},{3,19},{4,20},{5,21},{6,22},{7,23},{8,24},{9,... | collective-permute-start | bytes 172040 | tf_op jit(solution)/shard_map/backward/ppermute | solution.py:25
  60.0 4.8 %collective-permute-start.21 = (bf16[8,3584]{1,0:T(8,128)(2,1)S(1)}, bf16[8,3584]{1,0:T(8,128)(2,1)S(1)}, u32[]{:S(2)}, u32[]{:S(2)}) collective-permute-start(bf16[8,3584]{1,0:T(8,128)(2,1)S(1)} %get-tuple-element.47), channel_id=1, source_target_pairs={{0,8},{1,9},{2,10},{3,11},{4,12},{5,13},{6,14},{7,15},{8,0},{9,1},... | collective-permute-start | bytes 172040 | tf_op jit(solution)/shard_map/backward/ppermute | solution.py:25

commit v4 on v3

--- a/solution.py
+++ b/solution.py
@@ -161,7 +161,6 @@
         gate_other = with_core(w_gate[0, 0])
         up_other = with_core(w_up[0, 0])
         down_other = with_core(w_down[0, 0])
-        stash_other = with_core(stash[0, 0])
     chunks, weighted_fwd, scale_rows = slot_rows(
         forward_rows_kernel,
         "forward_rows",
@@ -192,11 +191,11 @@
         own = join([own_chunk] + arrived[1:])
     with jax.named_scope("backward"):
         grad_own = join(along_groups(chunks))
+        grad_own, stash_here = lax.optimization_barrier((grad_own, stash))
+        with jax.named_scope("swaps"):
+            stash_other = with_core(stash_here[0, 0])
     with jax.named_scope("forward"):
         half = join([own, with_first(own)])
-        half, stash_other = lax.optimization_barrier(
-            (half, stash_other)
-        )
         flat_rows = join([half, with_second(half)])
     with jax.named_scope("backward"):
         half = join([grad_own, with_first(grad_own)])

time: 66.2 us -> 63.2 us (0.955)
  waiting for transfers between devices: 22.7 us -> 18.9 us
    ppermute x24, waiting for transfers between devices: 22.7 us -> 18.9 us  [swap(): lax.ppermute(value, 'expert', [(i, i ^ mask_of(i)) for i in range(size)])]
  transfers between devices with their start and end apart: 24 -> 24, of which waited for: 14 -> 12; matrix products, arithmetic and copies ran while one was open for 7% -> 8% of each run, Pallas kernels for 3% -> 4%
where the time goes in v4:
time: 63.2 us; the launch traced here: 63 us
  starting transfers between devices  34.2 us (54%)
  waiting for transfers between devices  18.9 us (30%)
  matrix products  4.62 us (7%)
  Pallas kernels  2.28 us (4%)
  other arithmetic  1.1 us (2%)
  between operations  0.97 us (2%)
  local copies, waits for them, and re-layouts  0.89 us (1%)
    ppermute x24, starting transfers between devices, swap(): lax.ppermute(value, 'expert', [(i, i ^ mask_of(i)) for i in range(size)])  34.2 us
    ppermute x24, waiting for transfers between devices, swap(): lax.ppermute(value, 'expert', [(i, i ^ mask_of(i)) for i in range(size)])  18.9 us
    pallas_call x2, Pallas kernels, slot_rows(): pl.pallas_call(functools.partial(kernel, groups, capacity), out_shape=(ch...  2.28 us
    dot_general x1, matrix products, body(): jnp.einsum('rh,dh->rd', d_pre, w_in, preferred_element_type=F32)  1.32 us
  transfers between devices with their start and end apart: 24, of which 12 were waited for; matrix products, arithmetic and copies ran while one was open for 8% of the time, Pallas kernels for 4%

profile of v4, /device:TPU:0, one launch (start us, length us, event | category | flops | bytes accessed | tf_op | source)
XLA Modules:
  0.0 63.0 jit_solution(10548489297723766243)
XLA Ops:
  1.2 1.1 %forward_rows.1 = (bf16[8,3584]{1,0:T(8,128)(2,1)S(1)}, bf16[8,3584]{1,0:T(8,128)(2,1)S(1)}, bf16[8,3584]{1,0:T(8,128)(2,1)S(1)}, bf16[8,3584]{1,0:T(8,128)(2,1)...) custom-call(bf16[8,3584]{1,0:T(8,128)(2,1)} %inbound_ref.1, f32[1,3584]{1,0:T(1,128)} %scale_ref.1, s32[2,8]{1,0:T(2,128)} %bitcast.19, ...), custom_call_target="tpu_custom_call" | custom-call | tf_op jit(solution)/shard_map/forward_rows/pallas_call | solution.py:96
  2.4 3.1 %collective-permute-start.2 = (bf16[8,3584]{1,0:T(8,128)(2,1)S(1)}, bf16[8,3584]{1,0:T(8,128)(2,1)S(1)}, u32[]{:S(2)}, u32[]{:S(2)}) collective-permute-start(bf16[8,3584]{1,0:T(8,128)(2,1)S(1)} %get-tuple-element.23), channel_id=1, source_target_pairs={{0,8},{1,9},{2,10},{3,11},{4,12},{5,13},{6,14},{7,15},{8,0},{9,1},... | collective-permute-start | bytes 172040 | tf_op jit(solution)/shard_map/forward/ppermute | solution.py:25
  5.5 2.6 %collective-permute-start.3 = (bf16[8,3584]{1,0:T(8,128)(2,1)S(1)}, bf16[8,3584]{1,0:T(8,128)(2,1)S(1)}, u32[]{:S(2)}, u32[]{:S(2)}) collective-permute-start(bf16[8,3584]{1,0:T(8,128)(2,1)S(1)} %get-tuple-element.24), channel_id=1, source_target_pairs={{0,16},{1,17},{2,18},{3,19},{4,20},{5,21},{6,22},{7,23},{8,24},{9,... | collective-permute-start | bytes 172040 | tf_op jit(solution)/shard_map/forward/ppermute | solution.py:25
  8.2 1.1 %backward_rows.1 = (bf16[8,3584]{1,0:T(8,128)(2,1)S(1)}, bf16[8,3584]{1,0:T(8,128)(2,1)S(1)}, bf16[8,3584]{1,0:T(8,128)(2,1)S(1)}, bf16[8,3584]{1,0:T(8,128)(2,1...) custom-call(bf16[8,3584]{1,0:T(8,128)(2,1)} %cotangent_ref.1, s32[2,8]{1,0:T(2,128)} %bitcast.21, ...), custom_call_target="tpu_custom_call" | custom-call | tf_op jit(solution)/shard_map/backward_rows/pallas_call | solution.py:96
  9.3 1.0 %collective-permute-start.13 = (bf16[8,3584]{1,0:T(8,128)(2,1)S(1)}, bf16[8,3584]{1,0:T(8,128)(2,1)S(1)}, u32[]{:S(2)}, u32[]{:S(2)}) collective-permute-start(bf16[8,3584]{1,0:T(8,128)(2,1)S(1)} %get-tuple-element.30), channel_id=1, source_target_pairs={{0,8},{1,9},{2,10},{3,11},{4,12},{5,13},{6,14},{7,15},{8,0},{9,1},... | collective-permute-start | bytes 172040 | tf_op jit(solution)/shard_map/backward/ppermute | solution.py:25
  10.3 3.6 %collective-permute-start.14 = (bf16[8,3584]{1,0:T(8,128)(2,1)S(1)}, bf16[8,3584]{1,0:T(8,128)(2,1)S(1)}, u32[]{:S(2)}, u32[]{:S(2)}) collective-permute-start(bf16[8,3584]{1,0:T(8,128)(2,1)S(1)} %get-tuple-element.31), channel_id=1, source_target_pairs={{0,16},{1,17},{2,18},{3,19},{4,20},{5,21},{6,22},{7,23},{8,24},{9,... | collective-permute-start | bytes 172040 | tf_op jit(solution)/shard_map/backward/ppermute | solution.py:25
  13.8 1.7 %collective-permute-start.15 = (bf16[8,3584]{1,0:T(8,128)(2,1)S(1)}, bf16[8,3584]{1,0:T(8,128)(2,1)S(1)}, u32[]{:S(2)}, u32[]{:S(2)}) collective-permute-start(bf16[8,3584]{1,0:T(8,128)(2,1)S(1)} %get-tuple-element.32), channel_id=1, source_target_pairs={{0,24},{1,25},{2,26},{3,27},{4,28},{5,29},{6,30},{7,31},{8,16},{9,... | collective-permute-start | bytes 172040 | tf_op jit(solution)/shard_map/backward/ppermute | solution.py:25
  15.6 1.6 %collective-permute-start.5 = (bf16[32,3584]{1,0:T(8,128)(2,1)S(1)}, bf16[32,3584]{1,0:T(8,128)(2,1)S(1)}, u32[]{:S(2)}, u32[]{:S(2)}) collective-permute-start(bf16[32,3584]{1,0:T(8,128)(2,1)S(1)} %pad_maximum_fusion.7), channel_id=1, source_target_pairs={{0,2},{1,5},{2,0},{3,7},{4,6},{5,1},{6,4},{7,3},{8,10},{9,13},{10,... | collective-permute-start | bytes 688136 | tf_op jit(solution)/shard_map/forward/ppermute | solution.py:25
  17.6 2.2 %collective-permute-done.15 = bf16[8,3584]{1,0:T(8,128)(2,1)S(1)} collective-permute-done((bf16[8,3584]{1,0:T(8,128)(2,1)S(1)}, bf16[8,3584]{1,0:T(8,128)(2,1)S(1)}, u32[]{:S(2)}, u32[]{:S(2)}) %collective-permute-start.15) | collective-permute-done | bytes 57376 | tf_op jit(solution)/shard_map/backward/ppermute | solution.py:25
  20.0 1.6 %collective-permute-start.16 = (bf16[32,3584]{1,0:T(8,128)(2,1)S(1)}, bf16[32,3584]{1,0:T(8,128)(2,1)S(1)}, u32[]{:S(2)}, u32[]{:S(2)}) collective-permute-start(bf16[32,3584]{1,0:T(8,128)(2,1)S(1)} %pad_maximum_fusion.8), channel_id=1, source_target_pairs={{0,2},{1,5},{2,0},{3,7},{4,6},{5,1},{6,4},{7,3},{8,10},{9,13},{10,... | collective-permute-start | bytes 688136 | tf_op jit(solution)/shard_map/backward/ppermute | solution.py:25
  21.8 1.6 %collective-permute-start.6 = (bf16[64,3584]{1,0:T(8,128)(2,1)S(1)}, bf16[64,3584]{1,0:T(8,128)(2,1)S(1)}, u32[]{:S(2)}, u32[]{:S(2)}) collective-permute-start(bf16[64,3584]{1,0:T(8,128)(2,1)S(1)} %get-tuple-element.54), channel_id=1, source_target_pairs={{0,4},{1,3},{2,6},{3,1},{4,0},{5,7},{6,2},{7,5},{8,12},{9,11},{10,... | collective-permute-start | bytes 1376264 | tf_op jit(solution)/shard_map/forward/ppermute | solution.py:25
  23.4 4.0 %collective-permute-done.16 = bf16[32,3584]{1,0:T(8,128)(2,1)S(1)} collective-permute-done((bf16[32,3584]{1,0:T(8,128)(2,1)S(1)}, bf16[32,3584]{1,0:T(8,128)(2,1)S(1)}, u32[]{:S(2)}, u32[]{:S(2)}) %collective-permute-start.16) | collective-permute-done | bytes 229408 | tf_op jit(solution)/shard_map/backward/ppermute | solution.py:25
  27.4 1.7 %collective-permute-start.17 = (bf16[64,3584]{1,0:T(8,128)(2,1)S(1)}, bf16[64,3584]{1,0:T(8,128)(2,1)S(1)}, u32[]{:S(2)}, u32[]{:S(2)}) collective-permute-start(bf16[64,3584]{1,0:T(8,128)(2,1)S(1)} %pad_maximum_fusion.6), channel_id=1, source_target_pairs={{0,4},{1,3},{2,6},{3,1},{4,0},{5,7},{6,2},{7,5},{8,12},{9,11},{10,... | collective-permute-start | bytes 1376264 | tf_op jit(solution)/shard_map/backward/ppermute | solution.py:25
  29.1 1.3 %collective-permute-done.6 = bf16[64,3584]{1,0:T(8,128)(2,1)S(1)} collective-permute-done((bf16[64,3584]{1,0:T(8,128)(2,1)S(1)}, bf16[64,3584]{1,0:T(8,128)(2,1)S(1)}, u32[]{:S(2)}, u32[]{:S(2)}) %collective-permute-start.6) | collective-permute-done | bytes 458784 | tf_op jit(solution)/shard_map/forward/ppermute | solution.py:25
  32.2 1.6 %collective-permute-start.8 = (bf16[64,3584]{1,0:T(8,128)(2,1)S(1)}, bf16[64,3584]{1,0:T(8,128)(2,1)S(1)}, u32[]{:S(2)}, u32[]{:S(2)}) collective-permute-start(bf16[64,3584]{1,0:T(8,128)(2,1)S(1)} %slice.143), channel_id=1, source_target_pairs={{0,4},{1,3},{2,6},{3,1},{4,0},{5,7},{6,2},{7,5},{8,12},{9,11},{10,... | collective-permute-start | bytes 1376264 | tf_op jit(solution)/shard_map/forward/ppermute | solution.py:25
  33.8 2.2 %collective-permute-done.17 = bf16[64,3584]{1,0:T(8,128)(2,1)S(1)} collective-permute-done((bf16[64,3584]{1,0:T(8,128)(2,1)S(1)}, bf16[64,3584]{1,0:T(8,128)(2,1)S(1)}, u32[]{:S(2)}, u32[]{:S(2)}) %collective-permute-start.17) | collective-permute-done | bytes 458784 | tf_op jit(solution)/shard_map/backward/ppermute | solution.py:25
  36.0 0.7 %fusion.35 = (bf16[128,256]{1,0:T(8,128)(2,1)S(1)}, bf16[128,256]{1,0:T(8,128)(2,1)S(1)}) fusion(f32[128,128]{1,0:T(8,128)S(1)} %get-tuple-element.45, f32[128,128]{1,0:T(8,128)S(1)} %get-tuple-element.42, f32[128,128]{1,0:T(8,128)S(1)} %get-tuple-element.43, f32[128,128]{1,0:T(8,128)S(1)} %get-tuple-element.44, ...), kind=kOutput, calls=%fused_computation.55 | convolution fusion | flops 242712576 | bytes 3145728 | tf_op jit(solution)/shard_map/rd,hd->rh/dot_general | solution.py:225
  36.7 1.3 %fusion.10 = f32[128,3584]{1,0:T(8,128)S(1)} fusion(bf16[3584,128]{1,0:T(8,128)(2,1)S(1)} %collective-permute-done.1, bf16[3584,128]{1,0:T(8,128)(2,1)S(1)} %bitcast.25, bf16[3584,128]{1,0:T(8,128)(2,1)S(1)} %collective-permute-done, bf16[3584,128]{1,0:T(8,128)(2,1)S(1)} %bitcast.28, bf16[128,256]{1,0:T(8,128)(2,1)S(1)} %get-tuple-element.41, ...), kind=kOutput, calls=%fused_computation.18 | convolution fusion | flops 484704256 | bytes 5636096 | tf_op jit(solution)/shard_map/rh,dh->rd/dot_general | solution.py:230
  38.1 1.6 %collective-permute-start.19 = (bf16[64,3584]{1,0:T(8,128)(2,1)S(1)}, bf16[64,3584]{1,0:T(8,128)(2,1)S(1)}, u32[]{:S(2)}, u32[]{:S(2)}) collective-permute-start(bf16[64,3584]{1,0:T(8,128)(2,1)S(1)} %slice.142), channel_id=1, source_target_pairs={{0,2},{1,5},{2,0},{3,7},{4,6},{5,1},{6,4},{7,3},{8,10},{9,13},{10,... | collective-permute-start | bytes 1376264 | tf_op jit(solution)/shard_map/backward/ppermute | solution.py:25
  39.7 1.2 %collective-permute-done.8 = bf16[64,3584]{1,0:T(8,128)(2,1)S(1)} collective-permute-done((bf16[64,3584]{1,0:T(8,128)(2,1)S(1)}, bf16[64,3584]{1,0:T(8,128)(2,1)S(1)}, u32[]{:S(2)}, u32[]{:S(2)}) %collective-permute-start.8) | collective-permute-done | bytes 458784 | tf_op jit(solution)/shard_map/forward/ppermute | solution.py:25
  41.0 1.5 %collective-permute-start.9 = (bf16[32,3584]{1,0:T(8,128)(2,1)S(1)}, bf16[32,3584]{1,0:T(8,128)(2,1)S(1)}, u32[]{:S(2)}, u32[]{:S(2)}) collective-permute-start(bf16[32,3584]{1,0:T(8,128)(2,1)S(1)} %slice.145), channel_id=1, source_target_pairs={{0,2},{1,5},{2,0},{3,7},{4,6},{5,1},{6,4},{7,3},{8,10},{9,13},{10,... | collective-permute-start | bytes 688136 | tf_op jit(solution)/shard_map/forward/ppermute | solution.py:25
  42.5 4.1 %collective-permute-done.19 = bf16[64,3584]{1,0:T(8,128)(2,1)S(1)} collective-permute-done((bf16[64,3584]{1,0:T(8,128)(2,1)S(1)}, bf16[64,3584]{1,0:T(8,128)(2,1)S(1)}, u32[]{:S(2)}, u32[]{:S(2)}) %collective-permute-start.19) | collective-permute-done | bytes 458784 | tf_op jit(solution)/shard_map/backward/ppermute | solution.py:25
  46.8 1.7 %collective-permute-start.20 = (bf16[32,3584]{1,0:T(8,128)(2,1)S(1)}, bf16[32,3584]{1,0:T(8,128)(2,1)S(1)}, u32[]{:S(2)}, u32[]{:S(2)}) collective-permute-start(bf16[32,3584]{1,0:T(8,128)(2,1)S(1)} %slice.144), channel_id=1, source_target_pairs={{0,4},{1,3},{2,6},{3,1},{4,0},{5,7},{6,2},{7,5},{8,12},{9,11},{10,... | collective-permute-start | bytes 688136 | tf_op jit(solution)/shard_map/backward/ppermute | solution.py:25
  48.5 0.9 %collective-permute-done.9 = bf16[32,3584]{1,0:T(8,128)(2,1)S(1)} collective-permute-done((bf16[32,3584]{1,0:T(8,128)(2,1)S(1)}, bf16[32,3584]{1,0:T(8,128)(2,1)S(1)}, u32[]{:S(2)}, u32[]{:S(2)}) %collective-permute-start.9) | collective-permute-done | bytes 229408 | tf_op jit(solution)/shard_map/forward/ppermute | solution.py:25
  49.5 1.9 %collective-permute-start.12 = (bf16[8,3584]{1,0:T(8,128)(2,1)S(1)}, bf16[8,3584]{1,0:T(8,128)(2,1)S(1)}, u32[]{:S(2)}, u32[]{:S(2)}) collective-permute-start(bf16[8,3584]{1,0:T(8,128)(2,1)S(1)} %get-tuple-element.51), channel_id=1, source_target_pairs={{0,24},{1,25},{2,26},{3,27},{4,28},{5,29},{6,30},{7,31},{8,16},{9,... | collective-permute-start | bytes 172040 | tf_op jit(solution)/shard_map/forward/ppermute | solution.py:25
  51.4 2.6 %collective-permute-start.10 = (bf16[8,3584]{1,0:T(8,128)(2,1)S(1)}, bf16[8,3584]{1,0:T(8,128)(2,1)S(1)}, u32[]{:S(2)}, u32[]{:S(2)}) collective-permute-start(bf16[8,3584]{1,0:T(8,128)(2,1)S(1)} %get-tuple-element.53), channel_id=1, source_target_pairs={{0,8},{1,9},{2,10},{3,11},{4,12},{5,13},{6,14},{7,15},{8,0},{9,1},... | collective-permute-start | bytes 172040 | tf_op jit(solution)/shard_map/forward/ppermute | solution.py:25
  54.0 1.9 %collective-permute-start.23 = (bf16[8,3584]{1,0:T(8,128)(2,1)S(1)}, bf16[8,3584]{1,0:T(8,128)(2,1)S(1)}, u32[]{:S(2)}, u32[]{:S(2)}) collective-permute-start(bf16[8,3584]{1,0:T(8,128)(2,1)S(1)} %get-tuple-element.47), channel_id=1, source_target_pairs={{0,24},{1,25},{2,26},{3,27},{4,28},{5,29},{6,30},{7,31},{8,16},{9,... | collective-permute-start | bytes 172040 | tf_op jit(solution)/shard_map/backward/ppermute | solution.py:25
  56.1 2.4 %collective-permute-start.21 = (bf16[8,3584]{1,0:T(8,128)(2,1)S(1)}, bf16[8,3584]{1,0:T(8,128)(2,1)S(1)}, u32[]{:S(2)}, u32[]{:S(2)}) collective-permute-start(bf16[8,3584]{1,0:T(8,128)(2,1)S(1)} %get-tuple-element.49), channel_id=1, source_target_pairs={{0,8},{1,9},{2,10},{3,11},{4,12},{5,13},{6,14},{7,15},{8,0},{9,1},... | collective-permute-start | bytes 172040 | tf_op jit(solution)/shard_map/backward/ppermute | solution.py:25
  58.5 0.7 %collective-permute-done.11 = bf16[8,3584]{1,0:T(8,128)(2,1)S(1)} collective-permute-done((bf16[8,3584]{1,0:T(8,128)(2,1)S(1)}, bf16[8,3584]{1,0:T(8,128)(2,1)S(1)}, u32[]{:S(2)}, u32[]{:S(2)}) %collective-permute-start.11) | collective-permute-done | bytes 57376 | tf_op jit(solution)/shard_map/forward/ppermute | solution.py:25
  59.2 0.9 %fusion = bf16[8,3584]{1,0:T(8,128)(2,1)} fusion(f32[32,8]{1,0:T(8,128)S(1)} %get-tuple-element.19, bf16[8,3584]{1,0:T(8,128)(2,1)S(1)} %collective-permute-done.12, bf16[8,3584]{1,0:T(8,128)(2,1)S(1)} %collective-permute-done.11, bf16[8,3584]{1,0:T(8,128)(2,1)S(1)} %collective-permute-done.10, bf16[8,3584]{1,0:T(8,128)(2,1)S(1)} %get-tuple-element.50, ...), kind=kOutput, calls=%fused_computation.2 | convolution fusion | flops 12013568 | bytes 345088 | tf_op jit(solution)/shard_map/dot_general | solution.py:222
  60.2 1.6 %collective-permute-done.22 = bf16[8,3584]{1,0:T(8,128)(2,1)S(1)} collective-permute-done((bf16[8,3584]{1,0:T(8,128)(2,1)S(1)}, bf16[8,3584]{1,0:T(8,128)(2,1)S(1)}, u32[]{:S(2)}, u32[]{:S(2)}) %collective-permute-start.22) | collective-permute-done | bytes 57376 | tf_op jit(solution)/shard_map/backward/ppermute | solution.py:25
  62.2 0.7 %fusion.43 = bf16[8,3584]{1,0:T(8,128)(2,1)} fusion(bf16[8,3584]{1,0:T(8,128)(2,1)S(1)} %copy-done.4, f32[8,3584]{1,0:T(8,128)S(1)} %get-tuple-element.66, bf16[8,3584]{1,0:T(8,128)(2,1)S(1)} %copy-done.1, f32[8]{0:T(128)S(1)} %broadcast_multiply_fusion, f32[8]{0:T(128)S(1)} %get-tuple-element.65, f32[8]{0:T(128)S(1)} %get-tuple-element.64), kind=kLoop, calls=%fused_computation.67 | loop fusion | flops 229376 | bytes 286816 | tf_op jit(solution)/shard_map/convert_element_type | solution.py:240
  (64 shorter events, 4.5 us)
Async XLA Ops:
  0.6 20.9 %copy-start.2 = (bf16[1,1,32,8,256]{4,3,2,1,0:T(8,128)(2,1)S(1)}, bf16[1,1,32,8,256]{4,3,2,1,0:T(8,128)(2,1)}, u32[]{:S(2)}) copy-start(bf16[1,1,32,8,256]{4,3,2,1,0:T(8,128)(2,1)} %param.23) | copy-start | bytes 393220
  0.6 7.4 %collective-permute-start = (bf16[3584,128]{1,0:T(8,128)(2,1)}, bf16[3584,128]{1,0:T(8,128)(2,1)S(1)}, u32[]{:S(2)}, u32[]{:S(2)}) collective-permute-start(bf16[3584,128]{1,0:T(8,128)(2,1)} %bitcast.26), channel_id=1, source_target_pairs={{0,1},{1,0},{2,3},{3,2},{4,5},{5,4},{6,7},{7,6},{8,9},{9,8},{10,11... | collective-permute-start | bytes 2752520 | tf_op jit(solution)/shard_map/swaps/ppermute | solution.py:25
  1.2 7.0 %collective-permute-start.1 = (bf16[3584,128]{1,0:T(8,128)(2,1)}, bf16[3584,128]{1,0:T(8,128)(2,1)S(1)}, u32[]{:S(2)}, u32[]{:S(2)}) collective-permute-start(bf16[3584,128]{1,0:T(8,128)(2,1)} %bitcast.23), channel_id=1, source_target_pairs={{0,1},{1,0},{2,3},{3,2},{4,5},{5,4},{6,7},{7,6},{8,9},{9,8},{10,11... | collective-permute-start | bytes 2752520 | tf_op jit(solution)/shard_map/swaps/ppermute | solution.py:25
  2.4 7.9 %collective-permute-start.2 = (bf16[8,3584]{1,0:T(8,128)(2,1)S(1)}, bf16[8,3584]{1,0:T(8,128)(2,1)S(1)}, u32[]{:S(2)}, u32[]{:S(2)}) collective-permute-start(bf16[8,3584]{1,0:T(8,128)(2,1)S(1)} %get-tuple-element.23), channel_id=1, source_target_pairs={{0,8},{1,9},{2,10},{3,11},{4,12},{5,13},{6,14},{7,15},{8,0},{9,1},... | collective-permute-start | bytes 172040 | tf_op jit(solution)/shard_map/forward/ppermute | solution.py:25
  5.5 8.4 %collective-permute-start.3 = (bf16[8,3584]{1,0:T(8,128)(2,1)S(1)}, bf16[8,3584]{1,0:T(8,128)(2,1)S(1)}, u32[]{:S(2)}, u32[]{:S(2)}) collective-permute-start(bf16[8,3584]{1,0:T(8,128)(2,1)S(1)} %get-tuple-element.24), channel_id=1, source_target_pairs={{0,16},{1,17},{2,18},{3,19},{4,20},{5,21},{6,22},{7,23},{8,24},{9,... | collective-permute-start | bytes 172040 | tf_op jit(solution)/shard_map/forward/ppermute | solution.py:25
  8.1 7.5 %collective-permute-start.4 = (bf16[8,3584]{1,0:T(8,128)(2,1)S(1)}, bf16[8,3584]{1,0:T(8,128)(2,1)S(1)}, u32[]{:S(2)}, u32[]{:S(2)}) collective-permute-start(bf16[8,3584]{1,0:T(8,128)(2,1)S(1)} %get-tuple-element.25), channel_id=1, source_target_pairs={{0,24},{1,25},{2,26},{3,27},{4,28},{5,29},{6,30},{7,31},{8,16},{9,... | collective-permute-start | bytes 172040 | tf_op jit(solution)/shard_map/forward/ppermute | solution.py:25
  8.1 23.1 %collective-permute-start.7 = (bf16[128,3584]{1,0:T(8,128)(2,1)}, bf16[128,3584]{1,0:T(8,128)(2,1)S(1)}, u32[]{:S(2)}, u32[]{:S(2)}) collective-permute-start(bf16[128,3584]{1,0:T(8,128)(2,1)} %bitcast.13), channel_id=1, source_target_pairs={{0,1},{1,0},{2,3},{3,2},{4,5},{5,4},{6,7},{7,6},{8,9},{9,8},{10,11... | collective-permute-start | bytes 2752520 | tf_op jit(solution)/shard_map/swaps/ppermute | solution.py:25
  9.3 7.8 %collective-permute-start.13 = (bf16[8,3584]{1,0:T(8,128)(2,1)S(1)}, bf16[8,3584]{1,0:T(8,128)(2,1)S(1)}, u32[]{:S(2)}, u32[]{:S(2)}) collective-permute-start(bf16[8,3584]{1,0:T(8,128)(2,1)S(1)} %get-tuple-element.30), channel_id=1, source_target_pairs={{0,8},{1,9},{2,10},{3,11},{4,12},{5,13},{6,14},{7,15},{8,0},{9,1},... | collective-permute-start | bytes 172040 | tf_op jit(solution)/shard_map/backward/ppermute | solution.py:25
  10.3 7.3 %collective-permute-start.14 = (bf16[8,3584]{1,0:T(8,128)(2,1)S(1)}, bf16[8,3584]{1,0:T(8,128)(2,1)S(1)}, u32[]{:S(2)}, u32[]{:S(2)}) collective-permute-start(bf16[8,3584]{1,0:T(8,128)(2,1)S(1)} %get-tuple-element.31), channel_id=1, source_target_pairs={{0,16},{1,17},{2,18},{3,19},{4,20},{5,21},{6,22},{7,23},{8,24},{9,... | collective-permute-start | bytes 172040 | tf_op jit(solution)/shard_map/backward/ppermute | solution.py:25
  13.8 6.0 %collective-permute-start.15 = (bf16[8,3584]{1,0:T(8,128)(2,1)S(1)}, bf16[8,3584]{1,0:T(8,128)(2,1)S(1)}, u32[]{:S(2)}, u32[]{:S(2)}) collective-permute-start(bf16[8,3584]{1,0:T(8,128)(2,1)S(1)} %get-tuple-element.32), channel_id=1, source_target_pairs={{0,24},{1,25},{2,26},{3,27},{4,28},{5,29},{6,30},{7,31},{8,16},{9,... | collective-permute-start | bytes 172040 | tf_op jit(solution)/shard_map/backward/ppermute | solution.py:25
  15.6 6.2 %collective-permute-start.5 = (bf16[32,3584]{1,0:T(8,128)(2,1)S(1)}, bf16[32,3584]{1,0:T(8,128)(2,1)S(1)}, u32[]{:S(2)}, u32[]{:S(2)}) collective-permute-start(bf16[32,3584]{1,0:T(8,128)(2,1)S(1)} %pad_maximum_fusion.7), channel_id=1, source_target_pairs={{0,2},{1,5},{2,0},{3,7},{4,6},{5,1},{6,4},{7,3},{8,10},{9,13},{10,... | collective-permute-start | bytes 688136 | tf_op jit(solution)/shard_map/forward/ppermute | solution.py:25
  19.8 1.7 %collective-permute-start.18 = (bf16[32,8,256]{2,1,0:T(8,128)(2,1)}, bf16[32,8,256]{2,1,0:T(8,128)(2,1)S(1)}, u32[]{:S(2)}, u32[]{:S(2)}) collective-permute-start(bf16[32,8,256]{2,1,0:T(8,128)(2,1)} %bitcast.16), channel_id=1, source_target_pairs={{0,1},{1,0},{2,3},{3,2},{4,5},{5,4},{6,7},{7,6},{8,9},{9,8},{10,11... | collective-permute-start | bytes 393224 | tf_op jit(solution)/shard_map/backward/swaps/ppermute | solution.py:25
  19.9 10.6 %copy-start.5 = (bf16[1,1,3584,128]{3,2,1,0:T(8,128)(2,1)S(1)}, bf16[1,1,3584,128]{3,2,1,0:T(8,128)(2,1)}, u32[]{:S(2)}) copy-start(bf16[1,1,3584,128]{3,2,1,0:T(8,128)(2,1)} %param.21) | copy-start | bytes 2752516
  19.9 10.6 %copy-start.6 = (bf16[1,1,3584,128]{3,2,1,0:T(8,128)(2,1)S(1)}, bf16[1,1,3584,128]{3,2,1,0:T(8,128)(2,1)}, u32[]{:S(2)}) copy-start(bf16[1,1,3584,128]{3,2,1,0:T(8,128)(2,1)} %param.20) | copy-start | bytes 2752516
  20.0 7.4 %collective-permute-start.16 = (bf16[32,3584]{1,0:T(8,128)(2,1)S(1)}, bf16[32,3584]{1,0:T(8,128)(2,1)S(1)}, u32[]{:S(2)}, u32[]{:S(2)}) collective-permute-start(bf16[32,3584]{1,0:T(8,128)(2,1)S(1)} %pad_maximum_fusion.8), channel_id=1, source_target_pairs={{0,2},{1,5},{2,0},{3,7},{4,6},{5,1},{6,4},{7,3},{8,10},{9,13},{10,... | collective-permute-start | bytes 688136 | tf_op jit(solution)/shard_map/backward/ppermute | solution.py:25
  21.8 8.6 %collective-permute-start.6 = (bf16[64,3584]{1,0:T(8,128)(2,1)S(1)}, bf16[64,3584]{1,0:T(8,128)(2,1)S(1)}, u32[]{:S(2)}, u32[]{:S(2)}) collective-permute-start(bf16[64,3584]{1,0:T(8,128)(2,1)S(1)} %get-tuple-element.54), channel_id=1, source_target_pairs={{0,4},{1,3},{2,6},{3,1},{4,0},{5,7},{6,2},{7,5},{8,12},{9,11},{10,... | collective-permute-start | bytes 1376264 | tf_op jit(solution)/shard_map/forward/ppermute | solution.py:25
  27.4 8.5 %collective-permute-start.17 = (bf16[64,3584]{1,0:T(8,128)(2,1)S(1)}, bf16[64,3584]{1,0:T(8,128)(2,1)S(1)}, u32[]{:S(2)}, u32[]{:S(2)}) collective-permute-start(bf16[64,3584]{1,0:T(8,128)(2,1)S(1)} %pad_maximum_fusion.6), channel_id=1, source_target_pairs={{0,4},{1,3},{2,6},{3,1},{4,0},{5,7},{6,2},{7,5},{8,12},{9,11},{10,... | collective-permute-start | bytes 1376264 | tf_op jit(solution)/shard_map/backward/ppermute | solution.py:25
  30.5 1.2 %copy-start = (bf16[1,1,128,3584]{3,2,1,0:T(8,128)(2,1)S(1)}, bf16[1,1,128,3584]{3,2,1,0:T(8,128)(2,1)}, u32[]{:S(2)}) copy-start(bf16[1,1,128,3584]{3,2,1,0:T(8,128)(2,1)} %param.22) | copy-start | bytes 2752516
  32.2 8.7 %collective-permute-start.8 = (bf16[64,3584]{1,0:T(8,128)(2,1)S(1)}, bf16[64,3584]{1,0:T(8,128)(2,1)S(1)}, u32[]{:S(2)}, u32[]{:S(2)}) collective-permute-start(bf16[64,3584]{1,0:T(8,128)(2,1)S(1)} %slice.143), channel_id=1, source_target_pairs={{0,4},{1,3},{2,6},{3,1},{4,0},{5,7},{6,2},{7,5},{8,12},{9,11},{10,... | collective-permute-start | bytes 1376264 | tf_op jit(solution)/shard_map/forward/ppermute | solution.py:25
  38.1 8.5 %collective-permute-start.19 = (bf16[64,3584]{1,0:T(8,128)(2,1)S(1)}, bf16[64,3584]{1,0:T(8,128)(2,1)S(1)}, u32[]{:S(2)}, u32[]{:S(2)}) collective-permute-start(bf16[64,3584]{1,0:T(8,128)(2,1)S(1)} %slice.142), channel_id=1, source_target_pairs={{0,2},{1,5},{2,0},{3,7},{4,6},{5,1},{6,4},{7,3},{8,10},{9,13},{10,... | collective-permute-start | bytes 1376264 | tf_op jit(solution)/shard_map/backward/ppermute | solution.py:25
  41.0 8.4 %collective-permute-start.9 = (bf16[32,3584]{1,0:T(8,128)(2,1)S(1)}, bf16[32,3584]{1,0:T(8,128)(2,1)S(1)}, u32[]{:S(2)}, u32[]{:S(2)}) collective-permute-start(bf16[32,3584]{1,0:T(8,128)(2,1)S(1)} %slice.145), channel_id=1, source_target_pairs={{0,2},{1,5},{2,0},{3,7},{4,6},{5,1},{6,4},{7,3},{8,10},{9,13},{10,... | collective-permute-start | bytes 688136 | tf_op jit(solution)/shard_map/forward/ppermute | solution.py:25
  46.7 12.4 %copy-start.3 = (bf16[8,3584]{1,0:T(8,128)(2,1)S(1)}, bf16[8,3584]{1,0:T(8,128)(2,1)}, u32[]{:S(2)}) copy-start(bf16[8,3584]{1,0:T(8,128)(2,1)} %inbound_ref.1) | copy-start | bytes 172036
  46.8 15.0 %copy-start.4 = (bf16[8,3584]{1,0:T(8,128)(2,1)S(1)}, bf16[8,3584]{1,0:T(8,128)(2,1)}, u32[]{:S(2)}) copy-start(bf16[8,3584]{1,0:T(8,128)(2,1)} %param.14) | copy-start | bytes 172036
  46.8 7.2 %collective-permute-start.20 = (bf16[32,3584]{1,0:T(8,128)(2,1)S(1)}, bf16[32,3584]{1,0:T(8,128)(2,1)S(1)}, u32[]{:S(2)}, u32[]{:S(2)}) collective-permute-start(bf16[32,3584]{1,0:T(8,128)(2,1)S(1)} %slice.144), channel_id=1, source_target_pairs={{0,4},{1,3},{2,6},{3,1},{4,0},{5,7},{6,2},{7,5},{8,12},{9,11},{10,... | collective-permute-start | bytes 688136 | tf_op jit(solution)/shard_map/backward/ppermute | solution.py:25
  49.5 12.8 %copy-start.1 = (bf16[8,3584]{1,0:T(8,128)(2,1)S(1)}, bf16[8,3584]{1,0:T(8,128)(2,1)}, u32[]{:S(2)}) copy-start(bf16[8,3584]{1,0:T(8,128)(2,1)} %cotangent_ref.1) | copy-start | bytes 172036
  49.5 6.6 %collective-permute-start.12 = (bf16[8,3584]{1,0:T(8,128)(2,1)S(1)}, bf16[8,3584]{1,0:T(8,128)(2,1)S(1)}, u32[]{:S(2)}, u32[]{:S(2)}) collective-permute-start(bf16[8,3584]{1,0:T(8,128)(2,1)S(1)} %get-tuple-element.51), channel_id=1, source_target_pairs={{0,24},{1,25},{2,26},{3,27},{4,28},{5,29},{6,30},{7,31},{8,16},{9,... | collective-permute-start | bytes 172040 | tf_op jit(solution)/shard_map/forward/ppermute | solution.py:25
  51.4 7.8 %collective-permute-start.11 = (bf16[8,3584]{1,0:T(8,128)(2,1)S(1)}, bf16[8,3584]{1,0:T(8,128)(2,1)S(1)}, u32[]{:S(2)}, u32[]{:S(2)}) collective-permute-start(bf16[8,3584]{1,0:T(8,128)(2,1)S(1)} %get-tuple-element.52), channel_id=1, source_target_pairs={{0,16},{1,17},{2,18},{3,19},{4,20},{5,21},{6,22},{7,23},{8,24},{9,... | collective-permute-start | bytes 172040 | tf_op jit(solution)/shard_map/forward/ppermute | solution.py:25
  51.4 7.8 %collective-permute-start.10 = (bf16[8,3584]{1,0:T(8,128)(2,1)S(1)}, bf16[8,3584]{1,0:T(8,128)(2,1)S(1)}, u32[]{:S(2)}, u32[]{:S(2)}) collective-permute-start(bf16[8,3584]{1,0:T(8,128)(2,1)S(1)} %get-tuple-element.53), channel_id=1, source_target_pairs={{0,8},{1,9},{2,10},{3,11},{4,12},{5,13},{6,14},{7,15},{8,0},{9,1},... | collective-permute-start | bytes 172040 | tf_op jit(solution)/shard_map/forward/ppermute | solution.py:25
  54.0 6.2 %collective-permute-start.23 = (bf16[8,3584]{1,0:T(8,128)(2,1)S(1)}, bf16[8,3584]{1,0:T(8,128)(2,1)S(1)}, u32[]{:S(2)}, u32[]{:S(2)}) collective-permute-start(bf16[8,3584]{1,0:T(8,128)(2,1)S(1)} %get-tuple-element.47), channel_id=1, source_target_pairs={{0,24},{1,25},{2,26},{3,27},{4,28},{5,29},{6,30},{7,31},{8,16},{9,... | collective-permute-start | bytes 172040 | tf_op jit(solution)/shard_map/backward/ppermute | solution.py:25
  55.9 5.9 %collective-permute-start.22 = (bf16[8,3584]{1,0:T(8,128)(2,1)S(1)}, bf16[8,3584]{1,0:T(8,128)(2,1)S(1)}, u32[]{:S(2)}, u32[]{:S(2)}) collective-permute-start(bf16[8,3584]{1,0:T(8,128)(2,1)S(1)} %get-tuple-element.48), channel_id=1, source_target_pairs={{0,16},{1,17},{2,18},{3,19},{4,20},{5,21},{6,22},{7,23},{8,24},{9,... | collective-permute-start | bytes 172040 | tf_op jit(solution)/shard_map/backward/ppermute | solution.py:25
  56.1 5.7 %collective-permute-start.21 = (bf16[8,3584]{1,0:T(8,128)(2,1)S(1)}, bf16[8,3584]{1,0:T(8,128)(2,1)S(1)}, u32[]{:S(2)}, u32[]{:S(2)}) collective-permute-start(bf16[8,3584]{1,0:T(8,128)(2,1)S(1)} %get-tuple-element.49), channel_id=1, source_target_pairs={{0,8},{1,9},{2,10},{3,11},{4,12},{5,13},{6,14},{7,15},{8,0},{9,1},... | collective-permute-start | bytes 172040 | tf_op jit(solution)/shard_map/backward/ppermute | solution.py:25

commit v5 on v4

--- a/solution.py
+++ b/solution.py
@@ -174,8 +174,8 @@
     )
     with jax.named_scope("forward"):
         arrived = along_groups(chunks)
-    routes_back, gate_other, up_other = lax.optimization_barrier(
-        (routes_back, gate_other, up_other)
+    routes_back, gate_other, up_other, down_other = lax.optimization_barrier(
+        (routes_back, gate_other, up_other, down_other)
     )
     chunks, occupied_back, own_chunk = slot_rows(
         backward_rows_kernel,

time: 63.2 us -> 63 us (level)
  starting transfers between devices: 34.2 us -> 32.4 us
  waiting for transfers between devices: 18.9 us -> 20.5 us
    ppermute x24, starting transfers between devices: 34.2 us -> 32.4 us  [swap(): lax.ppermute(value, 'expert', [(i, i ^ mask_of(i)) for i in range(size)])]
    ppermute x24, waiting for transfers between devices: 18.9 us -> 20.5 us  [swap(): lax.ppermute(value, 'expert', [(i, i ^ mask_of(i)) for i in range(size)])]
  transfers between devices with their start and end apart: 24 -> 24, of which waited for: 12 -> 13; matrix products, arithmetic and copies ran while one was open for 8% -> 8% of each run, Pallas kernels for 4% -> 4%
where the time goes in v5:
time: 63 us; the launch traced here: 62.7 us
  starting transfers between devices  32.4 us (51%)
  waiting for transfers between devices  20.5 us (33%)
  matrix products  4.63 us (7%)
  Pallas kernels  2.27 us (4%)
  other arithmetic  1.11 us (2%)
  between operations  0.94 us (1%)
  local copies, waits for them, and re-layouts  0.89 us (1%)
    ppermute x24, starting transfers between devices, swap(): lax.ppermute(value, 'expert', [(i, i ^ mask_of(i)) for i in range(size)])  32.4 us
    ppermute x24, waiting for transfers between devices, swap(): lax.ppermute(value, 'expert', [(i, i ^ mask_of(i)) for i in range(size)])  20.5 us
    pallas_call x2, Pallas kernels, slot_rows(): pl.pallas_call(functools.partial(kernel, groups, capacity), out_shape=(ch...  2.27 us
    dot_general x1, matrix products, body(): jnp.einsum('rh,dh->rd', d_pre, w_in, preferred_element_type=F32)  1.33 us
  transfers between devices with their start and end apart: 24, of which 13 were waited for; matrix products, arithmetic and copies ran while one was open for 8% of the time, Pallas kernels for 4%

profile of v5, /device:TPU:0, one launch (start us, length us, event | category | flops | bytes accessed | tf_op | source)
XLA Modules:
  0.0 62.7 jit_solution(10830739610950937642)
XLA Ops:
  1.7 1.1 %forward_rows.1 = (bf16[8,3584]{1,0:T(8,128)(2,1)S(1)}, bf16[8,3584]{1,0:T(8,128)(2,1)S(1)}, bf16[8,3584]{1,0:T(8,128)(2,1)S(1)}, bf16[8,3584]{1,0:T(8,128)(2,1)...) custom-call(bf16[8,3584]{1,0:T(8,128)(2,1)} %inbound_ref.1, f32[1,3584]{1,0:T(1,128)} %scale_ref.1, s32[2,8]{1,0:T(2,128)} %bitcast.19, ...), custom_call_target="tpu_custom_call" | custom-call | tf_op jit(solution)/shard_map/forward_rows/pallas_call | solution.py:96
  2.8 2.7 %collective-permute-start.3 = (bf16[8,3584]{1,0:T(8,128)(2,1)S(1)}, bf16[8,3584]{1,0:T(8,128)(2,1)S(1)}, u32[]{:S(2)}, u32[]{:S(2)}) collective-permute-start(bf16[8,3584]{1,0:T(8,128)(2,1)S(1)} %get-tuple-element.24), channel_id=1, source_target_pairs={{0,8},{1,9},{2,10},{3,11},{4,12},{5,13},{6,14},{7,15},{8,0},{9,1},... | collective-permute-start | bytes 172040 | tf_op jit(solution)/shard_map/forward/ppermute | solution.py:25
  5.5 2.6 %collective-permute-start.4 = (bf16[8,3584]{1,0:T(8,128)(2,1)S(1)}, bf16[8,3584]{1,0:T(8,128)(2,1)S(1)}, u32[]{:S(2)}, u32[]{:S(2)}) collective-permute-start(bf16[8,3584]{1,0:T(8,128)(2,1)S(1)} %get-tuple-element.25), channel_id=1, source_target_pairs={{0,16},{1,17},{2,18},{3,19},{4,20},{5,21},{6,22},{7,23},{8,24},{9,... | collective-permute-start | bytes 172040 | tf_op jit(solution)/shard_map/forward/ppermute | solution.py:25
  8.4 1.1 %backward_rows.1 = (bf16[8,3584]{1,0:T(8,128)(2,1)S(1)}, bf16[8,3584]{1,0:T(8,128)(2,1)S(1)}, bf16[8,3584]{1,0:T(8,128)(2,1)S(1)}, bf16[8,3584]{1,0:T(8,128)(2,1...) custom-call(bf16[8,3584]{1,0:T(8,128)(2,1)} %cotangent_ref.1, s32[2,8]{1,0:T(2,128)} %bitcast.21, ...), custom_call_target="tpu_custom_call" | custom-call | tf_op jit(solution)/shard_map/backward_rows/pallas_call | solution.py:96
  9.6 0.7 %collective-permute-start.13 = (bf16[8,3584]{1,0:T(8,128)(2,1)S(1)}, bf16[8,3584]{1,0:T(8,128)(2,1)S(1)}, u32[]{:S(2)}, u32[]{:S(2)}) collective-permute-start(bf16[8,3584]{1,0:T(8,128)(2,1)S(1)} %get-tuple-element.32), channel_id=1, source_target_pairs={{0,8},{1,9},{2,10},{3,11},{4,12},{5,13},{6,14},{7,15},{8,0},{9,1},... | collective-permute-start | bytes 172040 | tf_op jit(solution)/shard_map/backward/ppermute | solution.py:25
  10.3 3.5 %collective-permute-start.14 = (bf16[8,3584]{1,0:T(8,128)(2,1)S(1)}, bf16[8,3584]{1,0:T(8,128)(2,1)S(1)}, u32[]{:S(2)}, u32[]{:S(2)}) collective-permute-start(bf16[8,3584]{1,0:T(8,128)(2,1)S(1)} %get-tuple-element.33), channel_id=1, source_target_pairs={{0,16},{1,17},{2,18},{3,19},{4,20},{5,21},{6,22},{7,23},{8,24},{9,... | collective-permute-start | bytes 172040 | tf_op jit(solution)/shard_map/backward/ppermute | solution.py:25
  14.8 1.6 %collective-permute-start.6 = (bf16[32,3584]{1,0:T(8,128)(2,1)S(1)}, bf16[32,3584]{1,0:T(8,128)(2,1)S(1)}, u32[]{:S(2)}, u32[]{:S(2)}) collective-permute-start(bf16[32,3584]{1,0:T(8,128)(2,1)S(1)} %pad_maximum_fusion.7), channel_id=1, source_target_pairs={{0,2},{1,5},{2,0},{3,7},{4,6},{5,1},{6,4},{7,3},{8,10},{9,13},{10,... | collective-permute-start | bytes 688136 | tf_op jit(solution)/shard_map/forward/ppermute | solution.py:25
  16.4 1.8 %collective-permute-done.14 = bf16[8,3584]{1,0:T(8,128)(2,1)S(1)} collective-permute-done((bf16[8,3584]{1,0:T(8,128)(2,1)S(1)}, bf16[8,3584]{1,0:T(8,128)(2,1)S(1)}, u32[]{:S(2)}, u32[]{:S(2)}) %collective-permute-start.14) | collective-permute-done | bytes 57376 | tf_op jit(solution)/shard_map/backward/ppermute | solution.py:25
  18.1 1.7 %collective-permute-done.15 = bf16[8,3584]{1,0:T(8,128)(2,1)S(1)} collective-permute-done((bf16[8,3584]{1,0:T(8,128)(2,1)S(1)}, bf16[8,3584]{1,0:T(8,128)(2,1)S(1)}, u32[]{:S(2)}, u32[]{:S(2)}) %collective-permute-start.15) | collective-permute-done | bytes 57376 | tf_op jit(solution)/shard_map/backward/ppermute | solution.py:25
  20.0 1.5 %collective-permute-start.16 = (bf16[32,3584]{1,0:T(8,128)(2,1)S(1)}, bf16[32,3584]{1,0:T(8,128)(2,1)S(1)}, u32[]{:S(2)}, u32[]{:S(2)}) collective-permute-start(bf16[32,3584]{1,0:T(8,128)(2,1)S(1)} %pad_maximum_fusion.8), channel_id=1, source_target_pairs={{0,2},{1,5},{2,0},{3,7},{4,6},{5,1},{6,4},{7,3},{8,10},{9,13},{10,... | collective-permute-start | bytes 688136 | tf_op jit(solution)/shard_map/backward/ppermute | solution.py:25
  21.9 1.6 %collective-permute-start.7 = (bf16[64,3584]{1,0:T(8,128)(2,1)S(1)}, bf16[64,3584]{1,0:T(8,128)(2,1)S(1)}, u32[]{:S(2)}, u32[]{:S(2)}) collective-permute-start(bf16[64,3584]{1,0:T(8,128)(2,1)S(1)} %get-tuple-element.56), channel_id=1, source_target_pairs={{0,4},{1,3},{2,6},{3,1},{4,0},{5,7},{6,2},{7,5},{8,12},{9,11},{10,... | collective-permute-start | bytes 1376264 | tf_op jit(solution)/shard_map/forward/ppermute | solution.py:25
  23.5 4.0 %collective-permute-done.16 = bf16[32,3584]{1,0:T(8,128)(2,1)S(1)} collective-permute-done((bf16[32,3584]{1,0:T(8,128)(2,1)S(1)}, bf16[32,3584]{1,0:T(8,128)(2,1)S(1)}, u32[]{:S(2)}, u32[]{:S(2)}) %collective-permute-start.16) | collective-permute-done | bytes 229408 | tf_op jit(solution)/shard_map/backward/ppermute | solution.py:25
  27.5 1.7 %collective-permute-start.17 = (bf16[64,3584]{1,0:T(8,128)(2,1)S(1)}, bf16[64,3584]{1,0:T(8,128)(2,1)S(1)}, u32[]{:S(2)}, u32[]{:S(2)}) collective-permute-start(bf16[64,3584]{1,0:T(8,128)(2,1)S(1)} %pad_maximum_fusion.6), channel_id=1, source_target_pairs={{0,4},{1,3},{2,6},{3,1},{4,0},{5,7},{6,2},{7,5},{8,12},{9,11},{10,... | collective-permute-start | bytes 1376264 | tf_op jit(solution)/shard_map/backward/ppermute | solution.py:25
  29.2 1.3 %collective-permute-done.7 = bf16[64,3584]{1,0:T(8,128)(2,1)S(1)} collective-permute-done((bf16[64,3584]{1,0:T(8,128)(2,1)S(1)}, bf16[64,3584]{1,0:T(8,128)(2,1)S(1)}, u32[]{:S(2)}, u32[]{:S(2)}) %collective-permute-start.7) | collective-permute-done | bytes 458784 | tf_op jit(solution)/shard_map/forward/ppermute | solution.py:25
  30.6 0.6 %fusion.11 = f32[128,512]{1,0:T(8,128)S(1)} fusion(bf16[128,3584]{1,0:T(8,128)(2,1)S(1)} %constant_dynamic-update-slice_fusion.5, bf16[3584,128]{1,0:T(8,128)(2,1)S(1)} %collective-permute-done.1, bf16[3584,128]{1,0:T(8,128)(2,1)S(1)} %bitcast.24, bf16[3584,128]{1,0:T(8,128)(2,1)S(1)} %collective-permute-done, bf16[3584,128]{1,0:T(8,128)(2,1)S(1)} %bitcast.27), kind=kOutput, calls=%fused_computation.19 | convolution fusion | flops 484442112 | bytes 4849664 | tf_op jit(solution)/shard_map/dot_general | solution.py:217
  32.2 1.6 %collective-permute-start.8 = (bf16[64,3584]{1,0:T(8,128)(2,1)S(1)}, bf16[64,3584]{1,0:T(8,128)(2,1)S(1)}, u32[]{:S(2)}, u32[]{:S(2)}) collective-permute-start(bf16[64,3584]{1,0:T(8,128)(2,1)S(1)} %slice.143), channel_id=1, source_target_pairs={{0,4},{1,3},{2,6},{3,1},{4,0},{5,7},{6,2},{7,5},{8,12},{9,11},{10,... | collective-permute-start | bytes 1376264 | tf_op jit(solution)/shard_map/forward/ppermute | solution.py:25
  33.8 2.2 %collective-permute-done.17 = bf16[64,3584]{1,0:T(8,128)(2,1)S(1)} collective-permute-done((bf16[64,3584]{1,0:T(8,128)(2,1)S(1)}, bf16[64,3584]{1,0:T(8,128)(2,1)S(1)}, u32[]{:S(2)}, u32[]{:S(2)}) %collective-permute-start.17) | collective-permute-done | bytes 458784 | tf_op jit(solution)/shard_map/backward/ppermute | solution.py:25
  36.1 0.7 %fusion.35 = (bf16[128,256]{1,0:T(8,128)(2,1)S(1)}, bf16[128,256]{1,0:T(8,128)(2,1)S(1)}) fusion(f32[128,128]{1,0:T(8,128)S(1)} %get-tuple-element.47, f32[128,128]{1,0:T(8,128)S(1)} %get-tuple-element.44, f32[128,128]{1,0:T(8,128)S(1)} %get-tuple-element.45, f32[128,128]{1,0:T(8,128)S(1)} %get-tuple-element.46, ...), kind=kOutput, calls=%fused_computation.55 | convolution fusion | flops 242712576 | bytes 3145728 | tf_op jit(solution)/shard_map/rd,hd->rh/dot_general | solution.py:225
  36.8 1.3 %fusion.10 = f32[128,3584]{1,0:T(8,128)S(1)} fusion(bf16[3584,128]{1,0:T(8,128)(2,1)S(1)} %collective-permute-done.1, bf16[3584,128]{1,0:T(8,128)(2,1)S(1)} %bitcast.25, bf16[3584,128]{1,0:T(8,128)(2,1)S(1)} %collective-permute-done, bf16[3584,128]{1,0:T(8,128)(2,1)S(1)} %bitcast.28, bf16[128,256]{1,0:T(8,128)(2,1)S(1)} %get-tuple-element.43, ...), kind=kOutput, calls=%fused_computation.18 | convolution fusion | flops 484704256 | bytes 5636096 | tf_op jit(solution)/shard_map/rh,dh->rd/dot_general | solution.py:230
  38.2 1.5 %collective-permute-start.19 = (bf16[64,3584]{1,0:T(8,128)(2,1)S(1)}, bf16[64,3584]{1,0:T(8,128)(2,1)S(1)}, u32[]{:S(2)}, u32[]{:S(2)}) collective-permute-start(bf16[64,3584]{1,0:T(8,128)(2,1)S(1)} %slice.142), channel_id=1, source_target_pairs={{0,2},{1,5},{2,0},{3,7},{4,6},{5,1},{6,4},{7,3},{8,10},{9,13},{10,... | collective-permute-start | bytes 1376264 | tf_op jit(solution)/shard_map/backward/ppermute | solution.py:25
  39.7 1.3 %collective-permute-done.8 = bf16[64,3584]{1,0:T(8,128)(2,1)S(1)} collective-permute-done((bf16[64,3584]{1,0:T(8,128)(2,1)S(1)}, bf16[64,3584]{1,0:T(8,128)(2,1)S(1)}, u32[]{:S(2)}, u32[]{:S(2)}) %collective-permute-start.8) | collective-permute-done | bytes 458784 | tf_op jit(solution)/shard_map/forward/ppermute | solution.py:25
  41.1 1.5 %collective-permute-start.9 = (bf16[32,3584]{1,0:T(8,128)(2,1)S(1)}, bf16[32,3584]{1,0:T(8,128)(2,1)S(1)}, u32[]{:S(2)}, u32[]{:S(2)}) collective-permute-start(bf16[32,3584]{1,0:T(8,128)(2,1)S(1)} %slice.145), channel_id=1, source_target_pairs={{0,2},{1,5},{2,0},{3,7},{4,6},{5,1},{6,4},{7,3},{8,10},{9,13},{10,... | collective-permute-start | bytes 688136 | tf_op jit(solution)/shard_map/forward/ppermute | solution.py:25
  42.6 4.1 %collective-permute-done.19 = bf16[64,3584]{1,0:T(8,128)(2,1)S(1)} collective-permute-done((bf16[64,3584]{1,0:T(8,128)(2,1)S(1)}, bf16[64,3584]{1,0:T(8,128)(2,1)S(1)}, u32[]{:S(2)}, u32[]{:S(2)}) %collective-permute-start.19) | collective-permute-done | bytes 458784 | tf_op jit(solution)/shard_map/backward/ppermute | solution.py:25
  46.9 1.7 %collective-permute-start.20 = (bf16[32,3584]{1,0:T(8,128)(2,1)S(1)}, bf16[32,3584]{1,0:T(8,128)(2,1)S(1)}, u32[]{:S(2)}, u32[]{:S(2)}) collective-permute-start(bf16[32,3584]{1,0:T(8,128)(2,1)S(1)} %slice.144), channel_id=1, source_target_pairs={{0,4},{1,3},{2,6},{3,1},{4,0},{5,7},{6,2},{7,5},{8,12},{9,11},{10,... | collective-permute-start | bytes 688136 | tf_op jit(solution)/shard_map/backward/ppermute | solution.py:25
  48.6 0.9 %collective-permute-done.9 = bf16[32,3584]{1,0:T(8,128)(2,1)S(1)} collective-permute-done((bf16[32,3584]{1,0:T(8,128)(2,1)S(1)}, bf16[32,3584]{1,0:T(8,128)(2,1)S(1)}, u32[]{:S(2)}, u32[]{:S(2)}) %collective-permute-start.9) | collective-permute-done | bytes 229408 | tf_op jit(solution)/shard_map/forward/ppermute | solution.py:25
  49.6 1.1 %collective-permute-start.12 = (bf16[8,3584]{1,0:T(8,128)(2,1)S(1)}, bf16[8,3584]{1,0:T(8,128)(2,1)S(1)}, u32[]{:S(2)}, u32[]{:S(2)}) collective-permute-start(bf16[8,3584]{1,0:T(8,128)(2,1)S(1)} %get-tuple-element.53), channel_id=1, source_target_pairs={{0,24},{1,25},{2,26},{3,27},{4,28},{5,29},{6,30},{7,31},{8,16},{9,... | collective-permute-start | bytes 172040 | tf_op jit(solution)/shard_map/forward/ppermute | solution.py:25
  50.7 3.4 %collective-permute-start.10 = (bf16[8,3584]{1,0:T(8,128)(2,1)S(1)}, bf16[8,3584]{1,0:T(8,128)(2,1)S(1)}, u32[]{:S(2)}, u32[]{:S(2)}) collective-permute-start(bf16[8,3584]{1,0:T(8,128)(2,1)S(1)} %get-tuple-element.55), channel_id=1, source_target_pairs={{0,8},{1,9},{2,10},{3,11},{4,12},{5,13},{6,14},{7,15},{8,0},{9,1},... | collective-permute-start | bytes 172040 | tf_op jit(solution)/shard_map/forward/ppermute | solution.py:25
  54.1 1.1 %collective-permute-start.23 = (bf16[8,3584]{1,0:T(8,128)(2,1)S(1)}, bf16[8,3584]{1,0:T(8,128)(2,1)S(1)}, u32[]{:S(2)}, u32[]{:S(2)}) collective-permute-start(bf16[8,3584]{1,0:T(8,128)(2,1)S(1)} %get-tuple-element.49), channel_id=1, source_target_pairs={{0,24},{1,25},{2,26},{3,27},{4,28},{5,29},{6,30},{7,31},{8,16},{9,... | collective-permute-start | bytes 172040 | tf_op jit(solution)/shard_map/backward/ppermute | solution.py:25
  56.1 2.5 %collective-permute-start.21 = (bf16[8,3584]{1,0:T(8,128)(2,1)S(1)}, bf16[8,3584]{1,0:T(8,128)(2,1)S(1)}, u32[]{:S(2)}, u32[]{:S(2)}) collective-permute-start(bf16[8,3584]{1,0:T(8,128)(2,1)S(1)} %get-tuple-element.51), channel_id=1, source_target_pairs={{0,8},{1,9},{2,10},{3,11},{4,12},{5,13},{6,14},{7,15},{8,0},{9,1},... | collective-permute-start | bytes 172040 | tf_op jit(solution)/shard_map/backward/ppermute | solution.py:25
  58.8 0.9 %fusion = bf16[8,3584]{1,0:T(8,128)(2,1)} fusion(f32[32,8]{1,0:T(8,128)S(1)} %get-tuple-element.20, bf16[8,3584]{1,0:T(8,128)(2,1)S(1)} %collective-permute-done.12, bf16[8,3584]{1,0:T(8,128)(2,1)S(1)} %collective-permute-done.11, bf16[8,3584]{1,0:T(8,128)(2,1)S(1)} %collective-permute-done.10, bf16[8,3584]{1,0:T(8,128)(2,1)S(1)} %get-tuple-element.52, ...), kind=kOutput, calls=%fused_computation.2 | convolution fusion | flops 12013568 | bytes 345088 | tf_op jit(solution)/shard_map/dot_general | solution.py:222
  60.3 1.3 %collective-permute-done.22 = bf16[8,3584]{1,0:T(8,128)(2,1)S(1)} collective-permute-done((bf16[8,3584]{1,0:T(8,128)(2,1)S(1)}, bf16[8,3584]{1,0:T(8,128)(2,1)S(1)}, u32[]{:S(2)}, u32[]{:S(2)}) %collective-permute-start.22) | collective-permute-done | bytes 57376 | tf_op jit(solution)/shard_map/backward/ppermute | solution.py:25
  62.0 0.7 %fusion.43 = bf16[8,3584]{1,0:T(8,128)(2,1)} fusion(bf16[8,3584]{1,0:T(8,128)(2,1)S(1)} %copy-done.4, f32[8,3584]{1,0:T(8,128)S(1)} %get-tuple-element.68, bf16[8,3584]{1,0:T(8,128)(2,1)S(1)} %copy-done.1, f32[8]{0:T(128)S(1)} %broadcast_multiply_fusion, f32[8]{0:T(128)S(1)} %get-tuple-element.67, f32[8]{0:T(128)S(1)} %get-tuple-element.66), kind=kLoop, calls=%fused_computation.67 | loop fusion | flops 229376 | bytes 286816 | tf_op jit(solution)/shard_map/convert_element_type | solution.py:240
  (64 shorter events, 6.3 us)
Async XLA Ops:
  0.6 20.9 %copy-start.2 = (bf16[1,1,32,8,256]{4,3,2,1,0:T(8,128)(2,1)S(1)}, bf16[1,1,32,8,256]{4,3,2,1,0:T(8,128)(2,1)}, u32[]{:S(2)}) copy-start(bf16[1,1,32,8,256]{4,3,2,1,0:T(8,128)(2,1)} %param.23) | copy-start | bytes 393220
  0.6 7.5 %collective-permute-start = (bf16[3584,128]{1,0:T(8,128)(2,1)}, bf16[3584,128]{1,0:T(8,128)(2,1)S(1)}, u32[]{:S(2)}, u32[]{:S(2)}) collective-permute-start(bf16[3584,128]{1,0:T(8,128)(2,1)} %bitcast.26), channel_id=1, source_target_pairs={{0,1},{1,0},{2,3},{3,2},{4,5},{5,4},{6,7},{7,6},{8,9},{9,8},{10,11... | collective-permute-start | bytes 2752520 | tf_op jit(solution)/shard_map/swaps/ppermute | solution.py:25
  1.2 7.3 %collective-permute-start.1 = (bf16[3584,128]{1,0:T(8,128)(2,1)}, bf16[3584,128]{1,0:T(8,128)(2,1)S(1)}, u32[]{:S(2)}, u32[]{:S(2)}) collective-permute-start(bf16[3584,128]{1,0:T(8,128)(2,1)} %bitcast.23), channel_id=1, source_target_pairs={{0,1},{1,0},{2,3},{3,2},{4,5},{5,4},{6,7},{7,6},{8,9},{9,8},{10,11... | collective-permute-start | bytes 2752520 | tf_op jit(solution)/shard_map/swaps/ppermute | solution.py:25
  1.2 7.2 %collective-permute-start.2 = (bf16[128,3584]{1,0:T(8,128)(2,1)}, bf16[128,3584]{1,0:T(8,128)(2,1)S(1)}, u32[]{:S(2)}, u32[]{:S(2)}) collective-permute-start(bf16[128,3584]{1,0:T(8,128)(2,1)} %bitcast.13), channel_id=1, source_target_pairs={{0,1},{1,0},{2,3},{3,2},{4,5},{5,4},{6,7},{7,6},{8,9},{9,8},{10,11... | collective-permute-start | bytes 2752520 | tf_op jit(solution)/shard_map/swaps/ppermute | solution.py:25
  2.8 11.0 %collective-permute-start.3 = (bf16[8,3584]{1,0:T(8,128)(2,1)S(1)}, bf16[8,3584]{1,0:T(8,128)(2,1)S(1)}, u32[]{:S(2)}, u32[]{:S(2)}) collective-permute-start(bf16[8,3584]{1,0:T(8,128)(2,1)S(1)} %get-tuple-element.24), channel_id=1, source_target_pairs={{0,8},{1,9},{2,10},{3,11},{4,12},{5,13},{6,14},{7,15},{8,0},{9,1},... | collective-permute-start | bytes 172040 | tf_op jit(solution)/shard_map/forward/ppermute | solution.py:25
  5.5 8.6 %collective-permute-start.4 = (bf16[8,3584]{1,0:T(8,128)(2,1)S(1)}, bf16[8,3584]{1,0:T(8,128)(2,1)S(1)}, u32[]{:S(2)}, u32[]{:S(2)}) collective-permute-start(bf16[8,3584]{1,0:T(8,128)(2,1)S(1)} %get-tuple-element.25), channel_id=1, source_target_pairs={{0,16},{1,17},{2,18},{3,19},{4,20},{5,21},{6,22},{7,23},{8,24},{9,... | collective-permute-start | bytes 172040 | tf_op jit(solution)/shard_map/forward/ppermute | solution.py:25
  8.2 6.6 %collective-permute-start.5 = (bf16[8,3584]{1,0:T(8,128)(2,1)S(1)}, bf16[8,3584]{1,0:T(8,128)(2,1)S(1)}, u32[]{:S(2)}, u32[]{:S(2)}) collective-permute-start(bf16[8,3584]{1,0:T(8,128)(2,1)S(1)} %get-tuple-element.26), channel_id=1, source_target_pairs={{0,24},{1,25},{2,26},{3,27},{4,28},{5,29},{6,30},{7,31},{8,16},{9,... | collective-permute-start | bytes 172040 | tf_op jit(solution)/shard_map/forward/ppermute | solution.py:25
  9.6 6.8 %collective-permute-start.13 = (bf16[8,3584]{1,0:T(8,128)(2,1)S(1)}, bf16[8,3584]{1,0:T(8,128)(2,1)S(1)}, u32[]{:S(2)}, u32[]{:S(2)}) collective-permute-start(bf16[8,3584]{1,0:T(8,128)(2,1)S(1)} %get-tuple-element.32), channel_id=1, source_target_pairs={{0,8},{1,9},{2,10},{3,11},{4,12},{5,13},{6,14},{7,15},{8,0},{9,1},... | collective-permute-start | bytes 172040 | tf_op jit(solution)/shard_map/backward/ppermute | solution.py:25
  10.3 7.8 %collective-permute-start.14 = (bf16[8,3584]{1,0:T(8,128)(2,1)S(1)}, bf16[8,3584]{1,0:T(8,128)(2,1)S(1)}, u32[]{:S(2)}, u32[]{:S(2)}) collective-permute-start(bf16[8,3584]{1,0:T(8,128)(2,1)S(1)} %get-tuple-element.33), channel_id=1, source_target_pairs={{0,16},{1,17},{2,18},{3,19},{4,20},{5,21},{6,22},{7,23},{8,24},{9,... | collective-permute-start | bytes 172040 | tf_op jit(solution)/shard_map/backward/ppermute | solution.py:25
  13.8 6.0 %collective-permute-start.15 = (bf16[8,3584]{1,0:T(8,128)(2,1)S(1)}, bf16[8,3584]{1,0:T(8,128)(2,1)S(1)}, u32[]{:S(2)}, u32[]{:S(2)}) collective-permute-start(bf16[8,3584]{1,0:T(8,128)(2,1)S(1)} %get-tuple-element.34), channel_id=1, source_target_pairs={{0,24},{1,25},{2,26},{3,27},{4,28},{5,29},{6,30},{7,31},{8,16},{9,... | collective-permute-start | bytes 172040 | tf_op jit(solution)/shard_map/backward/ppermute | solution.py:25
  14.8 7.1 %collective-permute-start.6 = (bf16[32,3584]{1,0:T(8,128)(2,1)S(1)}, bf16[32,3584]{1,0:T(8,128)(2,1)S(1)}, u32[]{:S(2)}, u32[]{:S(2)}) collective-permute-start(bf16[32,3584]{1,0:T(8,128)(2,1)S(1)} %pad_maximum_fusion.7), channel_id=1, source_target_pairs={{0,2},{1,5},{2,0},{3,7},{4,6},{5,1},{6,4},{7,3},{8,10},{9,13},{10,... | collective-permute-start | bytes 688136 | tf_op jit(solution)/shard_map/forward/ppermute | solution.py:25
  19.9 1.7 %collective-permute-start.18 = (bf16[32,8,256]{2,1,0:T(8,128)(2,1)}, bf16[32,8,256]{2,1,0:T(8,128)(2,1)S(1)}, u32[]{:S(2)}, u32[]{:S(2)}) collective-permute-start(bf16[32,8,256]{2,1,0:T(8,128)(2,1)} %bitcast.16), channel_id=1, source_target_pairs={{0,1},{1,0},{2,3},{3,2},{4,5},{5,4},{6,7},{7,6},{8,9},{9,8},{10,11... | collective-permute-start | bytes 393224 | tf_op jit(solution)/shard_map/backward/swaps/ppermute | solution.py:25
  20.0 10.6 %copy-start.5 = (bf16[1,1,3584,128]{3,2,1,0:T(8,128)(2,1)S(1)}, bf16[1,1,3584,128]{3,2,1,0:T(8,128)(2,1)}, u32[]{:S(2)}) copy-start(bf16[1,1,3584,128]{3,2,1,0:T(8,128)(2,1)} %param.21) | copy-start | bytes 2752516
  20.0 10.6 %copy-start.6 = (bf16[1,1,3584,128]{3,2,1,0:T(8,128)(2,1)S(1)}, bf16[1,1,3584,128]{3,2,1,0:T(8,128)(2,1)}, u32[]{:S(2)}) copy-start(bf16[1,1,3584,128]{3,2,1,0:T(8,128)(2,1)} %param.20) | copy-start | bytes 2752516
  20.0 7.4 %collective-permute-start.16 = (bf16[32,3584]{1,0:T(8,128)(2,1)S(1)}, bf16[32,3584]{1,0:T(8,128)(2,1)S(1)}, u32[]{:S(2)}, u32[]{:S(2)}) collective-permute-start(bf16[32,3584]{1,0:T(8,128)(2,1)S(1)} %pad_maximum_fusion.8), channel_id=1, source_target_pairs={{0,2},{1,5},{2,0},{3,7},{4,6},{5,1},{6,4},{7,3},{8,10},{9,13},{10,... | collective-permute-start | bytes 688136 | tf_op jit(solution)/shard_map/backward/ppermute | solution.py:25
  21.9 8.6 %collective-permute-start.7 = (bf16[64,3584]{1,0:T(8,128)(2,1)S(1)}, bf16[64,3584]{1,0:T(8,128)(2,1)S(1)}, u32[]{:S(2)}, u32[]{:S(2)}) collective-permute-start(bf16[64,3584]{1,0:T(8,128)(2,1)S(1)} %get-tuple-element.56), channel_id=1, source_target_pairs={{0,4},{1,3},{2,6},{3,1},{4,0},{5,7},{6,2},{7,5},{8,12},{9,11},{10,... | collective-permute-start | bytes 1376264 | tf_op jit(solution)/shard_map/forward/ppermute | solution.py:25
  27.5 8.5 %collective-permute-start.17 = (bf16[64,3584]{1,0:T(8,128)(2,1)S(1)}, bf16[64,3584]{1,0:T(8,128)(2,1)S(1)}, u32[]{:S(2)}, u32[]{:S(2)}) collective-permute-start(bf16[64,3584]{1,0:T(8,128)(2,1)S(1)} %pad_maximum_fusion.6), channel_id=1, source_target_pairs={{0,4},{1,3},{2,6},{3,1},{4,0},{5,7},{6,2},{7,5},{8,12},{9,11},{10,... | collective-permute-start | bytes 1376264 | tf_op jit(solution)/shard_map/backward/ppermute | solution.py:25
  30.6 1.2 %copy-start = (bf16[1,1,128,3584]{3,2,1,0:T(8,128)(2,1)S(1)}, bf16[1,1,128,3584]{3,2,1,0:T(8,128)(2,1)}, u32[]{:S(2)}) copy-start(bf16[1,1,128,3584]{3,2,1,0:T(8,128)(2,1)} %param.22) | copy-start | bytes 2752516
  32.2 8.7 %collective-permute-start.8 = (bf16[64,3584]{1,0:T(8,128)(2,1)S(1)}, bf16[64,3584]{1,0:T(8,128)(2,1)S(1)}, u32[]{:S(2)}, u32[]{:S(2)}) collective-permute-start(bf16[64,3584]{1,0:T(8,128)(2,1)S(1)} %slice.143), channel_id=1, source_target_pairs={{0,4},{1,3},{2,6},{3,1},{4,0},{5,7},{6,2},{7,5},{8,12},{9,11},{10,... | collective-permute-start | bytes 1376264 | tf_op jit(solution)/shard_map/forward/ppermute | solution.py:25
  38.2 8.5 %collective-permute-start.19 = (bf16[64,3584]{1,0:T(8,128)(2,1)S(1)}, bf16[64,3584]{1,0:T(8,128)(2,1)S(1)}, u32[]{:S(2)}, u32[]{:S(2)}) collective-permute-start(bf16[64,3584]{1,0:T(8,128)(2,1)S(1)} %slice.142), channel_id=1, source_target_pairs={{0,2},{1,5},{2,0},{3,7},{4,6},{5,1},{6,4},{7,3},{8,10},{9,13},{10,... | collective-permute-start | bytes 1376264 | tf_op jit(solution)/shard_map/backward/ppermute | solution.py:25
  41.1 8.4 %collective-permute-start.9 = (bf16[32,3584]{1,0:T(8,128)(2,1)S(1)}, bf16[32,3584]{1,0:T(8,128)(2,1)S(1)}, u32[]{:S(2)}, u32[]{:S(2)}) collective-permute-start(bf16[32,3584]{1,0:T(8,128)(2,1)S(1)} %slice.145), channel_id=1, source_target_pairs={{0,2},{1,5},{2,0},{3,7},{4,6},{5,1},{6,4},{7,3},{8,10},{9,13},{10,... | collective-permute-start | bytes 688136 | tf_op jit(solution)/shard_map/forward/ppermute | solution.py:25
  46.8 12.0 %copy-start.3 = (bf16[8,3584]{1,0:T(8,128)(2,1)S(1)}, bf16[8,3584]{1,0:T(8,128)(2,1)}, u32[]{:S(2)}) copy-start(bf16[8,3584]{1,0:T(8,128)(2,1)} %inbound_ref.1) | copy-start | bytes 172036
  46.9 14.7 %copy-start.4 = (bf16[8,3584]{1,0:T(8,128)(2,1)S(1)}, bf16[8,3584]{1,0:T(8,128)(2,1)}, u32[]{:S(2)}) copy-start(bf16[8,3584]{1,0:T(8,128)(2,1)} %param.14) | copy-start | bytes 172036
  46.9 7.2 %collective-permute-start.20 = (bf16[32,3584]{1,0:T(8,128)(2,1)S(1)}, bf16[32,3584]{1,0:T(8,128)(2,1)S(1)}, u32[]{:S(2)}, u32[]{:S(2)}) collective-permute-start(bf16[32,3584]{1,0:T(8,128)(2,1)S(1)} %slice.144), channel_id=1, source_target_pairs={{0,4},{1,3},{2,6},{3,1},{4,0},{5,7},{6,2},{7,5},{8,12},{9,11},{10,... | collective-permute-start | bytes 688136 | tf_op jit(solution)/shard_map/backward/ppermute | solution.py:25
  49.6 12.4 %copy-start.1 = (bf16[8,3584]{1,0:T(8,128)(2,1)S(1)}, bf16[8,3584]{1,0:T(8,128)(2,1)}, u32[]{:S(2)}) copy-start(bf16[8,3584]{1,0:T(8,128)(2,1)} %cotangent_ref.1) | copy-start | bytes 172036
  49.6 6.5 %collective-permute-start.12 = (bf16[8,3584]{1,0:T(8,128)(2,1)S(1)}, bf16[8,3584]{1,0:T(8,128)(2,1)S(1)}, u32[]{:S(2)}, u32[]{:S(2)}) collective-permute-start(bf16[8,3584]{1,0:T(8,128)(2,1)S(1)} %get-tuple-element.53), channel_id=1, source_target_pairs={{0,24},{1,25},{2,26},{3,27},{4,28},{5,29},{6,30},{7,31},{8,16},{9,... | collective-permute-start | bytes 172040 | tf_op jit(solution)/shard_map/forward/ppermute | solution.py:25
  50.7 8.2 %collective-permute-start.11 = (bf16[8,3584]{1,0:T(8,128)(2,1)S(1)}, bf16[8,3584]{1,0:T(8,128)(2,1)S(1)}, u32[]{:S(2)}, u32[]{:S(2)}) collective-permute-start(bf16[8,3584]{1,0:T(8,128)(2,1)S(1)} %get-tuple-element.54), channel_id=1, source_target_pairs={{0,16},{1,17},{2,18},{3,19},{4,20},{5,21},{6,22},{7,23},{8,24},{9,... | collective-permute-start | bytes 172040 | tf_op jit(solution)/shard_map/forward/ppermute | solution.py:25
  50.7 8.2 %collective-permute-start.10 = (bf16[8,3584]{1,0:T(8,128)(2,1)S(1)}, bf16[8,3584]{1,0:T(8,128)(2,1)S(1)}, u32[]{:S(2)}, u32[]{:S(2)}) collective-permute-start(bf16[8,3584]{1,0:T(8,128)(2,1)S(1)} %get-tuple-element.55), channel_id=1, source_target_pairs={{0,8},{1,9},{2,10},{3,11},{4,12},{5,13},{6,14},{7,15},{8,0},{9,1},... | collective-permute-start | bytes 172040 | tf_op jit(solution)/shard_map/forward/ppermute | solution.py:25
  54.1 6.2 %collective-permute-start.23 = (bf16[8,3584]{1,0:T(8,128)(2,1)S(1)}, bf16[8,3584]{1,0:T(8,128)(2,1)S(1)}, u32[]{:S(2)}, u32[]{:S(2)}) collective-permute-start(bf16[8,3584]{1,0:T(8,128)(2,1)S(1)} %get-tuple-element.49), channel_id=1, source_target_pairs={{0,24},{1,25},{2,26},{3,27},{4,28},{5,29},{6,30},{7,31},{8,16},{9,... | collective-permute-start | bytes 172040 | tf_op jit(solution)/shard_map/backward/ppermute | solution.py:25
  55.2 6.4 %collective-permute-start.22 = (bf16[8,3584]{1,0:T(8,128)(2,1)S(1)}, bf16[8,3584]{1,0:T(8,128)(2,1)S(1)}, u32[]{:S(2)}, u32[]{:S(2)}) collective-permute-start(bf16[8,3584]{1,0:T(8,128)(2,1)S(1)} %get-tuple-element.50), channel_id=1, source_target_pairs={{0,16},{1,17},{2,18},{3,19},{4,20},{5,21},{6,22},{7,23},{8,24},{9,... | collective-permute-start | bytes 172040 | tf_op jit(solution)/shard_map/backward/ppermute | solution.py:25
  56.1 5.5 %collective-permute-start.21 = (bf16[8,3584]{1,0:T(8,128)(2,1)S(1)}, bf16[8,3584]{1,0:T(8,128)(2,1)S(1)}, u32[]{:S(2)}, u32[]{:S(2)}) collective-permute-start(bf16[8,3584]{1,0:T(8,128)(2,1)S(1)} %get-tuple-element.51), channel_id=1, source_target_pairs={{0,8},{1,9},{2,10},{3,11},{4,12},{5,13},{6,14},{7,15},{8,0},{9,1},... | collective-permute-start | bytes 172040 | tf_op jit(solution)/shard_map/backward/ppermute | solution.py:25

commit v6 on v5

--- a/solution.py
+++ b/solution.py
@@ -111,9 +111,14 @@
     return value[:rows] + exchange(value[rows:].astype(BF16)).astype(F32)
 
 
-def give_back(partial, groups, first, second):
-    summed = halve(halve(partial, second), first).astype(BF16)
-    capacity = summed.shape[0] // groups
+def give_back_three(partial, groups, first, second):
+    rows = partial.shape[0] // 4
+    own, near, side, cross = [partial[q * rows : (q + 1) * rows] for q in range(4)]
+    cross = second(cross.astype(BF16)).astype(F32)
+    side = second(side.astype(BF16)).astype(F32)
+    near = first((near + cross).astype(BF16)).astype(F32)
+    summed = (own + side + near).astype(BF16)
+    capacity = rows // groups
     return join(along_groups([summed[k * capacity : (k + 1) * capacity] for k in range(groups)]))
 
 
@@ -218,7 +223,7 @@
     hidden = (jax.nn.silu(pre[:, :hidden_two]) * pre[:, hidden_two:]).astype(BF16)
     partial_fwd = jnp.dot(hidden, w_out, preferred_element_type=F32)
     with jax.named_scope("forward"):
-        summed = give_back(partial_fwd, groups, with_first, with_second)
+        summed = give_back_three(partial_fwd, groups, with_first, with_second)
     mixture = jnp.dot(weighted_fwd.T, summed.astype(F32), precision=HIGHEST)
     outbound = (inbound.astype(F32) + mixture).astype(BF16)
 
@@ -229,7 +234,7 @@
     d_pre = jnp.concatenate([d_gate, d_up], axis=1)
     grad_total = jnp.einsum("rh,dh->rd", d_pre, w_in, preferred_element_type=F32)
     with jax.named_scope("backward"):
-        grad_summed = give_back(grad_total, groups, with_second, with_first)
+        grad_summed = give_back_three(grad_total, groups, with_second, with_first)
     grad_normed = jnp.dot(occupied_back.T, grad_summed.astype(F32), precision=HIGHEST)
     saved32 = x_back.astype(F32)
     factor = lax.rsqrt(jnp.mean(saved32 * saved32, axis=-1, keepdims=True) + EPSILON)

time: 63 us -> 63 us (level)
  starting transfers between devices: 32.4 us -> 33.8 us
  waiting for transfers between devices: 20.5 us -> 19.2 us
    ppermute x24 -> x26, starting transfers between devices: 32.4 us -> 33.8 us  [swap(): lax.ppermute(value, 'expert', [(i, i ^ mask_of(i)) for i in range(size)])]
    ppermute x24 -> x26, waiting for transfers between devices: 20.5 us -> 19.2 us  [swap(): lax.ppermute(value, 'expert', [(i, i ^ mask_of(i)) for i in range(size)])]
  transfers between devices with their start and end apart: 24 -> 26, of which waited for: 13 -> 13; matrix products, arithmetic and copies ran while one was open for 8% -> 8% of each run, Pallas kernels for 4% -> 4%
where the time goes in v6:
time: 63 us; the launch traced here: 62.7 us
  starting transfers between devices  33.8 us (54%)
  waiting for transfers between devices  19.2 us (30%)
  matrix products  4.69 us (7%)
  Pallas kernels  2.27 us (4%)
  other arithmetic  1.04 us (2%)
  between operations  0.94 us (1%)
  local copies, waits for them, and re-layouts  0.79 us (1%)
    ppermute x26, starting transfers between devices, swap(): lax.ppermute(value, 'expert', [(i, i ^ mask_of(i)) for i in range(size)])  33.8 us
    ppermute x26, waiting for transfers between devices, swap(): lax.ppermute(value, 'expert', [(i, i ^ mask_of(i)) for i in range(size)])  19.2 us
    pallas_call x2, Pallas kernels, slot_rows(): pl.pallas_call(functools.partial(kernel, groups, capacity), out_shape=(ch...  2.27 us
    dot_general x1, matrix products, body(): jnp.einsum('rh,dh->rd', d_pre, w_in, preferred_element_type=F32)  1.36 us
  transfers between devices with their start and end apart: 26, of which 13 were waited for; matrix products, arithmetic and copies ran while one was open for 8% of the time, Pallas kernels for 4%

profile of v6, /device:TPU:0, one launch (start us, length us, event | category | flops | bytes accessed | tf_op | source)
XLA Modules:
  0.0 62.7 jit_solution(10015827904681990454)
XLA Ops:
  1.7 1.1 %forward_rows.1 = (bf16[8,3584]{1,0:T(8,128)(2,1)S(1)}, bf16[8,3584]{1,0:T(8,128)(2,1)S(1)}, bf16[8,3584]{1,0:T(8,128)(2,1)S(1)}, bf16[8,3584]{1,0:T(8,128)(2,1)...) custom-call(bf16[8,3584]{1,0:T(8,128)(2,1)} %inbound_ref.1, f32[1,3584]{1,0:T(1,128)} %scale_ref.1, s32[2,8]{1,0:T(2,128)} %bitcast.19, ...), custom_call_target="tpu_custom_call" | custom-call | tf_op jit(solution)/shard_map/forward_rows/pallas_call | solution.py:96
  2.8 2.7 %collective-permute-start.3 = (bf16[8,3584]{1,0:T(8,128)(2,1)S(1)}, bf16[8,3584]{1,0:T(8,128)(2,1)S(1)}, u32[]{:S(2)}, u32[]{:S(2)}) collective-permute-start(bf16[8,3584]{1,0:T(8,128)(2,1)S(1)} %get-tuple-element.24), channel_id=1, source_target_pairs={{0,8},{1,9},{2,10},{3,11},{4,12},{5,13},{6,14},{7,15},{8,0},{9,1},... | collective-permute-start | bytes 172040 | tf_op jit(solution)/shard_map/forward/ppermute | solution.py:25
  5.5 2.6 %collective-permute-start.4 = (bf16[8,3584]{1,0:T(8,128)(2,1)S(1)}, bf16[8,3584]{1,0:T(8,128)(2,1)S(1)}, u32[]{:S(2)}, u32[]{:S(2)}) collective-permute-start(bf16[8,3584]{1,0:T(8,128)(2,1)S(1)} %get-tuple-element.25), channel_id=1, source_target_pairs={{0,16},{1,17},{2,18},{3,19},{4,20},{5,21},{6,22},{7,23},{8,24},{9,... | collective-permute-start | bytes 172040 | tf_op jit(solution)/shard_map/forward/ppermute | solution.py:25
  8.4 1.1 %backward_rows.1 = (bf16[8,3584]{1,0:T(8,128)(2,1)S(1)}, bf16[8,3584]{1,0:T(8,128)(2,1)S(1)}, bf16[8,3584]{1,0:T(8,128)(2,1)S(1)}, bf16[8,3584]{1,0:T(8,128)(2,1...) custom-call(bf16[8,3584]{1,0:T(8,128)(2,1)} %cotangent_ref.1, s32[2,8]{1,0:T(2,128)} %bitcast.21, ...), custom_call_target="tpu_custom_call" | custom-call | tf_op jit(solution)/shard_map/backward_rows/pallas_call | solution.py:96
  9.6 0.7 %collective-permute-start.14 = (bf16[8,3584]{1,0:T(8,128)(2,1)S(1)}, bf16[8,3584]{1,0:T(8,128)(2,1)S(1)}, u32[]{:S(2)}, u32[]{:S(2)}) collective-permute-start(bf16[8,3584]{1,0:T(8,128)(2,1)S(1)} %get-tuple-element.32), channel_id=1, source_target_pairs={{0,8},{1,9},{2,10},{3,11},{4,12},{5,13},{6,14},{7,15},{8,0},{9,1},... | collective-permute-start | bytes 172040 | tf_op jit(solution)/shard_map/backward/ppermute | solution.py:25
  10.3 3.5 %collective-permute-start.15 = (bf16[8,3584]{1,0:T(8,128)(2,1)S(1)}, bf16[8,3584]{1,0:T(8,128)(2,1)S(1)}, u32[]{:S(2)}, u32[]{:S(2)}) collective-permute-start(bf16[8,3584]{1,0:T(8,128)(2,1)S(1)} %get-tuple-element.33), channel_id=1, source_target_pairs={{0,16},{1,17},{2,18},{3,19},{4,20},{5,21},{6,22},{7,23},{8,24},{9,... | collective-permute-start | bytes 172040 | tf_op jit(solution)/shard_map/backward/ppermute | solution.py:25
  14.8 1.6 %collective-permute-start.6 = (bf16[32,3584]{1,0:T(8,128)(2,1)S(1)}, bf16[32,3584]{1,0:T(8,128)(2,1)S(1)}, u32[]{:S(2)}, u32[]{:S(2)}) collective-permute-start(bf16[32,3584]{1,0:T(8,128)(2,1)S(1)} %pad_maximum_fusion.7), channel_id=1, source_target_pairs={{0,2},{1,5},{2,0},{3,7},{4,6},{5,1},{6,4},{7,3},{8,10},{9,13},{10,... | collective-permute-start | bytes 688136 | tf_op jit(solution)/shard_map/forward/ppermute | solution.py:25
  16.4 1.8 %collective-permute-done.15 = bf16[8,3584]{1,0:T(8,128)(2,1)S(1)} collective-permute-done((bf16[8,3584]{1,0:T(8,128)(2,1)S(1)}, bf16[8,3584]{1,0:T(8,128)(2,1)S(1)}, u32[]{:S(2)}, u32[]{:S(2)}) %collective-permute-start.15) | collective-permute-done | bytes 57376 | tf_op jit(solution)/shard_map/backward/ppermute | solution.py:25
  18.1 1.7 %collective-permute-done.16 = bf16[8,3584]{1,0:T(8,128)(2,1)S(1)} collective-permute-done((bf16[8,3584]{1,0:T(8,128)(2,1)S(1)}, bf16[8,3584]{1,0:T(8,128)(2,1)S(1)}, u32[]{:S(2)}, u32[]{:S(2)}) %collective-permute-start.16) | collective-permute-done | bytes 57376 | tf_op jit(solution)/shard_map/backward/ppermute | solution.py:25
  20.0 1.5 %collective-permute-start.17 = (bf16[32,3584]{1,0:T(8,128)(2,1)S(1)}, bf16[32,3584]{1,0:T(8,128)(2,1)S(1)}, u32[]{:S(2)}, u32[]{:S(2)}) collective-permute-start(bf16[32,3584]{1,0:T(8,128)(2,1)S(1)} %pad_maximum_fusion.8), channel_id=1, source_target_pairs={{0,2},{1,5},{2,0},{3,7},{4,6},{5,1},{6,4},{7,3},{8,10},{9,13},{10,... | collective-permute-start | bytes 688136 | tf_op jit(solution)/shard_map/backward/ppermute | solution.py:25
  21.9 1.6 %collective-permute-start.7 = (bf16[64,3584]{1,0:T(8,128)(2,1)S(1)}, bf16[64,3584]{1,0:T(8,128)(2,1)S(1)}, u32[]{:S(2)}, u32[]{:S(2)}) collective-permute-start(bf16[64,3584]{1,0:T(8,128)(2,1)S(1)} %get-tuple-element.60), channel_id=1, source_target_pairs={{0,4},{1,3},{2,6},{3,1},{4,0},{5,7},{6,2},{7,5},{8,12},{9,11},{10,... | collective-permute-start | bytes 1376264 | tf_op jit(solution)/shard_map/forward/ppermute | solution.py:25
  23.5 4.0 %collective-permute-done.17 = bf16[32,3584]{1,0:T(8,128)(2,1)S(1)} collective-permute-done((bf16[32,3584]{1,0:T(8,128)(2,1)S(1)}, bf16[32,3584]{1,0:T(8,128)(2,1)S(1)}, u32[]{:S(2)}, u32[]{:S(2)}) %collective-permute-start.17) | collective-permute-done | bytes 229408 | tf_op jit(solution)/shard_map/backward/ppermute | solution.py:25
  27.5 1.7 %collective-permute-start.18 = (bf16[64,3584]{1,0:T(8,128)(2,1)S(1)}, bf16[64,3584]{1,0:T(8,128)(2,1)S(1)}, u32[]{:S(2)}, u32[]{:S(2)}) collective-permute-start(bf16[64,3584]{1,0:T(8,128)(2,1)S(1)} %pad_maximum_fusion.6), channel_id=1, source_target_pairs={{0,4},{1,3},{2,6},{3,1},{4,0},{5,7},{6,2},{7,5},{8,12},{9,11},{10,... | collective-permute-start | bytes 1376264 | tf_op jit(solution)/shard_map/backward/ppermute | solution.py:25
  29.2 1.3 %collective-permute-done.7 = bf16[64,3584]{1,0:T(8,128)(2,1)S(1)} collective-permute-done((bf16[64,3584]{1,0:T(8,128)(2,1)S(1)}, bf16[64,3584]{1,0:T(8,128)(2,1)S(1)}, u32[]{:S(2)}, u32[]{:S(2)}) %collective-permute-start.7) | collective-permute-done | bytes 458784 | tf_op jit(solution)/shard_map/forward/ppermute | solution.py:25
  30.6 0.7 %fusion.11 = f32[128,512]{1,0:T(8,128)S(1)} fusion(bf16[128,3584]{1,0:T(8,128)(2,1)S(1)} %constant_dynamic-update-slice_fusion.5, bf16[3584,128]{1,0:T(8,128)(2,1)S(1)} %collective-permute-done.1, bf16[3584,128]{1,0:T(8,128)(2,1)S(1)} %bitcast.24, bf16[3584,128]{1,0:T(8,128)(2,1)S(1)} %collective-permute-done, bf16[3584,128]{1,0:T(8,128)(2,1)S(1)} %bitcast.27), kind=kOutput, calls=%fused_computation.15 | convolution fusion | flops 484442112 | bytes 4849664 | tf_op jit(solution)/shard_map/dot_general | solution.py:222
  32.2 1.6 %collective-permute-start.8 = (bf16[32,3584]{1,0:T(8,128)(2,1)S(1)}, bf16[32,3584]{1,0:T(8,128)(2,1)S(1)}, u32[]{:S(2)}, u32[]{:S(2)}) collective-permute-start(bf16[32,3584]{1,0:T(8,128)(2,1)S(1)} %get-tuple-element.42), channel_id=1, source_target_pairs={{0,4},{1,3},{2,6},{3,1},{4,0},{5,7},{6,2},{7,5},{8,12},{9,11},{10,... | collective-permute-start | bytes 688136 | tf_op jit(solution)/shard_map/forward/ppermute | solution.py:25
  34.3 1.7 %collective-permute-done.18 = bf16[64,3584]{1,0:T(8,128)(2,1)S(1)} collective-permute-done((bf16[64,3584]{1,0:T(8,128)(2,1)S(1)}, bf16[64,3584]{1,0:T(8,128)(2,1)S(1)}, u32[]{:S(2)}, u32[]{:S(2)}) %collective-permute-start.18) | collective-permute-done | bytes 458784 | tf_op jit(solution)/shard_map/backward/ppermute | solution.py:25
  36.1 0.7 %fusion.39 = (bf16[128,256]{1,0:T(8,128)(2,1)S(1)}, bf16[128,256]{1,0:T(8,128)(2,1)S(1)}) fusion(f32[128,128]{1,0:T(8,128)S(1)} %get-tuple-element.51, f32[128,128]{1,0:T(8,128)S(1)} %get-tuple-element.48, f32[128,128]{1,0:T(8,128)S(1)} %get-tuple-element.49, f32[128,128]{1,0:T(8,128)S(1)} %get-tuple-element.50, ...), kind=kOutput, calls=%fused_computation.55 | convolution fusion | flops 242712576 | bytes 3145728 | tf_op jit(solution)/shard_map/rd,hd->rh/dot_general | solution.py:230
  36.8 1.4 %fusion.77 = (bf16[128,3584]{1,0:T(8,128)(2,1)S(1)}, f32[128,3584]{1,0:T(8,128)S(1)}) fusion(bf16[3584,128]{1,0:T(8,128)(2,1)S(1)} %collective-permute-done.1, bf16[3584,128]{1,0:T(8,128)(2,1)S(1)} %bitcast.25, bf16[3584,128]{1,0:T(8,128)(2,1)S(1)} %collective-permute-done, bf16[3584,128]{1,0:T(8,128)(2,1)S(1)} %bitcast.28, ...), kind=kOutput, calls=%fused_computation.126 | convolution fusion | flops 485163008 | bytes 6553600 | tf_op jit(solution)/shard_map/rh,dh->rd/dot_general | solution.py:235
  38.2 1.5 %collective-permute-start.20 = (bf16[32,3584]{1,0:T(8,128)(2,1)S(1)}, bf16[32,3584]{1,0:T(8,128)(2,1)S(1)}, u32[]{:S(2)}, u32[]{:S(2)}) collective-permute-start(bf16[32,3584]{1,0:T(8,128)(2,1)S(1)} %get-tuple-element.40), channel_id=1, source_target_pairs={{0,2},{1,5},{2,0},{3,7},{4,6},{5,1},{6,4},{7,3},{8,10},{9,13},{10,... | collective-permute-start | bytes 688136 | tf_op jit(solution)/shard_map/backward/ppermute | solution.py:25
  41.0 1.5 %collective-permute-start.10 = (bf16[32,3584]{1,0:T(8,128)(2,1)S(1)}, bf16[32,3584]{1,0:T(8,128)(2,1)S(1)}, u32[]{:S(2)}, u32[]{:S(2)}) collective-permute-start(bf16[32,3584]{1,0:T(8,128)(2,1)S(1)} %fusion.15), channel_id=1, source_target_pairs={{0,2},{1,5},{2,0},{3,7},{4,6},{5,1},{6,4},{7,3},{8,10},{9,13},{10,... | collective-permute-start | bytes 688136 | tf_op jit(solution)/shard_map/forward/ppermute | solution.py:25
  42.5 4.2 %collective-permute-done.21 = bf16[32,3584]{1,0:T(8,128)(2,1)S(1)} collective-permute-done((bf16[32,3584]{1,0:T(8,128)(2,1)S(1)}, bf16[32,3584]{1,0:T(8,128)(2,1)S(1)}, u32[]{:S(2)}, u32[]{:S(2)}) %collective-permute-start.21) | collective-permute-done | bytes 229408 | tf_op jit(solution)/shard_map/backward/ppermute | solution.py:25
  46.8 1.7 %collective-permute-start.22 = (bf16[32,3584]{1,0:T(8,128)(2,1)S(1)}, bf16[32,3584]{1,0:T(8,128)(2,1)S(1)}, u32[]{:S(2)}, u32[]{:S(2)}) collective-permute-start(bf16[32,3584]{1,0:T(8,128)(2,1)S(1)} %fusion.12), channel_id=1, source_target_pairs={{0,4},{1,3},{2,6},{3,1},{4,0},{5,7},{6,2},{7,5},{8,12},{9,11},{10,... | collective-permute-start | bytes 688136 | tf_op jit(solution)/shard_map/backward/ppermute | solution.py:25
  48.5 1.1 %collective-permute-done.10 = bf16[32,3584]{1,0:T(8,128)(2,1)S(1)} collective-permute-done((bf16[32,3584]{1,0:T(8,128)(2,1)S(1)}, bf16[32,3584]{1,0:T(8,128)(2,1)S(1)}, u32[]{:S(2)}, u32[]{:S(2)}) %collective-permute-start.10) | collective-permute-done | bytes 229408 | tf_op jit(solution)/shard_map/forward/ppermute | solution.py:25
  49.7 1.0 %collective-permute-start.13 = (bf16[8,3584]{1,0:T(8,128)(2,1)S(1)}, bf16[8,3584]{1,0:T(8,128)(2,1)S(1)}, u32[]{:S(2)}, u32[]{:S(2)}) collective-permute-start(bf16[8,3584]{1,0:T(8,128)(2,1)S(1)} %get-tuple-element.57), channel_id=1, source_target_pairs={{0,24},{1,25},{2,26},{3,27},{4,28},{5,29},{6,30},{7,31},{8,16},{9,... | collective-permute-start | bytes 172040 | tf_op jit(solution)/shard_map/forward/ppermute | solution.py:25
  50.7 3.5 %collective-permute-start.11 = (bf16[8,3584]{1,0:T(8,128)(2,1)S(1)}, bf16[8,3584]{1,0:T(8,128)(2,1)S(1)}, u32[]{:S(2)}, u32[]{:S(2)}) collective-permute-start(bf16[8,3584]{1,0:T(8,128)(2,1)S(1)} %get-tuple-element.59), channel_id=1, source_target_pairs={{0,8},{1,9},{2,10},{3,11},{4,12},{5,13},{6,14},{7,15},{8,0},{9,1},... | collective-permute-start | bytes 172040 | tf_op jit(solution)/shard_map/forward/ppermute | solution.py:25
  54.3 1.0 %collective-permute-start.25 = (bf16[8,3584]{1,0:T(8,128)(2,1)S(1)}, bf16[8,3584]{1,0:T(8,128)(2,1)S(1)}, u32[]{:S(2)}, u32[]{:S(2)}) collective-permute-start(bf16[8,3584]{1,0:T(8,128)(2,1)S(1)} %get-tuple-element.53), channel_id=1, source_target_pairs={{0,24},{1,25},{2,26},{3,27},{4,28},{5,29},{6,30},{7,31},{8,16},{9,... | collective-permute-start | bytes 172040 | tf_op jit(solution)/shard_map/backward/ppermute | solution.py:25
  56.0 2.8 %collective-permute-start.23 = (bf16[8,3584]{1,0:T(8,128)(2,1)S(1)}, bf16[8,3584]{1,0:T(8,128)(2,1)S(1)}, u32[]{:S(2)}, u32[]{:S(2)}) collective-permute-start(bf16[8,3584]{1,0:T(8,128)(2,1)S(1)} %get-tuple-element.55), channel_id=1, source_target_pairs={{0,8},{1,9},{2,10},{3,11},{4,12},{5,13},{6,14},{7,15},{8,0},{9,1},... | collective-permute-start | bytes 172040 | tf_op jit(solution)/shard_map/backward/ppermute | solution.py:25
  58.8 0.9 %fusion = bf16[8,3584]{1,0:T(8,128)(2,1)} fusion(f32[32,8]{1,0:T(8,128)S(1)} %get-tuple-element.20, bf16[8,3584]{1,0:T(8,128)(2,1)S(1)} %collective-permute-done.13, bf16[8,3584]{1,0:T(8,128)(2,1)S(1)} %collective-permute-done.12, bf16[8,3584]{1,0:T(8,128)(2,1)S(1)} %collective-permute-done.11, bf16[8,3584]{1,0:T(8,128)(2,1)S(1)} %get-tuple-element.56, ...), kind=kOutput, calls=%fused_computation.2 | convolution fusion | flops 12013568 | bytes 345088 | tf_op jit(solution)/shard_map/dot_general | solution.py:227
  59.7 0.7 %collective-permute-done.25 = bf16[8,3584]{1,0:T(8,128)(2,1)S(1)} collective-permute-done((bf16[8,3584]{1,0:T(8,128)(2,1)S(1)}, bf16[8,3584]{1,0:T(8,128)(2,1)S(1)}, u32[]{:S(2)}, u32[]{:S(2)}) %collective-permute-start.25) | collective-permute-done | bytes 57376 | tf_op jit(solution)/shard_map/backward/ppermute | solution.py:25
  60.5 1.1 %collective-permute-done.24 = bf16[8,3584]{1,0:T(8,128)(2,1)S(1)} collective-permute-done((bf16[8,3584]{1,0:T(8,128)(2,1)S(1)}, bf16[8,3584]{1,0:T(8,128)(2,1)S(1)}, u32[]{:S(2)}, u32[]{:S(2)}) %collective-permute-start.24) | collective-permute-done | bytes 57376 | tf_op jit(solution)/shard_map/backward/ppermute | solution.py:25
  62.0 0.7 %fusion.47 = bf16[8,3584]{1,0:T(8,128)(2,1)} fusion(bf16[8,3584]{1,0:T(8,128)(2,1)S(1)} %copy-done.4, f32[8,3584]{1,0:T(8,128)S(1)} %get-tuple-element.76, bf16[8,3584]{1,0:T(8,128)(2,1)S(1)} %copy-done.1, f32[8]{0:T(128)S(1)} %broadcast_multiply_fusion, f32[8]{0:T(128)S(1)} %get-tuple-element.71, f32[8]{0:T(128)S(1)} %get-tuple-element.70), kind=kLoop, calls=%fused_computation.67 | loop fusion | flops 229376 | bytes 286816 | tf_op jit(solution)/shard_map/convert_element_type | solution.py:245
  (66 shorter events, 7.0 us)
Async XLA Ops:
  0.6 20.9 %copy-start.2 = (bf16[1,1,32,8,256]{4,3,2,1,0:T(8,128)(2,1)S(1)}, bf16[1,1,32,8,256]{4,3,2,1,0:T(8,128)(2,1)}, u32[]{:S(2)}) copy-start(bf16[1,1,32,8,256]{4,3,2,1,0:T(8,128)(2,1)} %param.23) | copy-start | bytes 393220
  0.6 7.5 %collective-permute-start = (bf16[3584,128]{1,0:T(8,128)(2,1)}, bf16[3584,128]{1,0:T(8,128)(2,1)S(1)}, u32[]{:S(2)}, u32[]{:S(2)}) collective-permute-start(bf16[3584,128]{1,0:T(8,128)(2,1)} %bitcast.26), channel_id=1, source_target_pairs={{0,1},{1,0},{2,3},{3,2},{4,5},{5,4},{6,7},{7,6},{8,9},{9,8},{10,11... | collective-permute-start | bytes 2752520 | tf_op jit(solution)/shard_map/swaps/ppermute | solution.py:25
  1.2 7.3 %collective-permute-start.1 = (bf16[3584,128]{1,0:T(8,128)(2,1)}, bf16[3584,128]{1,0:T(8,128)(2,1)S(1)}, u32[]{:S(2)}, u32[]{:S(2)}) collective-permute-start(bf16[3584,128]{1,0:T(8,128)(2,1)} %bitcast.23), channel_id=1, source_target_pairs={{0,1},{1,0},{2,3},{3,2},{4,5},{5,4},{6,7},{7,6},{8,9},{9,8},{10,11... | collective-permute-start | bytes 2752520 | tf_op jit(solution)/shard_map/swaps/ppermute | solution.py:25
  1.2 7.2 %collective-permute-start.2 = (bf16[128,3584]{1,0:T(8,128)(2,1)}, bf16[128,3584]{1,0:T(8,128)(2,1)S(1)}, u32[]{:S(2)}, u32[]{:S(2)}) collective-permute-start(bf16[128,3584]{1,0:T(8,128)(2,1)} %bitcast.13), channel_id=1, source_target_pairs={{0,1},{1,0},{2,3},{3,2},{4,5},{5,4},{6,7},{7,6},{8,9},{9,8},{10,11... | collective-permute-start | bytes 2752520 | tf_op jit(solution)/shard_map/swaps/ppermute | solution.py:25
  2.8 11.0 %collective-permute-start.3 = (bf16[8,3584]{1,0:T(8,128)(2,1)S(1)}, bf16[8,3584]{1,0:T(8,128)(2,1)S(1)}, u32[]{:S(2)}, u32[]{:S(2)}) collective-permute-start(bf16[8,3584]{1,0:T(8,128)(2,1)S(1)} %get-tuple-element.24), channel_id=1, source_target_pairs={{0,8},{1,9},{2,10},{3,11},{4,12},{5,13},{6,14},{7,15},{8,0},{9,1},... | collective-permute-start | bytes 172040 | tf_op jit(solution)/shard_map/forward/ppermute | solution.py:25
  5.5 8.6 %collective-permute-start.4 = (bf16[8,3584]{1,0:T(8,128)(2,1)S(1)}, bf16[8,3584]{1,0:T(8,128)(2,1)S(1)}, u32[]{:S(2)}, u32[]{:S(2)}) collective-permute-start(bf16[8,3584]{1,0:T(8,128)(2,1)S(1)} %get-tuple-element.25), channel_id=1, source_target_pairs={{0,16},{1,17},{2,18},{3,19},{4,20},{5,21},{6,22},{7,23},{8,24},{9,... | collective-permute-start | bytes 172040 | tf_op jit(solution)/shard_map/forward/ppermute | solution.py:25
  8.2 6.6 %collective-permute-start.5 = (bf16[8,3584]{1,0:T(8,128)(2,1)S(1)}, bf16[8,3584]{1,0:T(8,128)(2,1)S(1)}, u32[]{:S(2)}, u32[]{:S(2)}) collective-permute-start(bf16[8,3584]{1,0:T(8,128)(2,1)S(1)} %get-tuple-element.26), channel_id=1, source_target_pairs={{0,24},{1,25},{2,26},{3,27},{4,28},{5,29},{6,30},{7,31},{8,16},{9,... | collective-permute-start | bytes 172040 | tf_op jit(solution)/shard_map/forward/ppermute | solution.py:25
  9.6 6.8 %collective-permute-start.14 = (bf16[8,3584]{1,0:T(8,128)(2,1)S(1)}, bf16[8,3584]{1,0:T(8,128)(2,1)S(1)}, u32[]{:S(2)}, u32[]{:S(2)}) collective-permute-start(bf16[8,3584]{1,0:T(8,128)(2,1)S(1)} %get-tuple-element.32), channel_id=1, source_target_pairs={{0,8},{1,9},{2,10},{3,11},{4,12},{5,13},{6,14},{7,15},{8,0},{9,1},... | collective-permute-start | bytes 172040 | tf_op jit(solution)/shard_map/backward/ppermute | solution.py:25
  10.3 7.8 %collective-permute-start.15 = (bf16[8,3584]{1,0:T(8,128)(2,1)S(1)}, bf16[8,3584]{1,0:T(8,128)(2,1)S(1)}, u32[]{:S(2)}, u32[]{:S(2)}) collective-permute-start(bf16[8,3584]{1,0:T(8,128)(2,1)S(1)} %get-tuple-element.33), channel_id=1, source_target_pairs={{0,16},{1,17},{2,18},{3,19},{4,20},{5,21},{6,22},{7,23},{8,24},{9,... | collective-permute-start | bytes 172040 | tf_op jit(solution)/shard_map/backward/ppermute | solution.py:25
  13.8 6.0 %collective-permute-start.16 = (bf16[8,3584]{1,0:T(8,128)(2,1)S(1)}, bf16[8,3584]{1,0:T(8,128)(2,1)S(1)}, u32[]{:S(2)}, u32[]{:S(2)}) collective-permute-start(bf16[8,3584]{1,0:T(8,128)(2,1)S(1)} %get-tuple-element.34), channel_id=1, source_target_pairs={{0,24},{1,25},{2,26},{3,27},{4,28},{5,29},{6,30},{7,31},{8,16},{9,... | collective-permute-start | bytes 172040 | tf_op jit(solution)/shard_map/backward/ppermute | solution.py:25
  14.8 7.1 %collective-permute-start.6 = (bf16[32,3584]{1,0:T(8,128)(2,1)S(1)}, bf16[32,3584]{1,0:T(8,128)(2,1)S(1)}, u32[]{:S(2)}, u32[]{:S(2)}) collective-permute-start(bf16[32,3584]{1,0:T(8,128)(2,1)S(1)} %pad_maximum_fusion.7), channel_id=1, source_target_pairs={{0,2},{1,5},{2,0},{3,7},{4,6},{5,1},{6,4},{7,3},{8,10},{9,13},{10,... | collective-permute-start | bytes 688136 | tf_op jit(solution)/shard_map/forward/ppermute | solution.py:25
  19.9 1.7 %collective-permute-start.19 = (bf16[32,8,256]{2,1,0:T(8,128)(2,1)}, bf16[32,8,256]{2,1,0:T(8,128)(2,1)S(1)}, u32[]{:S(2)}, u32[]{:S(2)}) collective-permute-start(bf16[32,8,256]{2,1,0:T(8,128)(2,1)} %bitcast.16), channel_id=1, source_target_pairs={{0,1},{1,0},{2,3},{3,2},{4,5},{5,4},{6,7},{7,6},{8,9},{9,8},{10,11... | collective-permute-start | bytes 393224 | tf_op jit(solution)/shard_map/backward/swaps/ppermute | solution.py:25
  20.0 10.6 %copy-start.5 = (bf16[1,1,3584,128]{3,2,1,0:T(8,128)(2,1)S(1)}, bf16[1,1,3584,128]{3,2,1,0:T(8,128)(2,1)}, u32[]{:S(2)}) copy-start(bf16[1,1,3584,128]{3,2,1,0:T(8,128)(2,1)} %param.21) | copy-start | bytes 2752516
  20.0 10.6 %copy-start.6 = (bf16[1,1,3584,128]{3,2,1,0:T(8,128)(2,1)S(1)}, bf16[1,1,3584,128]{3,2,1,0:T(8,128)(2,1)}, u32[]{:S(2)}) copy-start(bf16[1,1,3584,128]{3,2,1,0:T(8,128)(2,1)} %param.20) | copy-start | bytes 2752516
  20.0 7.4 %collective-permute-start.17 = (bf16[32,3584]{1,0:T(8,128)(2,1)S(1)}, bf16[32,3584]{1,0:T(8,128)(2,1)S(1)}, u32[]{:S(2)}, u32[]{:S(2)}) collective-permute-start(bf16[32,3584]{1,0:T(8,128)(2,1)S(1)} %pad_maximum_fusion.8), channel_id=1, source_target_pairs={{0,2},{1,5},{2,0},{3,7},{4,6},{5,1},{6,4},{7,3},{8,10},{9,13},{10,... | collective-permute-start | bytes 688136 | tf_op jit(solution)/shard_map/backward/ppermute | solution.py:25
  21.9 8.6 %collective-permute-start.7 = (bf16[64,3584]{1,0:T(8,128)(2,1)S(1)}, bf16[64,3584]{1,0:T(8,128)(2,1)S(1)}, u32[]{:S(2)}, u32[]{:S(2)}) collective-permute-start(bf16[64,3584]{1,0:T(8,128)(2,1)S(1)} %get-tuple-element.60), channel_id=1, source_target_pairs={{0,4},{1,3},{2,6},{3,1},{4,0},{5,7},{6,2},{7,5},{8,12},{9,11},{10,... | collective-permute-start | bytes 1376264 | tf_op jit(solution)/shard_map/forward/ppermute | solution.py:25
  27.5 8.5 %collective-permute-start.18 = (bf16[64,3584]{1,0:T(8,128)(2,1)S(1)}, bf16[64,3584]{1,0:T(8,128)(2,1)S(1)}, u32[]{:S(2)}, u32[]{:S(2)}) collective-permute-start(bf16[64,3584]{1,0:T(8,128)(2,1)S(1)} %pad_maximum_fusion.6), channel_id=1, source_target_pairs={{0,4},{1,3},{2,6},{3,1},{4,0},{5,7},{6,2},{7,5},{8,12},{9,11},{10,... | collective-permute-start | bytes 1376264 | tf_op jit(solution)/shard_map/backward/ppermute | solution.py:25
  32.2 16.3 %collective-permute-start.8 = (bf16[32,3584]{1,0:T(8,128)(2,1)S(1)}, bf16[32,3584]{1,0:T(8,128)(2,1)S(1)}, u32[]{:S(2)}, u32[]{:S(2)}) collective-permute-start(bf16[32,3584]{1,0:T(8,128)(2,1)S(1)} %get-tuple-element.42), channel_id=1, source_target_pairs={{0,4},{1,3},{2,6},{3,1},{4,0},{5,7},{6,2},{7,5},{8,12},{9,11},{10,... | collective-permute-start | bytes 688136 | tf_op jit(solution)/shard_map/forward/ppermute | solution.py:25
  33.8 7.1 %collective-permute-start.9 = (bf16[32,3584]{1,0:T(8,128)(2,1)S(1)}, bf16[32,3584]{1,0:T(8,128)(2,1)S(1)}, u32[]{:S(2)}, u32[]{:S(2)}) collective-permute-start(bf16[32,3584]{1,0:T(8,128)(2,1)S(1)} %get-tuple-element.43), channel_id=1, source_target_pairs={{0,4},{1,3},{2,6},{3,1},{4,0},{5,7},{6,2},{7,5},{8,12},{9,11},{10,... | collective-permute-start | bytes 688136 | tf_op jit(solution)/shard_map/forward/ppermute | solution.py:25
  38.2 16.0 %collective-permute-start.20 = (bf16[32,3584]{1,0:T(8,128)(2,1)S(1)}, bf16[32,3584]{1,0:T(8,128)(2,1)S(1)}, u32[]{:S(2)}, u32[]{:S(2)}) collective-permute-start(bf16[32,3584]{1,0:T(8,128)(2,1)S(1)} %get-tuple-element.40), channel_id=1, source_target_pairs={{0,2},{1,5},{2,0},{3,7},{4,6},{5,1},{6,4},{7,3},{8,10},{9,13},{10,... | collective-permute-start | bytes 688136 | tf_op jit(solution)/shard_map/backward/ppermute | solution.py:25
  39.7 7.0 %collective-permute-start.21 = (bf16[32,3584]{1,0:T(8,128)(2,1)S(1)}, bf16[32,3584]{1,0:T(8,128)(2,1)S(1)}, u32[]{:S(2)}, u32[]{:S(2)}) collective-permute-start(bf16[32,3584]{1,0:T(8,128)(2,1)S(1)} %get-tuple-element.41), channel_id=1, source_target_pairs={{0,2},{1,5},{2,0},{3,7},{4,6},{5,1},{6,4},{7,3},{8,10},{9,13},{10,... | collective-permute-start | bytes 688136 | tf_op jit(solution)/shard_map/backward/ppermute | solution.py:25
  41.0 8.6 %collective-permute-start.10 = (bf16[32,3584]{1,0:T(8,128)(2,1)S(1)}, bf16[32,3584]{1,0:T(8,128)(2,1)S(1)}, u32[]{:S(2)}, u32[]{:S(2)}) collective-permute-start(bf16[32,3584]{1,0:T(8,128)(2,1)S(1)} %fusion.15), channel_id=1, source_target_pairs={{0,2},{1,5},{2,0},{3,7},{4,6},{5,1},{6,4},{7,3},{8,10},{9,13},{10,... | collective-permute-start | bytes 688136 | tf_op jit(solution)/shard_map/forward/ppermute | solution.py:25
  46.8 12.0 %copy-start.3 = (bf16[8,3584]{1,0:T(8,128)(2,1)S(1)}, bf16[8,3584]{1,0:T(8,128)(2,1)}, u32[]{:S(2)}) copy-start(bf16[8,3584]{1,0:T(8,128)(2,1)} %inbound_ref.1) | copy-start | bytes 172036
  46.8 14.8 %copy-start.4 = (bf16[8,3584]{1,0:T(8,128)(2,1)S(1)}, bf16[8,3584]{1,0:T(8,128)(2,1)}, u32[]{:S(2)}) copy-start(bf16[8,3584]{1,0:T(8,128)(2,1)} %param.14) | copy-start | bytes 172036
  46.8 7.4 %collective-permute-start.22 = (bf16[32,3584]{1,0:T(8,128)(2,1)S(1)}, bf16[32,3584]{1,0:T(8,128)(2,1)S(1)}, u32[]{:S(2)}, u32[]{:S(2)}) collective-permute-start(bf16[32,3584]{1,0:T(8,128)(2,1)S(1)} %fusion.12), channel_id=1, source_target_pairs={{0,4},{1,3},{2,6},{3,1},{4,0},{5,7},{6,2},{7,5},{8,12},{9,11},{10,... | collective-permute-start | bytes 688136 | tf_op jit(solution)/shard_map/backward/ppermute | solution.py:25
  49.7 12.3 %copy-start.1 = (bf16[8,3584]{1,0:T(8,128)(2,1)S(1)}, bf16[8,3584]{1,0:T(8,128)(2,1)}, u32[]{:S(2)}) copy-start(bf16[8,3584]{1,0:T(8,128)(2,1)} %cotangent_ref.1) | copy-start | bytes 172036
  49.7 6.2 %collective-permute-start.13 = (bf16[8,3584]{1,0:T(8,128)(2,1)S(1)}, bf16[8,3584]{1,0:T(8,128)(2,1)S(1)}, u32[]{:S(2)}, u32[]{:S(2)}) collective-permute-start(bf16[8,3584]{1,0:T(8,128)(2,1)S(1)} %get-tuple-element.57), channel_id=1, source_target_pairs={{0,24},{1,25},{2,26},{3,27},{4,28},{5,29},{6,30},{7,31},{8,16},{9,... | collective-permute-start | bytes 172040 | tf_op jit(solution)/shard_map/forward/ppermute | solution.py:25
  50.7 8.1 %collective-permute-start.12 = (bf16[8,3584]{1,0:T(8,128)(2,1)S(1)}, bf16[8,3584]{1,0:T(8,128)(2,1)S(1)}, u32[]{:S(2)}, u32[]{:S(2)}) collective-permute-start(bf16[8,3584]{1,0:T(8,128)(2,1)S(1)} %get-tuple-element.58), channel_id=1, source_target_pairs={{0,16},{1,17},{2,18},{3,19},{4,20},{5,21},{6,22},{7,23},{8,24},{9,... | collective-permute-start | bytes 172040 | tf_op jit(solution)/shard_map/forward/ppermute | solution.py:25
  50.7 8.1 %collective-permute-start.11 = (bf16[8,3584]{1,0:T(8,128)(2,1)S(1)}, bf16[8,3584]{1,0:T(8,128)(2,1)S(1)}, u32[]{:S(2)}, u32[]{:S(2)}) collective-permute-start(bf16[8,3584]{1,0:T(8,128)(2,1)S(1)} %get-tuple-element.59), channel_id=1, source_target_pairs={{0,8},{1,9},{2,10},{3,11},{4,12},{5,13},{6,14},{7,15},{8,0},{9,1},... | collective-permute-start | bytes 172040 | tf_op jit(solution)/shard_map/forward/ppermute | solution.py:25
  54.3 6.2 %collective-permute-start.25 = (bf16[8,3584]{1,0:T(8,128)(2,1)S(1)}, bf16[8,3584]{1,0:T(8,128)(2,1)S(1)}, u32[]{:S(2)}, u32[]{:S(2)}) collective-permute-start(bf16[8,3584]{1,0:T(8,128)(2,1)S(1)} %get-tuple-element.53), channel_id=1, source_target_pairs={{0,24},{1,25},{2,26},{3,27},{4,28},{5,29},{6,30},{7,31},{8,16},{9,... | collective-permute-start | bytes 172040 | tf_op jit(solution)/shard_map/backward/ppermute | solution.py:25
  55.3 6.3 %collective-permute-start.24 = (bf16[8,3584]{1,0:T(8,128)(2,1)S(1)}, bf16[8,3584]{1,0:T(8,128)(2,1)S(1)}, u32[]{:S(2)}, u32[]{:S(2)}) collective-permute-start(bf16[8,3584]{1,0:T(8,128)(2,1)S(1)} %get-tuple-element.54), channel_id=1, source_target_pairs={{0,16},{1,17},{2,18},{3,19},{4,20},{5,21},{6,22},{7,23},{8,24},{9,... | collective-permute-start | bytes 172040 | tf_op jit(solution)/shard_map/backward/ppermute | solution.py:25
  56.0 5.6 %collective-permute-start.23 = (bf16[8,3584]{1,0:T(8,128)(2,1)S(1)}, bf16[8,3584]{1,0:T(8,128)(2,1)S(1)}, u32[]{:S(2)}, u32[]{:S(2)}) collective-permute-start(bf16[8,3584]{1,0:T(8,128)(2,1)S(1)} %get-tuple-element.55), channel_id=1, source_target_pairs={{0,8},{1,9},{2,10},{3,11},{4,12},{5,13},{6,14},{7,15},{8,0},{9,1},... | collective-permute-start | bytes 172040 | tf_op jit(solution)/shard_map/backward/ppermute | solution.py:25
  (1 other events, 1.2 us)

commit v7 on v6

--- a/solution.py
+++ b/solution.py
@@ -103,7 +103,8 @@
 
 
 def along_groups(chunks):
-    return [chunks[0]] + [swap(chunks[k], lambda i, k=k: 8 * k) for k in range(1, len(chunks))]
+    arrived = [swap(chunks[k], lambda i, k=k: 8 * k) for k in range(len(chunks) - 1, 0, -1)]
+    return [chunks[0]] + arrived[::-1]
 
 
 def halve(value, exchange):

time: 63 us -> 63 us (level)
  no operation moved by 1% of the time
where the time goes in v7:
time: 63 us; the launch traced here: 62.7 us
  starting transfers between devices  33.8 us (54%)
  waiting for transfers between devices  19.2 us (30%)
  matrix products  4.69 us (7%)
  Pallas kernels  2.27 us (4%)
  other arithmetic  1.04 us (2%)
  between operations  0.94 us (1%)
  local copies, waits for them, and re-layouts  0.79 us (1%)
    ppermute x26, starting transfers between devices, swap(): lax.ppermute(value, 'expert', [(i, i ^ mask_of(i)) for i in range(size)])  33.8 us
    ppermute x26, waiting for transfers between devices, swap(): lax.ppermute(value, 'expert', [(i, i ^ mask_of(i)) for i in range(size)])  19.2 us
    pallas_call x2, Pallas kernels, slot_rows(): pl.pallas_call(functools.partial(kernel, groups, capacity), out_shape=(ch...  2.27 us
    dot_general x1, matrix products, body(): jnp.einsum('rh,dh->rd', d_pre, w_in, preferred_element_type=F32)  1.36 us
  transfers between devices with their start and end apart: 26, of which 13 were waited for; matrix products, arithmetic and copies ran while one was open for 8% of the time, Pallas kernels for 4%

profile of v7, /device:TPU:0, one launch (start us, length us, event | category | flops | bytes accessed | tf_op | source)
XLA Modules:
  0.0 62.7 jit_solution(10015827904681990454)
XLA Ops:
  1.7 1.1 %forward_rows.1 = (bf16[8,3584]{1,0:T(8,128)(2,1)S(1)}, bf16[8,3584]{1,0:T(8,128)(2,1)S(1)}, bf16[8,3584]{1,0:T(8,128)(2,1)S(1)}, bf16[8,3584]{1,0:T(8,128)(2,1)...) custom-call(bf16[8,3584]{1,0:T(8,128)(2,1)} %inbound_ref.1, f32[1,3584]{1,0:T(1,128)} %scale_ref.1, s32[2,8]{1,0:T(2,128)} %bitcast.19, ...), custom_call_target="tpu_custom_call" | custom-call | tf_op jit(solution)/shard_map/forward_rows/pallas_call | solution.py:96
  2.8 2.7 %collective-permute-start.3 = (bf16[8,3584]{1,0:T(8,128)(2,1)S(1)}, bf16[8,3584]{1,0:T(8,128)(2,1)S(1)}, u32[]{:S(2)}, u32[]{:S(2)}) collective-permute-start(bf16[8,3584]{1,0:T(8,128)(2,1)S(1)} %get-tuple-element.24), channel_id=1, source_target_pairs={{0,8},{1,9},{2,10},{3,11},{4,12},{5,13},{6,14},{7,15},{8,0},{9,1},... | collective-permute-start | bytes 172040 | tf_op jit(solution)/shard_map/forward/ppermute | solution.py:25
  5.5 2.6 %collective-permute-start.4 = (bf16[8,3584]{1,0:T(8,128)(2,1)S(1)}, bf16[8,3584]{1,0:T(8,128)(2,1)S(1)}, u32[]{:S(2)}, u32[]{:S(2)}) collective-permute-start(bf16[8,3584]{1,0:T(8,128)(2,1)S(1)} %get-tuple-element.25), channel_id=1, source_target_pairs={{0,16},{1,17},{2,18},{3,19},{4,20},{5,21},{6,22},{7,23},{8,24},{9,... | collective-permute-start | bytes 172040 | tf_op jit(solution)/shard_map/forward/ppermute | solution.py:25
  8.4 1.1 %backward_rows.1 = (bf16[8,3584]{1,0:T(8,128)(2,1)S(1)}, bf16[8,3584]{1,0:T(8,128)(2,1)S(1)}, bf16[8,3584]{1,0:T(8,128)(2,1)S(1)}, bf16[8,3584]{1,0:T(8,128)(2,1...) custom-call(bf16[8,3584]{1,0:T(8,128)(2,1)} %cotangent_ref.1, s32[2,8]{1,0:T(2,128)} %bitcast.21, ...), custom_call_target="tpu_custom_call" | custom-call | tf_op jit(solution)/shard_map/backward_rows/pallas_call | solution.py:96
  9.6 0.7 %collective-permute-start.14 = (bf16[8,3584]{1,0:T(8,128)(2,1)S(1)}, bf16[8,3584]{1,0:T(8,128)(2,1)S(1)}, u32[]{:S(2)}, u32[]{:S(2)}) collective-permute-start(bf16[8,3584]{1,0:T(8,128)(2,1)S(1)} %get-tuple-element.32), channel_id=1, source_target_pairs={{0,8},{1,9},{2,10},{3,11},{4,12},{5,13},{6,14},{7,15},{8,0},{9,1},... | collective-permute-start | bytes 172040 | tf_op jit(solution)/shard_map/backward/ppermute | solution.py:25
  10.3 3.5 %collective-permute-start.15 = (bf16[8,3584]{1,0:T(8,128)(2,1)S(1)}, bf16[8,3584]{1,0:T(8,128)(2,1)S(1)}, u32[]{:S(2)}, u32[]{:S(2)}) collective-permute-start(bf16[8,3584]{1,0:T(8,128)(2,1)S(1)} %get-tuple-element.33), channel_id=1, source_target_pairs={{0,16},{1,17},{2,18},{3,19},{4,20},{5,21},{6,22},{7,23},{8,24},{9,... | collective-permute-start | bytes 172040 | tf_op jit(solution)/shard_map/backward/ppermute | solution.py:25
  14.8 1.6 %collective-permute-start.6 = (bf16[32,3584]{1,0:T(8,128)(2,1)S(1)}, bf16[32,3584]{1,0:T(8,128)(2,1)S(1)}, u32[]{:S(2)}, u32[]{:S(2)}) collective-permute-start(bf16[32,3584]{1,0:T(8,128)(2,1)S(1)} %pad_maximum_fusion.7), channel_id=1, source_target_pairs={{0,2},{1,5},{2,0},{3,7},{4,6},{5,1},{6,4},{7,3},{8,10},{9,13},{10,... | collective-permute-start | bytes 688136 | tf_op jit(solution)/shard_map/forward/ppermute | solution.py:25
  16.4 1.8 %collective-permute-done.15 = bf16[8,3584]{1,0:T(8,128)(2,1)S(1)} collective-permute-done((bf16[8,3584]{1,0:T(8,128)(2,1)S(1)}, bf16[8,3584]{1,0:T(8,128)(2,1)S(1)}, u32[]{:S(2)}, u32[]{:S(2)}) %collective-permute-start.15) | collective-permute-done | bytes 57376 | tf_op jit(solution)/shard_map/backward/ppermute | solution.py:25
  18.1 1.7 %collective-permute-done.16 = bf16[8,3584]{1,0:T(8,128)(2,1)S(1)} collective-permute-done((bf16[8,3584]{1,0:T(8,128)(2,1)S(1)}, bf16[8,3584]{1,0:T(8,128)(2,1)S(1)}, u32[]{:S(2)}, u32[]{:S(2)}) %collective-permute-start.16) | collective-permute-done | bytes 57376 | tf_op jit(solution)/shard_map/backward/ppermute | solution.py:25
  20.0 1.5 %collective-permute-start.17 = (bf16[32,3584]{1,0:T(8,128)(2,1)S(1)}, bf16[32,3584]{1,0:T(8,128)(2,1)S(1)}, u32[]{:S(2)}, u32[]{:S(2)}) collective-permute-start(bf16[32,3584]{1,0:T(8,128)(2,1)S(1)} %pad_maximum_fusion.8), channel_id=1, source_target_pairs={{0,2},{1,5},{2,0},{3,7},{4,6},{5,1},{6,4},{7,3},{8,10},{9,13},{10,... | collective-permute-start | bytes 688136 | tf_op jit(solution)/shard_map/backward/ppermute | solution.py:25
  21.9 1.6 %collective-permute-start.7 = (bf16[64,3584]{1,0:T(8,128)(2,1)S(1)}, bf16[64,3584]{1,0:T(8,128)(2,1)S(1)}, u32[]{:S(2)}, u32[]{:S(2)}) collective-permute-start(bf16[64,3584]{1,0:T(8,128)(2,1)S(1)} %get-tuple-element.60), channel_id=1, source_target_pairs={{0,4},{1,3},{2,6},{3,1},{4,0},{5,7},{6,2},{7,5},{8,12},{9,11},{10,... | collective-permute-start | bytes 1376264 | tf_op jit(solution)/shard_map/forward/ppermute | solution.py:25
  23.5 4.0 %collective-permute-done.17 = bf16[32,3584]{1,0:T(8,128)(2,1)S(1)} collective-permute-done((bf16[32,3584]{1,0:T(8,128)(2,1)S(1)}, bf16[32,3584]{1,0:T(8,128)(2,1)S(1)}, u32[]{:S(2)}, u32[]{:S(2)}) %collective-permute-start.17) | collective-permute-done | bytes 229408 | tf_op jit(solution)/shard_map/backward/ppermute | solution.py:25
  27.5 1.7 %collective-permute-start.18 = (bf16[64,3584]{1,0:T(8,128)(2,1)S(1)}, bf16[64,3584]{1,0:T(8,128)(2,1)S(1)}, u32[]{:S(2)}, u32[]{:S(2)}) collective-permute-start(bf16[64,3584]{1,0:T(8,128)(2,1)S(1)} %pad_maximum_fusion.6), channel_id=1, source_target_pairs={{0,4},{1,3},{2,6},{3,1},{4,0},{5,7},{6,2},{7,5},{8,12},{9,11},{10,... | collective-permute-start | bytes 1376264 | tf_op jit(solution)/shard_map/backward/ppermute | solution.py:25
  29.2 1.3 %collective-permute-done.7 = bf16[64,3584]{1,0:T(8,128)(2,1)S(1)} collective-permute-done((bf16[64,3584]{1,0:T(8,128)(2,1)S(1)}, bf16[64,3584]{1,0:T(8,128)(2,1)S(1)}, u32[]{:S(2)}, u32[]{:S(2)}) %collective-permute-start.7) | collective-permute-done | bytes 458784 | tf_op jit(solution)/shard_map/forward/ppermute | solution.py:25
  30.6 0.7 %fusion.11 = f32[128,512]{1,0:T(8,128)S(1)} fusion(bf16[128,3584]{1,0:T(8,128)(2,1)S(1)} %constant_dynamic-update-slice_fusion.5, bf16[3584,128]{1,0:T(8,128)(2,1)S(1)} %collective-permute-done.1, bf16[3584,128]{1,0:T(8,128)(2,1)S(1)} %bitcast.24, bf16[3584,128]{1,0:T(8,128)(2,1)S(1)} %collective-permute-done, bf16[3584,128]{1,0:T(8,128)(2,1)S(1)} %bitcast.27), kind=kOutput, calls=%fused_computation.15 | convolution fusion | flops 484442112 | bytes 4849664 | tf_op jit(solution)/shard_map/dot_general | solution.py:223
  32.2 1.6 %collective-permute-start.8 = (bf16[32,3584]{1,0:T(8,128)(2,1)S(1)}, bf16[32,3584]{1,0:T(8,128)(2,1)S(1)}, u32[]{:S(2)}, u32[]{:S(2)}) collective-permute-start(bf16[32,3584]{1,0:T(8,128)(2,1)S(1)} %get-tuple-element.42), channel_id=1, source_target_pairs={{0,4},{1,3},{2,6},{3,1},{4,0},{5,7},{6,2},{7,5},{8,12},{9,11},{10,... | collective-permute-start | bytes 688136 | tf_op jit(solution)/shard_map/forward/ppermute | solution.py:25
  34.3 1.7 %collective-permute-done.18 = bf16[64,3584]{1,0:T(8,128)(2,1)S(1)} collective-permute-done((bf16[64,3584]{1,0:T(8,128)(2,1)S(1)}, bf16[64,3584]{1,0:T(8,128)(2,1)S(1)}, u32[]{:S(2)}, u32[]{:S(2)}) %collective-permute-start.18) | collective-permute-done | bytes 458784 | tf_op jit(solution)/shard_map/backward/ppermute | solution.py:25
  36.1 0.7 %fusion.39 = (bf16[128,256]{1,0:T(8,128)(2,1)S(1)}, bf16[128,256]{1,0:T(8,128)(2,1)S(1)}) fusion(f32[128,128]{1,0:T(8,128)S(1)} %get-tuple-element.51, f32[128,128]{1,0:T(8,128)S(1)} %get-tuple-element.48, f32[128,128]{1,0:T(8,128)S(1)} %get-tuple-element.49, f32[128,128]{1,0:T(8,128)S(1)} %get-tuple-element.50, ...), kind=kOutput, calls=%fused_computation.55 | convolution fusion | flops 242712576 | bytes 3145728 | tf_op jit(solution)/shard_map/rd,hd->rh/dot_general | solution.py:231
  36.8 1.4 %fusion.77 = (bf16[128,3584]{1,0:T(8,128)(2,1)S(1)}, f32[128,3584]{1,0:T(8,128)S(1)}) fusion(bf16[3584,128]{1,0:T(8,128)(2,1)S(1)} %collective-permute-done.1, bf16[3584,128]{1,0:T(8,128)(2,1)S(1)} %bitcast.25, bf16[3584,128]{1,0:T(8,128)(2,1)S(1)} %collective-permute-done, bf16[3584,128]{1,0:T(8,128)(2,1)S(1)} %bitcast.28, ...), kind=kOutput, calls=%fused_computation.126 | convolution fusion | flops 485163008 | bytes 6553600 | tf_op jit(solution)/shard_map/rh,dh->rd/dot_general | solution.py:236
  38.2 1.5 %collective-permute-start.20 = (bf16[32,3584]{1,0:T(8,128)(2,1)S(1)}, bf16[32,3584]{1,0:T(8,128)(2,1)S(1)}, u32[]{:S(2)}, u32[]{:S(2)}) collective-permute-start(bf16[32,3584]{1,0:T(8,128)(2,1)S(1)} %get-tuple-element.40), channel_id=1, source_target_pairs={{0,2},{1,5},{2,0},{3,7},{4,6},{5,1},{6,4},{7,3},{8,10},{9,13},{10,... | collective-permute-start | bytes 688136 | tf_op jit(solution)/shard_map/backward/ppermute | solution.py:25
  41.0 1.5 %collective-permute-start.10 = (bf16[32,3584]{1,0:T(8,128)(2,1)S(1)}, bf16[32,3584]{1,0:T(8,128)(2,1)S(1)}, u32[]{:S(2)}, u32[]{:S(2)}) collective-permute-start(bf16[32,3584]{1,0:T(8,128)(2,1)S(1)} %fusion.15), channel_id=1, source_target_pairs={{0,2},{1,5},{2,0},{3,7},{4,6},{5,1},{6,4},{7,3},{8,10},{9,13},{10,... | collective-permute-start | bytes 688136 | tf_op jit(solution)/shard_map/forward/ppermute | solution.py:25
  42.5 4.2 %collective-permute-done.21 = bf16[32,3584]{1,0:T(8,128)(2,1)S(1)} collective-permute-done((bf16[32,3584]{1,0:T(8,128)(2,1)S(1)}, bf16[32,3584]{1,0:T(8,128)(2,1)S(1)}, u32[]{:S(2)}, u32[]{:S(2)}) %collective-permute-start.21) | collective-permute-done | bytes 229408 | tf_op jit(solution)/shard_map/backward/ppermute | solution.py:25
  46.8 1.7 %collective-permute-start.22 = (bf16[32,3584]{1,0:T(8,128)(2,1)S(1)}, bf16[32,3584]{1,0:T(8,128)(2,1)S(1)}, u32[]{:S(2)}, u32[]{:S(2)}) collective-permute-start(bf16[32,3584]{1,0:T(8,128)(2,1)S(1)} %fusion.12), channel_id=1, source_target_pairs={{0,4},{1,3},{2,6},{3,1},{4,0},{5,7},{6,2},{7,5},{8,12},{9,11},{10,... | collective-permute-start | bytes 688136 | tf_op jit(solution)/shard_map/backward/ppermute | solution.py:25
  48.5 1.1 %collective-permute-done.10 = bf16[32,3584]{1,0:T(8,128)(2,1)S(1)} collective-permute-done((bf16[32,3584]{1,0:T(8,128)(2,1)S(1)}, bf16[32,3584]{1,0:T(8,128)(2,1)S(1)}, u32[]{:S(2)}, u32[]{:S(2)}) %collective-permute-start.10) | collective-permute-done | bytes 229408 | tf_op jit(solution)/shard_map/forward/ppermute | solution.py:25
  49.7 1.0 %collective-permute-start.13 = (bf16[8,3584]{1,0:T(8,128)(2,1)S(1)}, bf16[8,3584]{1,0:T(8,128)(2,1)S(1)}, u32[]{:S(2)}, u32[]{:S(2)}) collective-permute-start(bf16[8,3584]{1,0:T(8,128)(2,1)S(1)} %get-tuple-element.57), channel_id=1, source_target_pairs={{0,24},{1,25},{2,26},{3,27},{4,28},{5,29},{6,30},{7,31},{8,16},{9,... | collective-permute-start | bytes 172040 | tf_op jit(solution)/shard_map/forward/ppermute | solution.py:25
  50.7 3.5 %collective-permute-start.11 = (bf16[8,3584]{1,0:T(8,128)(2,1)S(1)}, bf16[8,3584]{1,0:T(8,128)(2,1)S(1)}, u32[]{:S(2)}, u32[]{:S(2)}) collective-permute-start(bf16[8,3584]{1,0:T(8,128)(2,1)S(1)} %get-tuple-element.59), channel_id=1, source_target_pairs={{0,8},{1,9},{2,10},{3,11},{4,12},{5,13},{6,14},{7,15},{8,0},{9,1},... | collective-permute-start | bytes 172040 | tf_op jit(solution)/shard_map/forward/ppermute | solution.py:25
  54.3 1.0 %collective-permute-start.25 = (bf16[8,3584]{1,0:T(8,128)(2,1)S(1)}, bf16[8,3584]{1,0:T(8,128)(2,1)S(1)}, u32[]{:S(2)}, u32[]{:S(2)}) collective-permute-start(bf16[8,3584]{1,0:T(8,128)(2,1)S(1)} %get-tuple-element.53), channel_id=1, source_target_pairs={{0,24},{1,25},{2,26},{3,27},{4,28},{5,29},{6,30},{7,31},{8,16},{9,... | collective-permute-start | bytes 172040 | tf_op jit(solution)/shard_map/backward/ppermute | solution.py:25
  56.0 2.8 %collective-permute-start.23 = (bf16[8,3584]{1,0:T(8,128)(2,1)S(1)}, bf16[8,3584]{1,0:T(8,128)(2,1)S(1)}, u32[]{:S(2)}, u32[]{:S(2)}) collective-permute-start(bf16[8,3584]{1,0:T(8,128)(2,1)S(1)} %get-tuple-element.55), channel_id=1, source_target_pairs={{0,8},{1,9},{2,10},{3,11},{4,12},{5,13},{6,14},{7,15},{8,0},{9,1},... | collective-permute-start | bytes 172040 | tf_op jit(solution)/shard_map/backward/ppermute | solution.py:25
  58.8 0.9 %fusion = bf16[8,3584]{1,0:T(8,128)(2,1)} fusion(f32[32,8]{1,0:T(8,128)S(1)} %get-tuple-element.20, bf16[8,3584]{1,0:T(8,128)(2,1)S(1)} %collective-permute-done.13, bf16[8,3584]{1,0:T(8,128)(2,1)S(1)} %collective-permute-done.12, bf16[8,3584]{1,0:T(8,128)(2,1)S(1)} %collective-permute-done.11, bf16[8,3584]{1,0:T(8,128)(2,1)S(1)} %get-tuple-element.56, ...), kind=kOutput, calls=%fused_computation.2 | convolution fusion | flops 12013568 | bytes 345088 | tf_op jit(solution)/shard_map/dot_general | solution.py:228
  59.7 0.7 %collective-permute-done.25 = bf16[8,3584]{1,0:T(8,128)(2,1)S(1)} collective-permute-done((bf16[8,3584]{1,0:T(8,128)(2,1)S(1)}, bf16[8,3584]{1,0:T(8,128)(2,1)S(1)}, u32[]{:S(2)}, u32[]{:S(2)}) %collective-permute-start.25) | collective-permute-done | bytes 57376 | tf_op jit(solution)/shard_map/backward/ppermute | solution.py:25
  60.5 1.1 %collective-permute-done.24 = bf16[8,3584]{1,0:T(8,128)(2,1)S(1)} collective-permute-done((bf16[8,3584]{1,0:T(8,128)(2,1)S(1)}, bf16[8,3584]{1,0:T(8,128)(2,1)S(1)}, u32[]{:S(2)}, u32[]{:S(2)}) %collective-permute-start.24) | collective-permute-done | bytes 57376 | tf_op jit(solution)/shard_map/backward/ppermute | solution.py:25
  62.0 0.7 %fusion.47 = bf16[8,3584]{1,0:T(8,128)(2,1)} fusion(bf16[8,3584]{1,0:T(8,128)(2,1)S(1)} %copy-done.4, f32[8,3584]{1,0:T(8,128)S(1)} %get-tuple-element.76, bf16[8,3584]{1,0:T(8,128)(2,1)S(1)} %copy-done.1, f32[8]{0:T(128)S(1)} %broadcast_multiply_fusion, f32[8]{0:T(128)S(1)} %get-tuple-element.71, f32[8]{0:T(128)S(1)} %get-tuple-element.70), kind=kLoop, calls=%fused_computation.67 | loop fusion | flops 229376 | bytes 286816 | tf_op jit(solution)/shard_map/convert_element_type | solution.py:246
  (66 shorter events, 7.0 us)
Async XLA Ops:
  0.6 20.9 %copy-start.2 = (bf16[1,1,32,8,256]{4,3,2,1,0:T(8,128)(2,1)S(1)}, bf16[1,1,32,8,256]{4,3,2,1,0:T(8,128)(2,1)}, u32[]{:S(2)}) copy-start(bf16[1,1,32,8,256]{4,3,2,1,0:T(8,128)(2,1)} %param.23) | copy-start | bytes 393220
  0.6 7.5 %collective-permute-start = (bf16[3584,128]{1,0:T(8,128)(2,1)}, bf16[3584,128]{1,0:T(8,128)(2,1)S(1)}, u32[]{:S(2)}, u32[]{:S(2)}) collective-permute-start(bf16[3584,128]{1,0:T(8,128)(2,1)} %bitcast.26), channel_id=1, source_target_pairs={{0,1},{1,0},{2,3},{3,2},{4,5},{5,4},{6,7},{7,6},{8,9},{9,8},{10,11... | collective-permute-start | bytes 2752520 | tf_op jit(solution)/shard_map/swaps/ppermute | solution.py:25
  1.2 7.3 %collective-permute-start.1 = (bf16[3584,128]{1,0:T(8,128)(2,1)}, bf16[3584,128]{1,0:T(8,128)(2,1)S(1)}, u32[]{:S(2)}, u32[]{:S(2)}) collective-permute-start(bf16[3584,128]{1,0:T(8,128)(2,1)} %bitcast.23), channel_id=1, source_target_pairs={{0,1},{1,0},{2,3},{3,2},{4,5},{5,4},{6,7},{7,6},{8,9},{9,8},{10,11... | collective-permute-start | bytes 2752520 | tf_op jit(solution)/shard_map/swaps/ppermute | solution.py:25
  1.2 7.2 %collective-permute-start.2 = (bf16[128,3584]{1,0:T(8,128)(2,1)}, bf16[128,3584]{1,0:T(8,128)(2,1)S(1)}, u32[]{:S(2)}, u32[]{:S(2)}) collective-permute-start(bf16[128,3584]{1,0:T(8,128)(2,1)} %bitcast.13), channel_id=1, source_target_pairs={{0,1},{1,0},{2,3},{3,2},{4,5},{5,4},{6,7},{7,6},{8,9},{9,8},{10,11... | collective-permute-start | bytes 2752520 | tf_op jit(solution)/shard_map/swaps/ppermute | solution.py:25
  2.8 11.0 %collective-permute-start.3 = (bf16[8,3584]{1,0:T(8,128)(2,1)S(1)}, bf16[8,3584]{1,0:T(8,128)(2,1)S(1)}, u32[]{:S(2)}, u32[]{:S(2)}) collective-permute-start(bf16[8,3584]{1,0:T(8,128)(2,1)S(1)} %get-tuple-element.24), channel_id=1, source_target_pairs={{0,8},{1,9},{2,10},{3,11},{4,12},{5,13},{6,14},{7,15},{8,0},{9,1},... | collective-permute-start | bytes 172040 | tf_op jit(solution)/shard_map/forward/ppermute | solution.py:25
  5.5 8.6 %collective-permute-start.4 = (bf16[8,3584]{1,0:T(8,128)(2,1)S(1)}, bf16[8,3584]{1,0:T(8,128)(2,1)S(1)}, u32[]{:S(2)}, u32[]{:S(2)}) collective-permute-start(bf16[8,3584]{1,0:T(8,128)(2,1)S(1)} %get-tuple-element.25), channel_id=1, source_target_pairs={{0,16},{1,17},{2,18},{3,19},{4,20},{5,21},{6,22},{7,23},{8,24},{9,... | collective-permute-start | bytes 172040 | tf_op jit(solution)/shard_map/forward/ppermute | solution.py:25
  8.2 6.6 %collective-permute-start.5 = (bf16[8,3584]{1,0:T(8,128)(2,1)S(1)}, bf16[8,3584]{1,0:T(8,128)(2,1)S(1)}, u32[]{:S(2)}, u32[]{:S(2)}) collective-permute-start(bf16[8,3584]{1,0:T(8,128)(2,1)S(1)} %get-tuple-element.26), channel_id=1, source_target_pairs={{0,24},{1,25},{2,26},{3,27},{4,28},{5,29},{6,30},{7,31},{8,16},{9,... | collective-permute-start | bytes 172040 | tf_op jit(solution)/shard_map/forward/ppermute | solution.py:25
  9.6 6.8 %collective-permute-start.14 = (bf16[8,3584]{1,0:T(8,128)(2,1)S(1)}, bf16[8,3584]{1,0:T(8,128)(2,1)S(1)}, u32[]{:S(2)}, u32[]{:S(2)}) collective-permute-start(bf16[8,3584]{1,0:T(8,128)(2,1)S(1)} %get-tuple-element.32), channel_id=1, source_target_pairs={{0,8},{1,9},{2,10},{3,11},{4,12},{5,13},{6,14},{7,15},{8,0},{9,1},... | collective-permute-start | bytes 172040 | tf_op jit(solution)/shard_map/backward/ppermute | solution.py:25
  10.3 7.8 %collective-permute-start.15 = (bf16[8,3584]{1,0:T(8,128)(2,1)S(1)}, bf16[8,3584]{1,0:T(8,128)(2,1)S(1)}, u32[]{:S(2)}, u32[]{:S(2)}) collective-permute-start(bf16[8,3584]{1,0:T(8,128)(2,1)S(1)} %get-tuple-element.33), channel_id=1, source_target_pairs={{0,16},{1,17},{2,18},{3,19},{4,20},{5,21},{6,22},{7,23},{8,24},{9,... | collective-permute-start | bytes 172040 | tf_op jit(solution)/shard_map/backward/ppermute | solution.py:25
  13.8 6.0 %collective-permute-start.16 = (bf16[8,3584]{1,0:T(8,128)(2,1)S(1)}, bf16[8,3584]{1,0:T(8,128)(2,1)S(1)}, u32[]{:S(2)}, u32[]{:S(2)}) collective-permute-start(bf16[8,3584]{1,0:T(8,128)(2,1)S(1)} %get-tuple-element.34), channel_id=1, source_target_pairs={{0,24},{1,25},{2,26},{3,27},{4,28},{5,29},{6,30},{7,31},{8,16},{9,... | collective-permute-start | bytes 172040 | tf_op jit(solution)/shard_map/backward/ppermute | solution.py:25
  14.8 7.1 %collective-permute-start.6 = (bf16[32,3584]{1,0:T(8,128)(2,1)S(1)}, bf16[32,3584]{1,0:T(8,128)(2,1)S(1)}, u32[]{:S(2)}, u32[]{:S(2)}) collective-permute-start(bf16[32,3584]{1,0:T(8,128)(2,1)S(1)} %pad_maximum_fusion.7), channel_id=1, source_target_pairs={{0,2},{1,5},{2,0},{3,7},{4,6},{5,1},{6,4},{7,3},{8,10},{9,13},{10,... | collective-permute-start | bytes 688136 | tf_op jit(solution)/shard_map/forward/ppermute | solution.py:25
  19.9 1.7 %collective-permute-start.19 = (bf16[32,8,256]{2,1,0:T(8,128)(2,1)}, bf16[32,8,256]{2,1,0:T(8,128)(2,1)S(1)}, u32[]{:S(2)}, u32[]{:S(2)}) collective-permute-start(bf16[32,8,256]{2,1,0:T(8,128)(2,1)} %bitcast.16), channel_id=1, source_target_pairs={{0,1},{1,0},{2,3},{3,2},{4,5},{5,4},{6,7},{7,6},{8,9},{9,8},{10,11... | collective-permute-start | bytes 393224 | tf_op jit(solution)/shard_map/backward/swaps/ppermute | solution.py:25
  20.0 10.6 %copy-start.5 = (bf16[1,1,3584,128]{3,2,1,0:T(8,128)(2,1)S(1)}, bf16[1,1,3584,128]{3,2,1,0:T(8,128)(2,1)}, u32[]{:S(2)}) copy-start(bf16[1,1,3584,128]{3,2,1,0:T(8,128)(2,1)} %param.21) | copy-start | bytes 2752516
  20.0 10.6 %copy-start.6 = (bf16[1,1,3584,128]{3,2,1,0:T(8,128)(2,1)S(1)}, bf16[1,1,3584,128]{3,2,1,0:T(8,128)(2,1)}, u32[]{:S(2)}) copy-start(bf16[1,1,3584,128]{3,2,1,0:T(8,128)(2,1)} %param.20) | copy-start | bytes 2752516
  20.0 7.4 %collective-permute-start.17 = (bf16[32,3584]{1,0:T(8,128)(2,1)S(1)}, bf16[32,3584]{1,0:T(8,128)(2,1)S(1)}, u32[]{:S(2)}, u32[]{:S(2)}) collective-permute-start(bf16[32,3584]{1,0:T(8,128)(2,1)S(1)} %pad_maximum_fusion.8), channel_id=1, source_target_pairs={{0,2},{1,5},{2,0},{3,7},{4,6},{5,1},{6,4},{7,3},{8,10},{9,13},{10,... | collective-permute-start | bytes 688136 | tf_op jit(solution)/shard_map/backward/ppermute | solution.py:25
  21.9 8.6 %collective-permute-start.7 = (bf16[64,3584]{1,0:T(8,128)(2,1)S(1)}, bf16[64,3584]{1,0:T(8,128)(2,1)S(1)}, u32[]{:S(2)}, u32[]{:S(2)}) collective-permute-start(bf16[64,3584]{1,0:T(8,128)(2,1)S(1)} %get-tuple-element.60), channel_id=1, source_target_pairs={{0,4},{1,3},{2,6},{3,1},{4,0},{5,7},{6,2},{7,5},{8,12},{9,11},{10,... | collective-permute-start | bytes 1376264 | tf_op jit(solution)/shard_map/forward/ppermute | solution.py:25
  27.5 8.5 %collective-permute-start.18 = (bf16[64,3584]{1,0:T(8,128)(2,1)S(1)}, bf16[64,3584]{1,0:T(8,128)(2,1)S(1)}, u32[]{:S(2)}, u32[]{:S(2)}) collective-permute-start(bf16[64,3584]{1,0:T(8,128)(2,1)S(1)} %pad_maximum_fusion.6), channel_id=1, source_target_pairs={{0,4},{1,3},{2,6},{3,1},{4,0},{5,7},{6,2},{7,5},{8,12},{9,11},{10,... | collective-permute-start | bytes 1376264 | tf_op jit(solution)/shard_map/backward/ppermute | solution.py:25
  32.2 16.3 %collective-permute-start.8 = (bf16[32,3584]{1,0:T(8,128)(2,1)S(1)}, bf16[32,3584]{1,0:T(8,128)(2,1)S(1)}, u32[]{:S(2)}, u32[]{:S(2)}) collective-permute-start(bf16[32,3584]{1,0:T(8,128)(2,1)S(1)} %get-tuple-element.42), channel_id=1, source_target_pairs={{0,4},{1,3},{2,6},{3,1},{4,0},{5,7},{6,2},{7,5},{8,12},{9,11},{10,... | collective-permute-start | bytes 688136 | tf_op jit(solution)/shard_map/forward/ppermute | solution.py:25
  33.8 7.1 %collective-permute-start.9 = (bf16[32,3584]{1,0:T(8,128)(2,1)S(1)}, bf16[32,3584]{1,0:T(8,128)(2,1)S(1)}, u32[]{:S(2)}, u32[]{:S(2)}) collective-permute-start(bf16[32,3584]{1,0:T(8,128)(2,1)S(1)} %get-tuple-element.43), channel_id=1, source_target_pairs={{0,4},{1,3},{2,6},{3,1},{4,0},{5,7},{6,2},{7,5},{8,12},{9,11},{10,... | collective-permute-start | bytes 688136 | tf_op jit(solution)/shard_map/forward/ppermute | solution.py:25
  38.2 16.0 %collective-permute-start.20 = (bf16[32,3584]{1,0:T(8,128)(2,1)S(1)}, bf16[32,3584]{1,0:T(8,128)(2,1)S(1)}, u32[]{:S(2)}, u32[]{:S(2)}) collective-permute-start(bf16[32,3584]{1,0:T(8,128)(2,1)S(1)} %get-tuple-element.40), channel_id=1, source_target_pairs={{0,2},{1,5},{2,0},{3,7},{4,6},{5,1},{6,4},{7,3},{8,10},{9,13},{10,... | collective-permute-start | bytes 688136 | tf_op jit(solution)/shard_map/backward/ppermute | solution.py:25
  39.7 7.0 %collective-permute-start.21 = (bf16[32,3584]{1,0:T(8,128)(2,1)S(1)}, bf16[32,3584]{1,0:T(8,128)(2,1)S(1)}, u32[]{:S(2)}, u32[]{:S(2)}) collective-permute-start(bf16[32,3584]{1,0:T(8,128)(2,1)S(1)} %get-tuple-element.41), channel_id=1, source_target_pairs={{0,2},{1,5},{2,0},{3,7},{4,6},{5,1},{6,4},{7,3},{8,10},{9,13},{10,... | collective-permute-start | bytes 688136 | tf_op jit(solution)/shard_map/backward/ppermute | solution.py:25
  41.0 8.6 %collective-permute-start.10 = (bf16[32,3584]{1,0:T(8,128)(2,1)S(1)}, bf16[32,3584]{1,0:T(8,128)(2,1)S(1)}, u32[]{:S(2)}, u32[]{:S(2)}) collective-permute-start(bf16[32,3584]{1,0:T(8,128)(2,1)S(1)} %fusion.15), channel_id=1, source_target_pairs={{0,2},{1,5},{2,0},{3,7},{4,6},{5,1},{6,4},{7,3},{8,10},{9,13},{10,... | collective-permute-start | bytes 688136 | tf_op jit(solution)/shard_map/forward/ppermute | solution.py:25
  46.8 12.0 %copy-start.3 = (bf16[8,3584]{1,0:T(8,128)(2,1)S(1)}, bf16[8,3584]{1,0:T(8,128)(2,1)}, u32[]{:S(2)}) copy-start(bf16[8,3584]{1,0:T(8,128)(2,1)} %inbound_ref.1) | copy-start | bytes 172036
  46.8 14.8 %copy-start.4 = (bf16[8,3584]{1,0:T(8,128)(2,1)S(1)}, bf16[8,3584]{1,0:T(8,128)(2,1)}, u32[]{:S(2)}) copy-start(bf16[8,3584]{1,0:T(8,128)(2,1)} %param.14) | copy-start | bytes 172036
  46.8 7.4 %collective-permute-start.22 = (bf16[32,3584]{1,0:T(8,128)(2,1)S(1)}, bf16[32,3584]{1,0:T(8,128)(2,1)S(1)}, u32[]{:S(2)}, u32[]{:S(2)}) collective-permute-start(bf16[32,3584]{1,0:T(8,128)(2,1)S(1)} %fusion.12), channel_id=1, source_target_pairs={{0,4},{1,3},{2,6},{3,1},{4,0},{5,7},{6,2},{7,5},{8,12},{9,11},{10,... | collective-permute-start | bytes 688136 | tf_op jit(solution)/shard_map/backward/ppermute | solution.py:25
  49.7 12.3 %copy-start.1 = (bf16[8,3584]{1,0:T(8,128)(2,1)S(1)}, bf16[8,3584]{1,0:T(8,128)(2,1)}, u32[]{:S(2)}) copy-start(bf16[8,3584]{1,0:T(8,128)(2,1)} %cotangent_ref.1) | copy-start | bytes 172036
  49.7 6.2 %collective-permute-start.13 = (bf16[8,3584]{1,0:T(8,128)(2,1)S(1)}, bf16[8,3584]{1,0:T(8,128)(2,1)S(1)}, u32[]{:S(2)}, u32[]{:S(2)}) collective-permute-start(bf16[8,3584]{1,0:T(8,128)(2,1)S(1)} %get-tuple-element.57), channel_id=1, source_target_pairs={{0,24},{1,25},{2,26},{3,27},{4,28},{5,29},{6,30},{7,31},{8,16},{9,... | collective-permute-start | bytes 172040 | tf_op jit(solution)/shard_map/forward/ppermute | solution.py:25
  50.7 8.1 %collective-permute-start.12 = (bf16[8,3584]{1,0:T(8,128)(2,1)S(1)}, bf16[8,3584]{1,0:T(8,128)(2,1)S(1)}, u32[]{:S(2)}, u32[]{:S(2)}) collective-permute-start(bf16[8,3584]{1,0:T(8,128)(2,1)S(1)} %get-tuple-element.58), channel_id=1, source_target_pairs={{0,16},{1,17},{2,18},{3,19},{4,20},{5,21},{6,22},{7,23},{8,24},{9,... | collective-permute-start | bytes 172040 | tf_op jit(solution)/shard_map/forward/ppermute | solution.py:25
  50.7 8.1 %collective-permute-start.11 = (bf16[8,3584]{1,0:T(8,128)(2,1)S(1)}, bf16[8,3584]{1,0:T(8,128)(2,1)S(1)}, u32[]{:S(2)}, u32[]{:S(2)}) collective-permute-start(bf16[8,3584]{1,0:T(8,128)(2,1)S(1)} %get-tuple-element.59), channel_id=1, source_target_pairs={{0,8},{1,9},{2,10},{3,11},{4,12},{5,13},{6,14},{7,15},{8,0},{9,1},... | collective-permute-start | bytes 172040 | tf_op jit(solution)/shard_map/forward/ppermute | solution.py:25
  54.3 6.2 %collective-permute-start.25 = (bf16[8,3584]{1,0:T(8,128)(2,1)S(1)}, bf16[8,3584]{1,0:T(8,128)(2,1)S(1)}, u32[]{:S(2)}, u32[]{:S(2)}) collective-permute-start(bf16[8,3584]{1,0:T(8,128)(2,1)S(1)} %get-tuple-element.53), channel_id=1, source_target_pairs={{0,24},{1,25},{2,26},{3,27},{4,28},{5,29},{6,30},{7,31},{8,16},{9,... | collective-permute-start | bytes 172040 | tf_op jit(solution)/shard_map/backward/ppermute | solution.py:25
  55.3 6.3 %collective-permute-start.24 = (bf16[8,3584]{1,0:T(8,128)(2,1)S(1)}, bf16[8,3584]{1,0:T(8,128)(2,1)S(1)}, u32[]{:S(2)}, u32[]{:S(2)}) collective-permute-start(bf16[8,3584]{1,0:T(8,128)(2,1)S(1)} %get-tuple-element.54), channel_id=1, source_target_pairs={{0,16},{1,17},{2,18},{3,19},{4,20},{5,21},{6,22},{7,23},{8,24},{9,... | collective-permute-start | bytes 172040 | tf_op jit(solution)/shard_map/backward/ppermute | solution.py:25
  56.0 5.6 %collective-permute-start.23 = (bf16[8,3584]{1,0:T(8,128)(2,1)S(1)}, bf16[8,3584]{1,0:T(8,128)(2,1)S(1)}, u32[]{:S(2)}, u32[]{:S(2)}) collective-permute-start(bf16[8,3584]{1,0:T(8,128)(2,1)S(1)} %get-tuple-element.55), channel_id=1, source_target_pairs={{0,8},{1,9},{2,10},{3,11},{4,12},{5,13},{6,14},{7,15},{8,0},{9,1},... | collective-permute-start | bytes 172040 | tf_op jit(solution)/shard_map/backward/ppermute | solution.py:25
  (1 other events, 1.2 us)
